TPU v7x, 512 devices: a whole 4x4x16 slice. The times are simulated.
512 devices in a mesh: dp: 4 (over x_lo, core), seq: 128 (over x_hi, y, z).
Axes of the slice: x: 4 (x_hi: 2, x_lo: 2; x = x_hi * 2 + x_lo), y: 4, z: 16, core: 2. Of those that a mesh axis runs over, the one named last changes fastest.
Arguments:
- features: bfloat16 [32768, 768], P(('dp', 'seq')), parts along dimension 0, may hold values from -6 to 6
- conv_gain: float32 [768], replicated, may hold values from 0.1 to 1.9
- conv_weight: bfloat16 [3840, 768], P('seq'), may hold values from -0.09375 to 0.09375
- attn_gain: float32 [768], replicated, may hold values from 0.1 to 1.9
- query_weight: bfloat16 [768, 1024], replicated, may hold values from -2 to 2
- key_weight: bfloat16 [768, 128], replicated, may hold values from -2 to 2
- value_weight: bfloat16 [768, 192], replicated, may hold values from -0.21875 to 0.21875
Outputs:
- stream: bfloat16 [32768, 768], P(('dp', 'seq')), parts along dimension 0
- attended: bfloat16 [32768, 1536], P(('dp', 'seq')), parts along dimension 0
There are 4 independent parts, one for each index of `dp`. A program takes and returns all parts, laid end to end along the dimension named above; an argument that names none is the same for every part. Nothing has to cross between parts.
All inputs are finite; a program needn't handle non-finite values.
Results may differ from a plain program's by a relative error of at most 0.0075.
Values may be sent and summed in bfloat16 or wider, within the bound.
No kernel may reach another device: no remote copies, remote signals or barrier semaphores. Data moves between devices by JAX's collectives and lax.ppermute only.
A program may use at most 64 MiB of HBM per device.

v0:
```python
import jax
import jax.numpy as jnp
from jax import lax
from jax.sharding import PartitionSpec as P

KW = 5


def extended(cells, sides, width):
    for axis, dim in sides:
        count = lax.axis_size(axis)
        ends = count - 1
        head = lax.slice_in_dim(cells, 0, width, axis=dim)
        tail = lax.slice_in_dim(cells, cells.shape[dim] - width, cells.shape[dim], axis=dim)
        cells = jnp.concatenate(
            [
                lax.ppermute(tail, axis, [(i, (i + 1) % count) for i in range(ends)]),
                cells,
                lax.ppermute(head, axis, [((i + 1) % count, i) for i in range(ends)]),
            ],
            axis=dim,
        )
    return cells


def normalize(values, gain):
    mean_square = jnp.mean(values * values, axis=-1, keepdims=True)
    return values * lax.rsqrt(mean_square + 1e-06) * gain


def local(features, conv_gain, conv_weight, attn_gain, query_weight, key_weight, value_weight):
    row_count, width = features.shape
    key_size = key_weight.shape[1]
    value_size = value_weight.shape[1]
    head_count = query_weight.shape[1] // key_size
    inputs = features.astype(jnp.float32)
    activated = jax.nn.gelu(normalize(inputs, conv_gain), approximate=True).astype(jnp.bfloat16)
    padded = extended(activated, (("seq", 0),), KW // 2)
    windows = jnp.concatenate([padded[offset : offset + row_count] for offset in range(KW)], axis=1)
    kernel = lax.all_gather(conv_weight, "seq", axis=0, tiled=True)
    conv_out = jnp.dot(windows, kernel, preferred_element_type=jnp.float32)
    stream = (inputs + conv_out).astype(jnp.bfloat16)
    attn_in = normalize(stream.astype(jnp.float32), attn_gain).astype(jnp.bfloat16)
    queries = (
        jnp.dot(attn_in, query_weight, preferred_element_type=jnp.float32) * key_size ** (-0.5)
    ).astype(jnp.bfloat16)
    keys = jnp.dot(attn_in, key_weight, preferred_element_type=jnp.float32).astype(jnp.bfloat16)
    values = jnp.dot(attn_in, value_weight, preferred_element_type=jnp.float32).astype(jnp.bfloat16)
    query_heads = queries.reshape(row_count, head_count, key_size)

    def attend_block(state, key_block, value_block):
        running_max, totals, accumulated = state
        scores = jnp.einsum(
            "thd,nd->htn", query_heads, key_block, preferred_element_type=jnp.float32
        )
        new_max = jnp.maximum(running_max, jnp.max(scores, axis=-1))
        rescale = jnp.exp(running_max - new_max)
        probs = jnp.exp(scores - new_max[..., None])
        totals = totals * rescale + jnp.sum(probs, axis=-1)
        accumulated = accumulated * rescale[..., None] + jnp.einsum(
            "htn,ne->hte",
            probs.astype(jnp.bfloat16),
            value_block,
            preferred_element_type=jnp.float32,
        )
        return (new_max, totals, accumulated)

    initial = (
        jnp.full((head_count, row_count), -1e30, jnp.float32),
        jnp.zeros((head_count, row_count), jnp.float32),
        jnp.zeros((head_count, row_count, value_size), jnp.float32),
    )
    all_keys, all_values = (
        lax.all_gather(keys, "seq", axis=0, tiled=True),
        lax.all_gather(values, "seq", axis=0, tiled=True),
    )
    state = initial
    length = all_keys.shape[0]
    key_blocks = all_keys.reshape(length // 1024, 1024, key_size)
    value_blocks = all_values.reshape(length // 1024, 1024, value_size)

    def scan_step(carry, blocks):
        return (attend_block(carry, blocks[0], blocks[1]), None)

    state, unused = lax.scan(scan_step, state, (key_blocks, value_blocks))
    running_max, totals, accumulated = state
    weighted = accumulated / totals[..., None]
    attended = (
        jnp.transpose(weighted, (1, 0, 2))
        .reshape(row_count, head_count * value_size)
        .astype(jnp.bfloat16)
    )
    return (stream, attended)


def solution(mesh):
    placed = (P(("dp", "seq"), None), P(), P("seq", None), P(), P(), P(), P())
    return jax.shard_map(
        local,
        mesh=mesh,
        in_specs=placed,
        out_specs=(P(("dp", "seq"), None), P(("dp", "seq"), None)),
        check_vma=False,
    )
```

profile of v0, /device:TPU:6, one launch (start us, length us, event | category | flops | bytes accessed | tf_op | source)
XLA Modules:
  0.0 731.7 jit_solution(11597873838824502436)
XLA Ops:
  7.2 0.7 all-gather.9.cloned.1.call-update
  8.0 1.0 fusion.20
  9.0 1.1 fusion.24
  10.1 3.8 collective-permute-start
  13.9 12.8 %collective-permute-start.1 = (bf16[2,768]{1,0:T(2,128)(2,1)S(1)}, bf16[2,768]{1,0:T(2,128)(2,1)S(1)}, u32[]{:S(2)}, u32[]{:S(2)}) collective-permute-start(bf16[2,768]{1,0:T(2,128)(2,1)S(1)} %get-tuple-element.105), channel_id=1, source_target_pairs={{1,0},{2,1},{3,2},{4,3},{5,4},{6,5},{7,6},{8,7},{9,8},{10,9},{11,1... | collective-permute-start | bytes 9224 | tf_op jit(solution)/shard_map/ppermute | solution.py:19
  26.8 1.1 constant_dynamic-update-slice_fusion
  28.1 221.9 %all-gather.9.cloned.1.call-done = bf16[128,30,768]{2,1,0:T(8,128)(2,1)} async-done(((bf16[1,30,768]{2,1,0:T(8,128)(2,1)}), bf16[128,30,768]{2,1,0:T(8,128)(2,1)}) %all-gather.9.cloned.1.call-update) | async-done | bytes 5898256 | tf_op jit(solution)/shard_map/all_gather | solution.py:40
  250.0 9.4 %reshape.40 = bf16[3840,768]{1,0:T(8,128)(2,1)} reshape(bf16[128,30,768]{2,1,0:T(8,128)(2,1)} %all-gather.9.cloned.1.call-done) | data formatting | bytes 11796480
  259.4 4.0 fusion.17
  263.4 0.9 convolution_convert_fusion
  264.4 0.8 convolution_convert_fusion.1
  265.7 217.7 %all-gather.7.cloned.1.call-done = bf16[8192,192]{1,0:T(8,128)(2,1)} async-done(((bf16[64,192]{1,0:T(8,128)(2,1)}), bf16[8192,192]{1,0:T(8,128)(2,1)}) %all-gather.7.cloned.1.call-update) | async-done | bytes 3145744 | tf_op jit(solution)/shard_map/all_gather | solution.py:75
  483.4 6.2 copy.16
  489.6 205.8 %all-gather.5.cloned.1.call-done = bf16[8192,128]{1,0:T(8,128)(2,1)} async-done(((bf16[64,128]{1,0:T(8,128)(2,1)}), bf16[8192,128]{1,0:T(8,128)(2,1)}) %all-gather.5.cloned.1.call-update) | async-done | bytes 2097168 | tf_op jit(solution)/shard_map/all_gather | solution.py:74
  695.4 28.5 %while.15 = (s32[]{:T(128)}, f32[8,64]{1,0:T(8,128)S(1)}, f32[8,64]{1,0:T(8,128)S(1)}, f32[8,64,192]{2,1,0:T(8,128)S(1)}, bf16[8,1024,128]{2,1,0:T(8,128)(2,1)},...) while((s32[]{:T(128)}, f32[8,64]{1,0:T(8,128)S(1)}, ...), condition=%wide.region_5.6_spmd.clone, body=%wide.region_2.5_spmd.clone.sunk | while | flops 338463232 | bytes 7897209 | solution.py:85
  695.4 1.5 bitcast_reduce_fusion.2
  697.5 1.5 convolution_add_fusion.3
  699.0 1.5 bitcast_reduce_fusion.2
  701.0 1.5 convolution_add_fusion.3
  702.6 1.5 bitcast_reduce_fusion.2
  704.6 1.5 convolution_add_fusion.3
  706.1 1.5 bitcast_reduce_fusion.2
  708.1 1.5 convolution_add_fusion.3
  709.7 1.5 bitcast_reduce_fusion.2
  711.7 1.5 convolution_add_fusion.3
  713.2 1.5 bitcast_reduce_fusion.2
  715.3 1.5 convolution_add_fusion.3
  716.8 1.5 bitcast_reduce_fusion.2
  718.8 1.5 convolution_add_fusion.3
  720.4 1.5 bitcast_reduce_fusion.2
  722.4 1.5 convolution_add_fusion.3
  724.2 0.9 convert_element_type.46
  (65 shorter events, 5.5 us)
Async XLA Ops:
  7.2 258.1 %copy-start = (bf16[768,1024]{1,0:T(8,128)(2,1)S(1)}, bf16[768,1024]{1,0:T(8,128)(2,1)}, u32[]{:S(2)}) copy-start(bf16[768,1024]{1,0:T(8,128)(2,1)} %param.13) | copy-start | bytes 4718596
  7.2 242.8 %all-gather.9.cloned.1.call-start = ((), (), s32[]{:S(2)}) async-start(), calls=%async_computation.2 | async-start | bytes 6340608 | tf_op jit(solution)/shard_map/all_gather | solution.py:40
  7.9 475.5 %all-gather.7.cloned.1.call-start = ((), (), s32[]{:S(2)}) async-start(), calls=%async_computation.1 | async-start | bytes 4227072 | tf_op jit(solution)/shard_map/all_gather | solution.py:75
  10.1 16.6 %collective-permute-start = (bf16[2,768]{1,0:T(2,128)(2,1)S(1)}, bf16[2,768]{1,0:T(2,128)(2,1)S(1)}, u32[]{:S(2)}, u32[]{:S(2)}) collective-permute-start(bf16[2,768]{1,0:T(2,128)(2,1)S(1)} %get-tuple-element.106), channel_id=1, source_target_pairs={{0,1},{1,2},{2,3},{3,4},{4,5},{5,6},{6,7},{7,8},{8,9},{9,10},{10,1... | collective-permute-start | bytes 9224 | tf_op jit(solution)/shard_map/ppermute | solution.py:17
  13.9 14.1 %collective-permute-start.1 = (bf16[2,768]{1,0:T(2,128)(2,1)S(1)}, bf16[2,768]{1,0:T(2,128)(2,1)S(1)}, u32[]{:S(2)}, u32[]{:S(2)}) collective-permute-start(bf16[2,768]{1,0:T(2,128)(2,1)S(1)} %get-tuple-element.105), channel_id=1, source_target_pairs={{1,0},{2,1},{3,2},{4,3},{5,4},{6,5},{7,6},{8,7},{9,8},{10,9},{11,1... | collective-permute-start | bytes 9224 | tf_op jit(solution)/shard_map/ppermute | solution.py:19
  28.1 231.3 %copy-start.1 = (bf16[64,768]{1,0:T(8,128)(2,1)S(1)}, bf16[64,768]{1,0:T(8,128)(2,1)}, u32[]{:S(2)}) copy-start(bf16[64,768]{1,0:T(8,128)(2,1)} %param.9) | copy-start | bytes 294916
  259.3 4.0 copy-start.3
  259.4 4.0 copy-start.5
  259.4 5.0 copy-start.4
  263.4 226.3 %copy-start.2 = (bf16[64,768]{1,0:T(8,128)(2,1)}, bf16[64,768]{1,0:T(8,128)(2,1)S(1)}, u32[]{:S(2)}) copy-start(bf16[64,768]{1,0:T(8,128)(2,1)S(1)} %get-tuple-element.108) | copy-start | bytes 294916
  264.3 431.1 %all-gather.5.cloned.1.call-start = ((), (), s32[]{:S(2)}) async-start(), calls=%async_computation | async-start | bytes 2113536 | tf_op jit(solution)/shard_map/all_gather | solution.py:74
Sparse Core Ops, SparseCore 0:
  12.6 237.3 all-gather.8
  264.4 218.9 all-gather.6
  487.9 207.4 all-gather.4
where the time goes:
time: 734 us; the launch traced here: 732 us
  waiting for transfers between devices  646 us (88%)
  matrix products  29.9 us (4%)
  local copies, waits for them, and re-layouts  16.8 us (2%)
  starting transfers between devices  16.7 us (2%)
  between operations  14 us (2%)
  other arithmetic  7.69 us (1%)
    all_gather x1, waiting for transfers between devices, local(): kernel = lax.all_gather(conv_weight, 'seq', axis=0, tiled=True)  222 us
    all_gather x1, waiting for transfers between devices, local(): lax.all_gather(values, 'seq', axis=0, tiled=True)  218 us
    all_gather x1, waiting for transfers between devices, local(): lax.all_gather(keys, 'seq', axis=0, tiled=True)  206 us
    unnamed x14, local copies, waits for them, and re-layouts  15.7 us
  transfers between devices with their start and end apart: 5, of which 4 were waited for; matrix products, arithmetic and copies ran while one was open for 1% of the time, Pallas kernels for 0%

commit v1 on v0

v1 whole, which is shorter than its diff:
```python
import functools

import jax
import jax.numpy as jnp
from jax import lax
from jax.experimental import pallas as pl
from jax.experimental.pallas import tpu as pltpu
from jax.sharding import Mesh
from jax.sharding import PartitionSpec as P

KW = 5
DP = ("xl", "co")
SEQ = ("xh", "y", "zt", "zp")
AXES = DP + SEQ
SIZES = (2, 2, 2, 4, 8, 2)
SHARE = ("xl", "co", "zp")
SPREAD = ("xh", "y")
STATS = 128


def everyone(block, axes, count):
    sent = jnp.broadcast_to(block[None], (count,) + block.shape)
    return lax.all_to_all(sent, axes, 0, 0, tiled=True)


def normalize(values, gain):
    mean_square = jnp.mean(values * values, axis=-1, keepdims=True)
    return values * lax.rsqrt(mean_square + 1e-06) * gain


def attention_kernel(heads, size, x_ref, qw_ref, k_ref, ve_ref, vo_ref, out_ref):
    rows = x_ref.shape[0]
    chunk = 256
    lane = lax.broadcasted_iota(jnp.int32, (chunk, 128), 1)
    scale = size ** (-0.5)
    for start in range(0, rows, chunk):
        part = pl.ds(start, chunk)
        x = x_ref[part, :]
        stats = jnp.zeros((chunk, STATS), jnp.float32)
        for pair in range(heads // 2):
            halves = []
            for odd in range(2):
                head = 2 * pair + odd
                q = jnp.dot(x, qw_ref[:, head * size : (head + 1) * size], preferred_element_type=jnp.float32)
                q = (q * scale).astype(jnp.bfloat16)
                s = lax.dot_general(q, k_ref[...], (((1,), (1,)), ((), ())), preferred_element_type=jnp.float32)
                top = jnp.max(s, axis=-1, keepdims=True)
                p = jnp.exp(s - top).astype(jnp.bfloat16)
                o = jnp.dot(p, (vo_ref if odd else ve_ref)[...], preferred_element_type=jnp.float32)
                total = o[:, 0:1] if odd else o[:, 255:256]
                halves.append(o * (1.0 / total))
                level = top + jnp.log(total)
                first = level.astype(jnp.bfloat16).astype(jnp.float32)
                rest = level - first
                second = rest.astype(jnp.bfloat16).astype(jnp.float32)
                third = rest - second
                stats = jnp.where(lane == head, first, stats)
                stats = jnp.where(lane == 8 + head, second, stats)
                stats = jnp.where(lane == 16 + head, third, stats)
            even, odd = halves
            base = pair * 384
            out_ref[part, base : base + 128] = even[:, :128].astype(jnp.bfloat16)
            out_ref[part, base + 128 : base + 256] = jnp.where(lane < 64, even[:, 128:], odd[:, :128]).astype(jnp.bfloat16)
            out_ref[part, base + 256 : base + 384] = odd[:, 128:].astype(jnp.bfloat16)
        out_ref[part, heads * 192 :] = stats.astype(jnp.bfloat16)


def combine_kernel(heads, parts_ref, out_ref):
    count, rows, _ = parts_ref.shape
    lane = lax.broadcasted_iota(jnp.int32, (rows, 128), 1)
    base = heads * 192
    weights = []
    for head in range(heads):
        levels = []
        for i in range(count):
            stats = parts_ref[i, :, base:].astype(jnp.float32)
            levels.append(stats[:, head : head + 1] + stats[:, 8 + head : 9 + head] + stats[:, 16 + head : 17 + head])
        top = functools.reduce(jnp.maximum, levels)
        shares = [jnp.exp(level - top) for level in levels]
        inverse = 1.0 / functools.reduce(jnp.add, shares)
        weights.append([share * inverse for share in shares])
    for tile in range(heads * 192 // 128):
        low, high = tile * 128 // 192, (tile * 128 + 127) // 192
        total = jnp.zeros((rows, 128), jnp.float32)
        for i in range(count):
            weight = weights[low][i]
            if high != low:
                weight = jnp.where(lane < high * 192 - tile * 128, weight, weights[high][i])
            total = total + weight * parts_ref[i, :, tile * 128 : tile * 128 + 128].astype(jnp.float32)
        out_ref[:, tile * 128 : tile * 128 + 128] = total.astype(jnp.bfloat16)


def local(features, conv_gain, conv_weight, attn_gain, query_weight, key_weight, value_weight):
    rows, width = features.shape
    size = key_weight.shape[1]
    value_size = value_weight.shape[1]
    heads = query_weight.shape[1] // size
    zp = lax.axis_index("zp")
    group = lax.axis_index(DP)
    columns = width // 4

    mine = lax.dynamic_slice_in_dim(conv_weight, group * columns, columns, axis=1)
    blocks = everyone(mine, "zt", 8)
    blocks = everyone(blocks, SPREAD, 8).reshape(64, 1, conv_weight.shape[0], columns)
    empty = jnp.zeros_like(blocks)
    kernel = jnp.concatenate(
        [jnp.where(zp == 0, blocks, empty), jnp.where(zp == 1, blocks, empty)], axis=1
    ).reshape(KW, width, columns)

    edge = jnp.where(zp == 0, features[:2], features[rows - 2 :])
    swaps = [(i, i + 1) for i in range(1, 127, 2)] + [(i + 1, i) for i in range(1, 127, 2)]
    beyond = lax.ppermute(edge, SEQ, swaps)
    inputs = features.astype(jnp.float32)
    extended = jnp.concatenate([inputs, beyond.astype(jnp.float32), jnp.zeros((14, width), jnp.float32)])
    activated = jax.nn.gelu(normalize(extended, conv_gain), approximate=True).astype(jnp.bfloat16)
    shared = everyone(activated, SHARE, 8).reshape(4, 2, rows + 16, width)
    padded = jnp.concatenate(
        [shared[:, 0, rows : rows + 2], shared[:, 0, :rows], shared[:, 1, :rows], shared[:, 1, rows : rows + 2]], axis=1
    )
    windows = jnp.concatenate([padded[:, o : o + 2 * rows] for o in range(KW)], axis=2)
    partial = jnp.dot(
        windows.reshape(8 * rows, KW * width), kernel.reshape(KW * width, columns), preferred_element_type=jnp.float32
    )
    partial = lax.all_to_all(partial.reshape(8, rows, columns), SHARE, 0, 0, tiled=True)
    partial = partial.reshape(4, 2, rows, columns).sum(axis=1)
    conv_out = jnp.concatenate([partial[i] for i in range(4)], axis=1)

    stream = (inputs + conv_out).astype(jnp.bfloat16)
    attn_in = normalize(stream.astype(jnp.float32), attn_gain).astype(jnp.bfloat16)
    both = jnp.concatenate([key_weight, value_weight], axis=1)
    pairs = jnp.dot(attn_in, both, preferred_element_type=jnp.float32).astype(jnp.bfloat16)
    near = everyone(pairs, "zt", 8)
    asked = everyone(attn_in, SPREAD, 8).reshape(8 * rows, width)
    far = lax.ppermute(near, "zp", [(0, 1), (1, 0)])
    pairs = jnp.concatenate([near, far]).reshape(16 * rows, size + value_size)
    keys, values = pairs[:, :size], pairs[:, size:]
    ones = jnp.ones((16 * rows, 256 - value_size), jnp.bfloat16)
    out = pl.pallas_call(
        functools.partial(attention_kernel, heads, size),
        out_shape=jax.ShapeDtypeStruct((8 * rows, heads * value_size + STATS), jnp.bfloat16),
        compiler_params=pltpu.CompilerParams(vmem_limit_bytes=48 * 1024 * 1024),
        name="attention",
    )(asked, query_weight, keys, jnp.concatenate([values, ones], axis=1), jnp.concatenate([ones, values], axis=1))
    parts = lax.all_to_all(out.reshape(8, rows, -1), SPREAD, 0, 0, tiled=True)
    attended = pl.pallas_call(
        functools.partial(combine_kernel, heads),
        out_shape=jax.ShapeDtypeStruct((rows, heads * value_size), jnp.bfloat16),
        compiler_params=pltpu.CompilerParams(vmem_limit_bytes=32 * 1024 * 1024),
        name="combine",
    )(parts)
    return (stream, attended)


def solution(mesh):
    finer = Mesh(mesh.devices.reshape(SIZES), AXES)
    placed = (P(AXES, None), P(), P(SEQ, None), P(), P(), P(), P())
    return jax.shard_map(
        local,
        mesh=finer,
        in_specs=placed,
        out_specs=(P(AXES, None), P(AXES, None)),
        check_vma=False,
    )
```

time: 734 us -> 183 us (0.25)
  waiting for transfers between devices: 646 us -> 51.1 us
  blocking collectives: 0 us -> 57.6 us
  matrix products: 29.9 us -> 2.25 us
  starting transfers between devices: 16.7 us -> 43 us
  between operations: 14 us -> 0.92 us
  Pallas kernels: 0 us -> 12.4 us
    all_gather x3 -> x0, waiting for transfers between devices: 645 us -> none  [the longest x1 222 us: local(): kernel = lax.all_gather(conv_weight, 'seq', axis=0, tiled=True)]
    all_to_all x0 -> x2, blocking collectives: none -> 57.6 us  [the longest x1 30.3 us: everyone(): return lax.all_to_all(sent, axes, 0, 0, tiled=True)]
    all_to_all x0 -> x5, starting transfers between devices: none -> 37.6 us  [the longest x4 32.6 us: everyone(): return lax.all_to_all(sent, axes, 0, 0, tiled=True)]
    all_to_all x0 -> x5, waiting for transfers between devices: none -> 32.8 us  [the longest x4 25.1 us: everyone(): return lax.all_to_all(sent, axes, 0, 0, tiled=True)]
    dot_general x20 -> x2, matrix products: 29.9 us -> 2.25 us  [the longest x1 1.98 us: local(): jnp.dot(windows.reshape(8 * rows, KW * width), kernel.reshape(KW * width,...]
    ppermute x2, waiting for transfers between devices: 0.14 us -> 18.4 us  [the longest x1 9.92 us: local(): far = lax.ppermute(near, 'zp', [(0, 1), (1, 0)])]
    pallas_call x0 -> x2, Pallas kernels: none -> 12.4 us  [the longest x1 10.8 us: local(): pl.pallas_call(functools.partial(attention_kernel, heads, size), out_shap...]
    unnamed x14 -> x24, local copies, waits for them, and re-layouts: 15.7 us -> 3.92 us
  transfers between devices with their start and end apart: 5 -> 7, of which waited for: 4 -> 5; matrix products, arithmetic and copies ran while one was open for 1% -> 3% of each run, Pallas kernels for 0% -> 0%
where the time goes in v1:
time: 183 us; the launch traced here: 181 us
  blocking collectives  57.6 us (31%)
  waiting for transfers between devices  51.1 us (28%)
  starting transfers between devices  43 us (23%)
  Pallas kernels  12.4 us (7%)
  local copies, waits for them, and re-layouts  12.2 us (7%)
  matrix products  2.25 us (1%)
    all_to_all x4, starting transfers between devices, everyone(): return lax.all_to_all(sent, axes, 0, 0, tiled=True)  32.6 us
    all_to_all x1, blocking collectives, everyone(): return lax.all_to_all(sent, axes, 0, 0, tiled=True)  30.3 us
    all_to_all x1, blocking collectives, local(): parts = lax.all_to_all(out.reshape(8, rows, -1), SPREAD, 0, 0, tiled=True)  27.4 us
    all_to_all x4, waiting for transfers between devices, everyone(): return lax.all_to_all(sent, axes, 0, 0, tiled=True)  25.1 us
    pallas_call x1, Pallas kernels, local(): pl.pallas_call(functools.partial(attention_kernel, heads, size), out_shap...  10.8 us
    ppermute x1, waiting for transfers between devices, local(): far = lax.ppermute(near, 'zp', [(0, 1), (1, 0)])  9.92 us
    ppermute x1, waiting for transfers between devices, local(): beyond = lax.ppermute(edge, SEQ, swaps)  8.44 us
    all_to_all x1, waiting for transfers between devices, local(): lax.all_to_all(partial.reshape(8, rows, columns), SHARE, 0, 0, tiled=True)  7.63 us
  transfers between devices with their start and end apart: 7, of which 5 were waited for; matrix products, arithmetic and copies ran while one was open for 3% of the time, Pallas kernels for 0%

profile of v1, /device:TPU:6, one launch (start us, length us, event | category | flops | bytes accessed | tf_op | source)
XLA Modules:
  0.0 181.2 jit_solution(14559993250781628067)
XLA Ops:
  0.7 0.8 copy-done
  1.5 0.7 broadcast_in_dim.16
  2.2 15.1 %all-to-all-start.1 = ((bf16[8,30,192]{2,1,0:T(8,128)(2,1)}), bf16[8,30,192]{2,1,0:T(8,128)(2,1)S(1)}, u32[]{:S(2)}, u32[]{:S(2)}) async-start(bf16[8,30,192]{2,1,0:T(8,128)(2,1)} %broadcast_in_dim.16), calls=%async_computation.1 | async-start | bytes 262144 | tf_op jit(solution)/shard_map/all_to_all | solution.py:23
  17.3 16.0 %all-to-all-done.1 = bf16[8,30,192]{2,1,0:T(8,128)(2,1)S(1)} async-done(((bf16[8,30,192]{2,1,0:T(8,128)(2,1)}), bf16[8,30,192]{2,1,0:T(8,128)(2,1)S(1)}, u32[]{:S(2)}, u32[]{:S(2)}) %all-to-all-start.1) | async-done | bytes 92192 | tf_op jit(solution)/shard_map/all_to_all | solution.py:23
  33.3 1.0 broadcast_in_dim.17
  34.4 7.4 %all-to-all-start.2 = ((bf16[8,8,30,192]{3,1,2,0:T(8,128)(2,1)}), bf16[8,8,30,192]{3,1,2,0:T(8,128)(2,1)S(1)}, u32[]{:S(2)}, u32[]{:S(2)}) async-start(bf16[8,8,30,192]{3,1,2,0:T(8,128)(2,1)} %broadcast_in_dim.17), calls=%async_computation.2 | async-start | bytes 1966080 | tf_op jit(solution)/shard_map/all_to_all | solution.py:23
  41.8 2.7 %collective-permute-start = (bf16[2,768]{1,0:T(2,128)(2,1)S(1)}, bf16[2,768]{1,0:T(2,128)(2,1)S(1)}, u32[]{:S(2)}, u32[]{:S(2)}) collective-permute-start(bf16[2,768]{1,0:T(2,128)(2,1)S(1)} %broadcast_select_fusion), channel_id=1, source_target_pairs={{1,2},{3,4},{5,6},{7,8},{9,10},{11,12},{13,14},{15,16},{17,18},{19... | collective-permute-start | bytes 9224 | tf_op jit(solution)/shard_map/ppermute | solution.py:112
  44.6 8.4 %collective-permute-done = bf16[2,768]{1,0:T(2,128)(2,1)S(1)} collective-permute-done((bf16[2,768]{1,0:T(2,128)(2,1)S(1)}, bf16[2,768]{1,0:T(2,128)(2,1)S(1)}, u32[]{:S(2)}, u32[]{:S(2)}) %collective-permute-start) | collective-permute-done | bytes 3104 | tf_op jit(solution)/shard_map/ppermute | solution.py:112
  53.4 1.0 broadcast_in_dim.15
  54.5 4.3 %all-to-all-start = ((bf16[8,80,768]{2,1,0:T(8,128)(2,1)}), bf16[8,80,768]{2,1,0:T(8,128)(2,1)S(1)}, u32[]{:S(2)}, u32[]{:S(2)}) async-start(bf16[8,80,768]{2,1,0:T(8,128)(2,1)} %broadcast_in_dim.15), calls=%async_computation | async-start | bytes 1966080 | tf_op jit(solution)/shard_map/all_to_all | solution.py:23
  58.9 0.4 pad_maximum_fusion
  59.3 1.1 copy.21
  60.4 1.9 %reshape_reshape.3 = bf16[3840,192]{1,0:T(8,128)(2,1)} reshape(bf16[64,2,30,192]{3,2,1,0:T(8,128)(2,1)S(1)} %copy.21) | data formatting | bytes 2949120 | tf_op jit(solution)/shard_map/reshape;reshape | solution.py:122
  62.4 9.2 %all-to-all-done = bf16[8,80,768]{2,1,0:T(8,128)(2,1)S(1)} async-done(((bf16[8,80,768]{2,1,0:T(8,128)(2,1)}), bf16[8,80,768]{2,1,0:T(8,128)(2,1)S(1)}, u32[]{:S(2)}, u32[]{:S(2)}) %all-to-all-start) | async-done | bytes 983072 | tf_op jit(solution)/shard_map/all_to_all | solution.py:23
  71.6 0.3 pad_maximum_fusion.2
  72.6 1.1 copy-done.3
  73.7 2.0 %fusion = f32[8,64,192]{2,1,0:T(8,128)} fusion(bf16[8,64,3840]{2,1,0:T(8,128)(2,1)S(1)} %bitcast.42, bf16[3840,192]{1,0:T(8,128)(2,1)S(1)} %copy-done.3), kind=kOutput, calls=%fused_computation.1 | convolution fusion | flops 754974720 | bytes 5799936 | tf_op jit(solution)/shard_map/dot_general | solution.py:121
  75.7 5.0 %all-to-all-start.3 = ((f32[8,64,192]{2,1,0:T(8,128)}), f32[8,64,192]{2,1,0:T(8,128)S(1)}, u32[]{:S(2)}, u32[]{:S(2)}) async-start(f32[8,64,192]{2,1,0:T(8,128)} %fusion), calls=%async_computation.3 | async-start | bytes 1048576 | tf_op jit(solution)/shard_map/all_to_all | solution.py:124
  80.9 7.6 %all-to-all-done.3 = f32[8,64,192]{2,1,0:T(8,128)S(1)} async-done(((f32[8,64,192]{2,1,0:T(8,128)}), f32[8,64,192]{2,1,0:T(8,128)S(1)}, u32[]{:S(2)}, u32[]{:S(2)}) %all-to-all-start.3) | async-done | bytes 393248 | tf_op jit(solution)/shard_map/all_to_all | solution.py:124
  88.9 0.3 convolution_convert_fusion
  89.3 30.3 %all_to_all.35 = bf16[8,64,320]{2,1,0:T(8,128)(2,1)S(1)} all-to-all(bf16[8,64,320]{2,1,0:T(8,128)(2,1)S(1)} %broadcast_in_dim.20), channel_id=1, replica_groups=mesh['xl'=2,'co'=2,'xh'=2,'y'=4,'zt'=8,'zp'=2] {'zt'}, dimensions={0} | all-to-all | bytes 655360 | tf_op jit(solution)/shard_map/all_to_all | solution.py:23
  119.6 0.9 broadcast_in_dim.19
  120.5 5.8 %all-to-all-start.4 = ((bf16[8,64,768]{2,1,0:T(8,128)(2,1)}), bf16[8,64,768]{2,1,0:T(8,128)(2,1)S(1)}, u32[]{:S(2)}, u32[]{:S(2)}) async-start(bf16[8,64,768]{2,1,0:T(8,128)(2,1)} %broadcast_in_dim.19), calls=%async_computation.4 | async-start | bytes 1572864 | tf_op jit(solution)/shard_map/all_to_all | solution.py:23
  126.3 2.7 %collective-permute-start.1 = (bf16[8,64,320]{2,1,0:T(8,128)(2,1)S(1)}, bf16[8,64,320]{2,1,0:T(8,128)(2,1)S(1)}, u32[]{:S(2)}, u32[]{:S(2)}) collective-permute-start(bf16[8,64,320]{2,1,0:T(8,128)(2,1)S(1)} %all_to_all.35), channel_id=1, source_target_pairs={{0,1},{1,0},{2,3},{3,2},{4,5},{5,4},{6,7},{7,6},{8,9},{9,8},{10,11... | collective-permute-start | bytes 983048 | tf_op jit(solution)/shard_map/ppermute | solution.py:134
  128.9 9.9 %collective-permute-done.1 = bf16[8,64,320]{2,1,0:T(8,128)(2,1)S(1)} collective-permute-done((bf16[8,64,320]{2,1,0:T(8,128)(2,1)S(1)}, bf16[8,64,320]{2,1,0:T(8,128)(2,1)S(1)}, u32[]{:S(2)}, u32[]{:S(2)}) %collective-permute-start.1) | collective-permute-done | bytes 327712 | tf_op jit(solution)/shard_map/ppermute | solution.py:134
  139.0 0.7 slice.82.k_ref
  139.8 0.3 fusion.19
  140.1 0.4 copy-done.1
  140.5 0.9 copy-done.2
  141.4 10.8 %attention.1 = bf16[512,1664]{1,0:T(8,128)(2,1)S(1)} custom-call(bf16[512,768]{1,0:T(8,128)(2,1)S(1)} %bitcast.37, bf16[768,1024]{1,0:T(8,128)(2,1)S(1)} %copy-done.1, bf16[1024,128]{1,0:T(8,128)(2,1)S(1)} %copy-done.2, bf16[1024,256]{1,0:T(8,128)(2,1)S(1)} %get-tuple-element.13.ve_ref, bf16[1024,256]{1,0:T(8,128)(2,1)S(1)} %get-tuple-element.12.vo_ref), custom_call_target="tpu_custom_call" | custom-call | tf_op jit(solution)/shard_map/attention/pallas_call | solution.py:138
  152.3 27.4 %all_to_all.36.parts_ref = bf16[8,64,1664]{2,1,0:T(8,128)(2,1)S(1)} all-to-all(bf16[8,64,1664]{2,1,0:T(8,128)(2,1)S(1)} %bitcast.36), channel_id=1, replica_groups=mesh['xl'=2,'co'=2,'xh'=2,'y'=4,'zt'=8,'zp'=2] {'xh','y'}, dimensions={0} | all-to-all | bytes 3407872 | tf_op jit(solution)/shard_map/all_to_all | solution.py:144
  179.7 1.5 combine.1
  (45 shorter events, 2.3 us)
Async XLA Ops:
  0.6 0.8 copy-start
  0.6 41.2 %copy-start.4 = (bf16[64,768]{1,0:T(8,128)(2,1)S(1)}, bf16[64,768]{1,0:T(8,128)(2,1)}, u32[]{:S(2)}) copy-start(bf16[64,768]{1,0:T(8,128)(2,1)} %param.7) | copy-start | bytes 294916
  2.2 31.1 %all-to-all-start.1 = ((bf16[8,30,192]{2,1,0:T(8,128)(2,1)}), bf16[8,30,192]{2,1,0:T(8,128)(2,1)S(1)}, u32[]{:S(2)}, u32[]{:S(2)}) async-start(bf16[8,30,192]{2,1,0:T(8,128)(2,1)} %broadcast_in_dim.16), calls=%async_computation.1 | async-start | bytes 262144 | tf_op jit(solution)/shard_map/all_to_all | solution.py:23
  17.3 36.0 %copy-start.7 = (f32[768]{0:T(1024)S(1)}, f32[768]{0:T(1024)}, u32[]{:S(2)}) copy-start(f32[768]{0:T(1024)} %param.8) | copy-start | bytes 9220
  34.4 19.1 %all-to-all-start.2 = ((bf16[8,8,30,192]{3,1,2,0:T(8,128)(2,1)}), bf16[8,8,30,192]{3,1,2,0:T(8,128)(2,1)S(1)}, u32[]{:S(2)}, u32[]{:S(2)}) async-start(bf16[8,8,30,192]{3,1,2,0:T(8,128)(2,1)} %broadcast_in_dim.17), calls=%async_computation.2 | async-start | bytes 1966080 | tf_op jit(solution)/shard_map/all_to_all | solution.py:23
  41.8 11.2 %collective-permute-start = (bf16[2,768]{1,0:T(2,128)(2,1)S(1)}, bf16[2,768]{1,0:T(2,128)(2,1)S(1)}, u32[]{:S(2)}, u32[]{:S(2)}) collective-permute-start(bf16[2,768]{1,0:T(2,128)(2,1)S(1)} %broadcast_select_fusion), channel_id=1, source_target_pairs={{1,2},{3,4},{5,6},{7,8},{9,10},{11,12},{13,14},{15,16},{17,18},{19... | collective-permute-start | bytes 9224 | tf_op jit(solution)/shard_map/ppermute | solution.py:112
  54.5 17.1 %all-to-all-start = ((bf16[8,80,768]{2,1,0:T(8,128)(2,1)}), bf16[8,80,768]{2,1,0:T(8,128)(2,1)S(1)}, u32[]{:S(2)}, u32[]{:S(2)}) async-start(bf16[8,80,768]{2,1,0:T(8,128)(2,1)} %broadcast_in_dim.15), calls=%async_computation | async-start | bytes 1966080 | tf_op jit(solution)/shard_map/all_to_all | solution.py:23
  72.2 1.5 copy-start.3
  73.7 7.0 %copy-start.6 = (bf16[768,128]{1,0:T(8,128)(2,1)S(1)}, bf16[768,128]{1,0:T(8,128)(2,1)}, u32[]{:S(2)}) copy-start(bf16[768,128]{1,0:T(8,128)(2,1)} %param.12) | copy-start | bytes 589828
  75.7 13.1 %copy-start.8 = (f32[768]{0:T(1024)S(1)}, f32[768]{0:T(1024)}, u32[]{:S(2)}) copy-start(f32[768]{0:T(1024)} %param.10) | copy-start | bytes 9220
  75.7 13.2 %copy-start.9 = (bf16[768,192]{0,1:T(8,128)(2,1)S(1)}, bf16[768,192]{0,1:T(8,128)(2,1)}, u32[]{:S(2)}) copy-start(bf16[768,192]{0,1:T(8,128)(2,1)} %param.13) | copy-start | bytes 884740
  75.7 12.8 %all-to-all-start.3 = ((f32[8,64,192]{2,1,0:T(8,128)}), f32[8,64,192]{2,1,0:T(8,128)S(1)}, u32[]{:S(2)}, u32[]{:S(2)}) async-start(f32[8,64,192]{2,1,0:T(8,128)} %fusion), calls=%async_computation.3 | async-start | bytes 1048576 | tf_op jit(solution)/shard_map/all_to_all | solution.py:124
  88.8 31.7 %copy-start.5 = (bf16[64,768]{1,0:T(8,128)(2,1)}, bf16[64,768]{1,0:T(8,128)(2,1)S(1)}, u32[]{:S(2)}) copy-start(bf16[64,768]{1,0:T(8,128)(2,1)S(1)} %get-tuple-element.3) | copy-start | bytes 294916
  120.5 19.6 %all-to-all-start.4 = ((bf16[8,64,768]{2,1,0:T(8,128)(2,1)}), bf16[8,64,768]{2,1,0:T(8,128)(2,1)S(1)}, u32[]{:S(2)}, u32[]{:S(2)}) async-start(bf16[8,64,768]{2,1,0:T(8,128)(2,1)} %broadcast_in_dim.19), calls=%async_computation.4 | async-start | bytes 1572864 | tf_op jit(solution)/shard_map/all_to_all | solution.py:23
  126.3 12.6 %collective-permute-start.1 = (bf16[8,64,320]{2,1,0:T(8,128)(2,1)S(1)}, bf16[8,64,320]{2,1,0:T(8,128)(2,1)S(1)}, u32[]{:S(2)}, u32[]{:S(2)}) collective-permute-start(bf16[8,64,320]{2,1,0:T(8,128)(2,1)S(1)} %all_to_all.35), channel_id=1, source_target_pairs={{0,1},{1,0},{2,3},{3,2},{4,5},{5,4},{6,7},{7,6},{8,9},{9,8},{10,11... | collective-permute-start | bytes 983048 | tf_op jit(solution)/shard_map/ppermute | solution.py:134
  139.0 1.5 copy-start.1
  140.5 0.9 copy-start.2

commit v2 on v1

v2 whole, which is shorter than its diff:
```python
import functools

import jax
import jax.numpy as jnp
from jax import lax
from jax.experimental import pallas as pl
from jax.experimental.pallas import tpu as pltpu
from jax.sharding import Mesh
from jax.sharding import PartitionSpec as P

KW = 5
DP = ("xl", "co")
SEQ = ("xh", "y1", "y0", "zt", "zp")
AXES = DP + SEQ
SIZES = (2, 2, 2, 2, 2, 8, 2)
SHARE = ("xl", "co", "zp")
WEIGHT = ("xh", "y1", "y0")
COLUMN = ("y1", "y0")
SPREAD = COLUMN + ("zp",)
STATS = 128


def everyone(block, axes, count):
    sent = jnp.broadcast_to(block[None], (count,) + block.shape)
    return lax.all_to_all(sent, axes, 0, 0, tiled=True)


def swapped(block, axis):
    return lax.ppermute(block, axis, [(0, 1), (1, 0)])


def by_masks(block, axes):
    count = 2 ** len(axes)
    return [block] + [
        lax.ppermute(block, axes, [(i, i ^ mask) for i in range(count)]) for mask in range(1, count)
    ]


def normalize(values, gain):
    mean_square = jnp.mean(values * values, axis=-1, keepdims=True)
    return values * lax.rsqrt(mean_square + 1e-06) * gain


def conv_kernel(place_ref, mine_ref, other_ref, end_ref, far_end_ref, w_ref, out_ref, wide_ref):
    group, zp = place_ref[0], place_ref[1]
    parts, rows, width = mine_ref.shape
    count, depth = w_ref.shape[0], KW * width // 128
    wide_ref[...] = jnp.zeros_like(wide_ref)
    for side in range(2):

        @pl.when(zp == side)
        def _():
            for i in range(count):
                start = (2 * i + side) * depth
                block = w_ref[i].astype(jnp.float32)
                tail = block[32:48]
                wide_ref[start : start + depth, :128] = block[:depth]
                wide_ref[start : start + depth // 2, 128:] = tail[: depth // 2]
                wide_ref[start + depth // 2 : start + depth, 128:] = pltpu.roll(tail, 64, 1)[: depth // 2]

    even = zp == 0
    mine, other = mine_ref[...], other_ref[:parts]
    first, second = jnp.where(even, mine, other), jnp.where(even, other, mine)
    x = jnp.concatenate([first, second], axis=1).reshape(2 * parts * rows, width)
    end, far_end = end_ref[...].astype(jnp.float32), far_end_ref[...].astype(jnp.float32)
    before, after = jnp.where(even, end, far_end), jnp.where(even, far_end, end)
    ends = jnp.concatenate([before.reshape(2 * parts, width), after.reshape(2 * parts, width)]).astype(jnp.bfloat16)
    sums = [None] * parts
    for offset in range(KW):
        w = wide_ref[offset * width : (offset + 1) * width, :].astype(jnp.bfloat16)
        y = jnp.dot(x, w, preferred_element_type=jnp.float32)
        z = jnp.dot(ends, w, preferred_element_type=jnp.float32)
        for part in range(parts):
            body = y[2 * part * rows : 2 * (part + 1) * rows]
            before, after = z[2 * part : 2 * part + 2], z[2 * (parts + part) : 2 * (parts + part) + 2]
            term = jnp.concatenate([before, body, after])[offset : offset + 2 * rows]
            sums[part] = term if offset == 0 else sums[part] + term
    for part in range(parts):
        index = jnp.bitwise_xor(group, part)
        value = sums[part][:, : out_ref.shape[2]].astype(jnp.bfloat16)
        out_ref[2 * index] = value
        out_ref[2 * index + 1] = value


def unpack(ref, k_ref, ve_ref, vo_ref):
    lane = lax.broadcasted_iota(jnp.int32, (32, 128), 1)
    one = jnp.ones((32, 128), jnp.float32)
    count = ref.shape[0]
    keys = jnp.concatenate([ref[block, 0:64, :] for block in range(count)])
    k_ref[...] = keys.astype(jnp.float32).T.astype(jnp.bfloat16)
    for block in range(count):
        base = block * 64
        tail = ref[block, 128:160, :].astype(jnp.float32)
        turned = pltpu.roll(tail, 64, 1)
        for half in range(2):
            here = slice(base + 32 * half, base + 32 * half + 32)
            low = ref[block, 64 + 32 * half : 96 + 32 * half, :].astype(jnp.float32)
            shifted = pltpu.roll(low, 64, 1)
            left, right = (turned, tail) if half else (tail, turned)
            ve_ref[here, 0:128] = low.astype(jnp.bfloat16)
            ve_ref[here, 128:256] = jnp.where(lane < 64, left, one).astype(jnp.bfloat16)
            vo_ref[here, 0:128] = jnp.where(lane < 64, one, shifted).astype(jnp.bfloat16)
            vo_ref[here, 128:256] = jnp.where(lane < 64, shifted, right).astype(jnp.bfloat16)


def near_kernel(heads, size, *refs):
    x_refs, (qw_ref, pack_ref, q_ref, o_ref, top_ref, k_ref, ve_ref, vo_ref) = refs[:4], refs[4:]
    unpack(pack_ref, k_ref, ve_ref, vo_ref)
    x = jnp.concatenate([ref[...] for ref in x_refs])
    q = jnp.dot(x, qw_ref[...], preferred_element_type=jnp.float32) * size ** (-0.5)
    q_ref[...] = q.astype(jnp.bfloat16)
    rows, chunk = x.shape[0], 256
    lane = lax.broadcasted_iota(jnp.int32, (chunk, 128), 1)
    for start in range(0, rows, chunk):
        part = slice(start, start + chunk)
        tops = jnp.zeros((chunk, 128), jnp.float32)
        for head in range(heads):
            q = q_ref[part, head * size : (head + 1) * size]
            s = jnp.dot(q, k_ref[...], preferred_element_type=jnp.float32)
            top = jnp.max(s, axis=-1, keepdims=True)
            p = jnp.exp(s - top).astype(jnp.bfloat16)
            v_ref = vo_ref if head % 2 else ve_ref
            o_ref[head, part, :] = jnp.dot(p, v_ref[...], preferred_element_type=jnp.float32)
            tops = jnp.where(lane == head, top, tops)
        top_ref[part, :] = tops


def far_kernel(heads, size, place_ref, q_ref, o_ref, top_ref, pack_ref, out_ref, k_ref, ve_ref, vo_ref):
    unpack(pack_ref, k_ref, ve_ref, vo_ref)
    place = place_ref[0]
    rows, chunk, block = q_ref.shape[0], 256, out_ref.shape[1]
    lane = lax.broadcasted_iota(jnp.int32, (chunk, 128), 1)
    for start in range(0, rows, chunk):
        part = slice(start, start + chunk)
        tops = top_ref[part, :]

        def put(low, value):
            value = value.astype(jnp.bfloat16)
            for i in range(chunk // block):
                at = start // block + i
                index = 2 * jnp.bitwise_xor(place, at // 2) + at % 2
                out_ref[index, :, low : low + 128] = value[i * block : (i + 1) * block]

        stats = jnp.zeros((chunk, STATS), jnp.float32)
        for pair in range(heads // 2):
            halves = []
            for odd in range(2):
                head = 2 * pair + odd
                q = q_ref[part, head * size : (head + 1) * size]
                s = jnp.dot(q, k_ref[...], preferred_element_type=jnp.float32)
                old = tops[:, head : head + 1]
                peak = jnp.maximum(jnp.max(s, axis=-1, keepdims=True), old)
                p = jnp.exp(s - peak).astype(jnp.bfloat16)
                v_ref = vo_ref if odd else ve_ref
                o = jnp.dot(p, v_ref[...], preferred_element_type=jnp.float32)
                o = o + o_ref[head, part, :] * jnp.exp(old - peak)
                halves.append(o)
                if odd:
                    stats = jnp.where(lane == head, o[:, :128], stats)
                else:
                    stats = jnp.where(lane == 64 + head, o[:, 128:], stats)
                stats = jnp.where(lane == 16 + head, peak, stats)
            even, odd = halves
            base = pair * 384
            put(base, even[:, :128])
            put(base + 128, jnp.where(lane < 64, even[:, 128:], odd[:, :128]))
            put(base + 256, odd[:, 128:])
        first = stats.astype(jnp.bfloat16).astype(jnp.float32)
        rest = stats - first
        second = rest.astype(jnp.bfloat16).astype(jnp.float32)
        third = rest - second
        put(heads * 192, first + pltpu.roll(second, 8, 1) + pltpu.roll(third, 32, 1))


def combine_kernel(heads, parts_ref, out_ref):
    count, rows, _ = parts_ref.shape
    lane = lax.broadcasted_iota(jnp.int32, (rows, 128), 1)
    base = heads * 192
    parts = []
    for i in range(count):
        stats = parts_ref[i, :, base:].astype(jnp.float32)
        parts.append(stats + pltpu.roll(stats, STATS - 8, 1) + pltpu.roll(stats, STATS - 32, 1))
    weights = []
    for head in range(heads):
        sum_lane = head if head % 2 else 64 + head
        peaks = [part[:, 16 + head : 17 + head] for part in parts]
        top = functools.reduce(jnp.maximum, peaks)
        scales = [jnp.exp(peak - top) for peak in peaks]
        terms = [part[:, sum_lane : sum_lane + 1] * scale for part, scale in zip(parts, scales)]
        inverse = 1.0 / functools.reduce(jnp.add, terms)
        weights.append([scale * inverse for scale in scales])
    for tile in range(heads * 192 // 128):
        low, high = tile * 128 // 192, (tile * 128 + 127) // 192
        total = jnp.zeros((rows, 128), jnp.float32)
        for i in range(count):
            weight = weights[low][i]
            if high != low:
                weight = jnp.where(lane < high * 192 - tile * 128, weight, weights[high][i])
            total = total + weight * parts_ref[i, :, tile * 128 : tile * 128 + 128].astype(jnp.float32)
        out_ref[:, tile * 128 : tile * 128 + 128] = total.astype(jnp.bfloat16)


def local(features, conv_gain, conv_weight, attn_gain, query_weight, key_weight, value_weight):
    rows, width = features.shape
    size = key_weight.shape[1]
    value_size = value_weight.shape[1]
    heads = query_weight.shape[1] // size
    zp = lax.axis_index("zp")
    group = lax.axis_index(DP)
    columns = width // 4

    half = conv_weight.shape[0] // 2
    whole = lax.dynamic_slice_in_dim(conv_weight, group * 128, 128, axis=1)
    rest = lax.dynamic_slice_in_dim(conv_weight, 512 + group * 64, 64, axis=1)
    rest = jnp.concatenate([rest[:half], rest[half:]], axis=1)
    blocks = everyone(jnp.concatenate([jnp.pad(whole, ((0, 2), (0, 0))), jnp.pad(rest, ((0, 1), (0, 0)))]), "zt", 8)
    shared = by_masks(features, DP)
    blocks, *shared = lax.optimization_barrier((blocks, *shared))

    shared = jnp.stack(shared).astype(jnp.float32)
    activated = jax.nn.gelu(normalize(shared, conv_gain), approximate=True).astype(jnp.bfloat16)
    blocks = everyone(blocks, WEIGHT, 8).reshape(64, 48, 128)
    edge = jnp.where(zp == 0, activated[:, :2], activated[:, rows - 2 :])
    odd, even = range(1, 128, 2), range(0, 128, 2)
    steps = [
        [(i, i + step) for i in odd if i + step < 128] + [(i, i - step) for i in even if i - step >= 0]
        for step in (1, 2)
    ]
    end, far_end = (lax.ppermute(edge, SEQ, step) for step in steps)
    other = swapped(jnp.concatenate([activated, features[None]]), "zp")
    beside = other[4]
    partial = pl.pallas_call(
        conv_kernel,
        out_shape=jax.ShapeDtypeStruct((8, 2 * rows, columns), jnp.bfloat16),
        in_specs=[pl.BlockSpec(memory_space=pltpu.SMEM)] + [pl.BlockSpec(memory_space=pltpu.VMEM)] * 5,
        out_specs=pl.BlockSpec(memory_space=pltpu.VMEM),
        scratch_shapes=[pltpu.VMEM((KW * width, 256), jnp.float32)],
        compiler_params=pltpu.CompilerParams(vmem_limit_bytes=32 * 1024 * 1024),
        name="conv",
    )(jnp.stack([group, zp]), activated, other, end, far_end, blocks)
    partial = lax.all_to_all(partial, SHARE, 0, 0, tiled=True).astype(jnp.float32)
    partial = partial.reshape(4, 2, 2 * rows, columns).sum(axis=1)
    conv_out = jnp.concatenate(
        [partial[i][:, :128] for i in range(4)] + [partial[i][:, 128:] for i in range(4)], axis=1
    )
    mine_first = jnp.concatenate([features, beside])
    other_first = jnp.concatenate([beside, features])
    inputs = jnp.where(zp == 0, mine_first, other_first).astype(jnp.float32)

    wide_stream = (inputs + conv_out).astype(jnp.bfloat16)
    stream = jnp.where(zp == 0, wide_stream[:rows], wide_stream[rows:])
    wide_in = normalize(wide_stream.astype(jnp.float32), attn_gain).astype(jnp.bfloat16)
    attn_in = jnp.where(zp == 0, wide_in[:rows], wide_in[rows:])
    both = jnp.concatenate([key_weight, value_weight], axis=1)
    pairs = jnp.dot(attn_in, both, preferred_element_type=jnp.float32).astype(jnp.bfloat16)
    tail = pairs[:, 256:]
    tail = jnp.concatenate([tail[: rows // 2], tail[rows // 2 :]], axis=1)
    packed = jnp.concatenate([pairs[:, :128], pairs[:, 128:256], tail])
    near = everyone(packed, "zt", 8)
    asked = by_masks(wide_in, COLUMN)
    near, *asked = lax.optimization_barrier((near, *asked))
    far = swapped(near, "xh")
    scratch = [
        pltpu.VMEM((size, 8 * rows), jnp.bfloat16),
        pltpu.VMEM((8 * rows, 256), jnp.bfloat16),
        pltpu.VMEM((8 * rows, 256), jnp.bfloat16),
    ]
    in_vmem = pl.BlockSpec(memory_space=pltpu.VMEM)
    cost = pl.CostEstimate(flops=4_500_000_000, bytes_accessed=8_000_000, transcendentals=2_200_000)
    params = pltpu.CompilerParams(vmem_limit_bytes=32 * 1024 * 1024)
    queries, weighted, tops = pl.pallas_call(
        functools.partial(near_kernel, heads, size),
        out_shape=[
            jax.ShapeDtypeStruct((8 * rows, heads * size), jnp.bfloat16),
            jax.ShapeDtypeStruct((heads, 8 * rows, 256), jnp.float32),
            jax.ShapeDtypeStruct((8 * rows, 128), jnp.float32),
        ],
        in_specs=[in_vmem] * 6,
        out_specs=[in_vmem] * 3,
        scratch_shapes=scratch,
        compiler_params=params,
        cost_estimate=cost,
        name="near",
    )(*asked, query_weight, near)
    out = pl.pallas_call(
        functools.partial(far_kernel, heads, size),
        out_shape=jax.ShapeDtypeStruct((8, rows, heads * value_size + STATS), jnp.bfloat16),
        in_specs=[pl.BlockSpec(memory_space=pltpu.SMEM)] + [in_vmem] * 4,
        out_specs=in_vmem,
        scratch_shapes=scratch,
        compiler_params=params,
        cost_estimate=cost,
        name="far",
    )(lax.axis_index(COLUMN)[None], queries, weighted, tops, far)
    parts = lax.all_to_all(out, SPREAD, 0, 0, tiled=True)
    attended = pl.pallas_call(
        functools.partial(combine_kernel, heads),
        out_shape=jax.ShapeDtypeStruct((rows, heads * value_size), jnp.bfloat16),
        compiler_params=pltpu.CompilerParams(vmem_limit_bytes=32 * 1024 * 1024),
        name="combine",
    )(parts)
    return (stream, attended)


def solution(mesh):
    finer = Mesh(mesh.devices.reshape(SIZES), AXES)
    placed = (P(AXES, None), P(), P(SEQ, None), P(), P(), P(), P())
    return jax.shard_map(
        local,
        mesh=finer,
        in_specs=placed,
        out_specs=(P(AXES, None), P(AXES, None)),
        check_vma=False,
    )
```

time: 183 us -> 154 us (0.84)
  blocking collectives: 57.6 us -> 0 us
  starting transfers between devices: 43 us -> 69.9 us
  waiting for transfers between devices: 51.1 us -> 58.2 us
  local copies, waits for them, and re-layouts: 12.2 us -> 5.93 us
  matrix products: 2.25 us -> 0.27 us
    all_to_all x2 -> x0, blocking collectives: 57.6 us -> none  [the longest x1 30.3 us: everyone(): return lax.all_to_all(sent, axes, 0, 0, tiled=True)]
    ppermute x2 -> x10, starting transfers between devices: 5.32 us -> 35.3 us  [the longest x6 17.4 us: by_masks(): lax.ppermute(block, axes, [(i, i ^ mask) for i in range(count)])]
    all_to_all x1 -> x2, waiting for transfers between devices: 7.63 us -> 27.6 us  [the longest x1 21.4 us: local(): parts = lax.all_to_all(out, SPREAD, 0, 0, tiled=True)]
    all_to_all x4 -> x3, waiting for transfers between devices: 25.1 us -> 12.6 us  [everyone(): return lax.all_to_all(sent, axes, 0, 0, tiled=True)]
    all_to_all x4 -> x3, starting transfers between devices: 32.6 us -> 26.2 us  [everyone(): return lax.all_to_all(sent, axes, 0, 0, tiled=True)]
    all_to_all x1 -> x2, starting transfers between devices: 5.03 us -> 8.42 us  [the longest x1 4.22 us: local(): parts = lax.all_to_all(out, SPREAD, 0, 0, tiled=True)]
    unnamed x24 -> x17, local copies, waits for them, and re-layouts: 3.92 us -> 0.78 us
    dot_general x1 -> x0, matrix products: 1.98 us -> none  [local(): jnp.dot(windows.reshape(8 * rows, KW * width), kernel.reshape(KW * width,...]
  transfers between devices with their start and end apart: 7 -> 15, of which waited for: 5 -> 10; matrix products, arithmetic and copies ran while one was open for 3% -> 1% of each run, Pallas kernels for 0% -> 2%
where the time goes in v2:
time: 154 us; the launch traced here: 152 us
  starting transfers between devices  69.9 us (45%)
  waiting for transfers between devices  58.2 us (38%)
  Pallas kernels  14.2 us (9%)
  local copies, waits for them, and re-layouts  5.93 us (4%)
  other arithmetic  2.77 us (2%)
    all_to_all x3, starting transfers between devices, everyone(): return lax.all_to_all(sent, axes, 0, 0, tiled=True)  26.2 us
    all_to_all x1, waiting for transfers between devices, local(): parts = lax.all_to_all(out, SPREAD, 0, 0, tiled=True)  21.4 us
    ppermute x6, starting transfers between devices, by_masks(): lax.ppermute(block, axes, [(i, i ^ mask) for i in range(count)])  17.4 us
    all_to_all x3, waiting for transfers between devices, everyone(): return lax.all_to_all(sent, axes, 0, 0, tiled=True)  12.6 us
    ppermute x2, starting transfers between devices, local(): end, far_end = (lax.ppermute(edge, SEQ, step) for step in steps)  11.9 us
    ppermute x6, waiting for transfers between devices, by_masks(): lax.ppermute(block, axes, [(i, i ^ mask) for i in range(count)])  8.99 us
    ppermute x2, waiting for transfers between devices, swapped(): return lax.ppermute(block, axis, [(0, 1), (1, 0)])  6.33 us
    pallas_call x1, Pallas kernels, local(): pl.pallas_call(functools.partial(far_kernel, heads, size), out_shape=jax....  6.29 us
  transfers between devices with their start and end apart: 15, of which 10 were waited for; matrix products, arithmetic and copies ran while one was open for 1% of the time, Pallas kernels for 2%

profile of v2, /device:TPU:6, one launch (start us, length us, event | category | flops | bytes accessed | tf_op | source)
XLA Modules:
  0.0 152.3 jit_solution(4120727745480779918)
XLA Ops:
  3.0 15.1 %all-to-all-start = ((bf16[8,48,128]{2,1,0:T(8,128)(2,1)}), bf16[8,48,128]{2,1,0:T(8,128)(2,1)S(1)}, u32[]{:S(2)}, u32[]{:S(2)}) async-start(bf16[8,48,128]{2,1,0:T(8,128)(2,1)} %broadcast_in_dim.10), calls=%async_computation | async-start | bytes 196608 | tf_op jit(solution)/shard_map/all_to_all | solution.py:25
  18.1 1.9 %collective-permute-start.2 = (bf16[64,768]{1,0:T(8,128)(2,1)}, bf16[64,768]{1,0:T(8,128)(2,1)S(1)}, u32[]{:S(2)}, u32[]{:S(2)}) collective-permute-start(bf16[64,768]{1,0:T(8,128)(2,1)} %param.7), channel_id=1, source_target_pairs={{0,384},{128,256},{256,128},{384,0},{1,385},{129,257},{257,129},{3... | collective-permute-start | bytes 294920 | tf_op jit(solution)/shard_map/ppermute | solution.py:35
  20.0 3.1 %collective-permute-start.1 = (bf16[64,768]{1,0:T(8,128)(2,1)}, bf16[64,768]{1,0:T(8,128)(2,1)S(1)}, u32[]{:S(2)}, u32[]{:S(2)}) collective-permute-start(bf16[64,768]{1,0:T(8,128)(2,1)} %param.7), channel_id=1, source_target_pairs={{0,256},{128,384},{256,0},{384,128},{1,257},{129,385},{257,1},{385... | collective-permute-start | bytes 294920 | tf_op jit(solution)/shard_map/ppermute | solution.py:35
  23.1 2.6 %collective-permute-start = (bf16[64,768]{1,0:T(8,128)(2,1)}, bf16[64,768]{1,0:T(8,128)(2,1)S(1)}, u32[]{:S(2)}, u32[]{:S(2)}) collective-permute-start(bf16[64,768]{1,0:T(8,128)(2,1)} %param.7), channel_id=1, source_target_pairs={{0,128},{128,0},{256,384},{384,256},{1,129},{129,1},{257,385},{385... | collective-permute-start | bytes 294920 | tf_op jit(solution)/shard_map/ppermute | solution.py:35
  25.7 2.0 %collective-permute-done.1 = bf16[64,768]{1,0:T(8,128)(2,1)S(1)} collective-permute-done((bf16[64,768]{1,0:T(8,128)(2,1)}, bf16[64,768]{1,0:T(8,128)(2,1)S(1)}, u32[]{:S(2)}, u32[]{:S(2)}) %collective-permute-start.1) | collective-permute-done | bytes 98336 | tf_op jit(solution)/shard_map/ppermute | solution.py:35
  27.7 5.3 %all-to-all-done = bf16[8,48,128]{2,1,0:T(8,128)(2,1)S(1)} async-done(((bf16[8,48,128]{2,1,0:T(8,128)(2,1)}), bf16[8,48,128]{2,1,0:T(8,128)(2,1)S(1)}, u32[]{:S(2)}, u32[]{:S(2)}) %all-to-all-start) | async-done | bytes 98336 | tf_op jit(solution)/shard_map/all_to_all | solution.py:25
  33.0 1.0 fusion
  34.1 1.0 broadcast_in_dim.12
  35.1 7.4 %all-to-all-start.1 = ((bf16[8,8,48,128]{3,2,1,0:T(8,128)(2,1)}), bf16[8,8,48,128]{3,2,1,0:T(8,128)(2,1)S(1)}, u32[]{:S(2)}, u32[]{:S(2)}) async-start(bf16[8,8,48,128]{3,2,1,0:T(8,128)(2,1)} %broadcast_in_dim.12), calls=%async_computation.1 | async-start | bytes 1572864 | tf_op jit(solution)/shard_map/all_to_all | solution.py:25
  42.9 3.1 %collective-permute-start.3 = (bf16[5,64,768]{2,1,0:T(8,128)(2,1)S(1)}, bf16[5,64,768]{2,1,0:T(8,128)(2,1)S(1)}, u32[]{:S(2)}, u32[]{:S(2)}) collective-permute-start(bf16[5,64,768]{2,1,0:T(8,128)(2,1)S(1)} %pad_maximum_fusion), channel_id=1, source_target_pairs={{0,1},{1,0},{2,3},{3,2},{4,5},{5,4},{6,7},{7,6},{8,9},{9,8},{10,11... | collective-permute-start | bytes 1474568 | tf_op jit(solution)/shard_map/ppermute | solution.py:29
  46.1 3.3 %collective-permute-start.5 = (bf16[4,2,768]{2,1,0:T(2,128)(2,1)S(1)}, bf16[4,2,768]{2,1,0:T(2,128)(2,1)S(1)}, u32[]{:S(2)}, u32[]{:S(2)}) collective-permute-start(bf16[4,2,768]{2,1,0:T(2,128)(2,1)S(1)} %broadcast_select_fusion), channel_id=1, source_target_pairs={{1,3},{3,5},{5,7},{7,9},{9,11},{11,13},{13,15},{15,17},{17,19},{19... | collective-permute-start | bytes 36872 | tf_op jit(solution)/shard_map/ppermute | solution.py:229
  49.4 8.5 %collective-permute-start.4 = (bf16[4,2,768]{2,1,0:T(2,128)(2,1)S(1)}, bf16[4,2,768]{2,1,0:T(2,128)(2,1)S(1)}, u32[]{:S(2)}, u32[]{:S(2)}) collective-permute-start(bf16[4,2,768]{2,1,0:T(2,128)(2,1)S(1)} %broadcast_select_fusion), channel_id=1, source_target_pairs={{1,2},{3,4},{5,6},{7,8},{9,10},{11,12},{13,14},{15,16},{17,18},{19... | collective-permute-start | bytes 36872 | tf_op jit(solution)/shard_map/ppermute | solution.py:229
  58.0 2.7 %collective-permute-done.4.end_ref = bf16[4,2,768]{2,1,0:T(2,128)(2,1)S(1)} collective-permute-done((bf16[4,2,768]{2,1,0:T(2,128)(2,1)S(1)}, bf16[4,2,768]{2,1,0:T(2,128)(2,1)S(1)}, u32[]{:S(2)}, u32[]{:S(2)}) %collective-permute-start.4) | collective-permute-done | bytes 12320 | tf_op jit(solution)/shard_map/ppermute | solution.py:229
  60.7 2.5 %conv.1 = bf16[8,128,192]{2,1,0:T(8,128)(2,1)S(1)} custom-call(s32[2]{0:T(128)S(1)} %pad_add_fusion.place_ref, bf16[4,64,768]{2,1,0:T(8,128)(2,1)S(1)} %fusion.4.mine_ref, bf16[5,64,768]{2,1,0:T(8,128)(2,1)S(1)} %collective-permute-done.3.other_ref, bf16[4,2,768]{2,1,0:T(2,128)(2,1)S(1)} %collective-permute-done.4.end_ref, ...), custom_call_target="tpu_custom_call" | custom-call | tf_op jit(solution)/shard_map/conv/pallas_call | solution.py:232
  63.2 1.0 copy.12
  64.2 4.2 %all-to-all-start.2 = ((bf16[8,128,192]{1,2,0:T(8,128)(2,1)}), bf16[8,128,192]{1,2,0:T(8,128)(2,1)S(1)}, u32[]{:S(2)}, u32[]{:S(2)}) async-start(bf16[8,128,192]{1,2,0:T(8,128)(2,1)} %copy.12), calls=%async_computation.2 | async-start | bytes 786432 | tf_op jit(solution)/shard_map/all_to_all | solution.py:241
  68.6 6.2 %all-to-all-done.2 = bf16[8,128,192]{1,2,0:T(8,128)(2,1)S(1)} async-done(((bf16[8,128,192]{1,2,0:T(8,128)(2,1)}), bf16[8,128,192]{1,2,0:T(8,128)(2,1)S(1)}, u32[]{:S(2)}, u32[]{:S(2)}) %all-to-all-start.2) | async-done | bytes 393248 | tf_op jit(solution)/shard_map/all_to_all | solution.py:241
  77.2 3.6 %all-to-all-start.3 = ((bf16[8,160,128]{2,1,0:T(8,128)(2,1)}), bf16[8,160,128]{2,1,0:T(8,128)(2,1)S(1)}, u32[]{:S(2)}, u32[]{:S(2)}) async-start(bf16[8,160,128]{2,1,0:T(8,128)(2,1)} %broadcast_in_dim.14), calls=%async_computation.3 | async-start | bytes 655360 | tf_op jit(solution)/shard_map/all_to_all | solution.py:25
  80.9 4.6 %collective-permute-start.8 = (bf16[128,768]{1,0:T(8,128)(2,1)S(1)}, bf16[128,768]{1,0:T(8,128)(2,1)S(1)}, u32[]{:S(2)}, u32[]{:S(2)}) collective-permute-start(bf16[128,768]{1,0:T(8,128)(2,1)S(1)} %fusion.15.refs_0_), channel_id=1, source_target_pairs={{0,48},{16,32},{32,16},{48,0},{1,49},{17,33},{33,17},{49,1},{2,50}... | collective-permute-start | bytes 589832 | tf_op jit(solution)/shard_map/ppermute | solution.py:35
  85.5 2.8 %collective-permute-start.7 = (bf16[128,768]{1,0:T(8,128)(2,1)S(1)}, bf16[128,768]{1,0:T(8,128)(2,1)S(1)}, u32[]{:S(2)}, u32[]{:S(2)}) collective-permute-start(bf16[128,768]{1,0:T(8,128)(2,1)S(1)} %fusion.15.refs_0_), channel_id=1, source_target_pairs={{0,32},{16,48},{32,0},{48,16},{1,33},{17,49},{33,1},{49,17},{2,34}... | collective-permute-start | bytes 589832 | tf_op jit(solution)/shard_map/ppermute | solution.py:35
  88.2 2.5 %collective-permute-start.6 = (bf16[128,768]{1,0:T(8,128)(2,1)S(1)}, bf16[128,768]{1,0:T(8,128)(2,1)S(1)}, u32[]{:S(2)}, u32[]{:S(2)}) collective-permute-start(bf16[128,768]{1,0:T(8,128)(2,1)S(1)} %fusion.15.refs_0_), channel_id=1, source_target_pairs={{0,16},{16,0},{32,48},{48,32},{1,17},{17,1},{33,49},{49,33},{2,18}... | collective-permute-start | bytes 589832 | tf_op jit(solution)/shard_map/ppermute | solution.py:35
  90.7 3.3 %collective-permute-done.8.refs_3_ = bf16[128,768]{1,0:T(8,128)(2,1)S(1)} collective-permute-done((bf16[128,768]{1,0:T(8,128)(2,1)S(1)}, bf16[128,768]{1,0:T(8,128)(2,1)S(1)}, u32[]{:S(2)}, u32[]{:S(2)}) %collective-permute-start.8) | collective-permute-done | bytes 196640 | tf_op jit(solution)/shard_map/ppermute | solution.py:35
  94.1 2.6 %collective-permute-done.7.refs_2_ = bf16[128,768]{1,0:T(8,128)(2,1)S(1)} collective-permute-done((bf16[128,768]{1,0:T(8,128)(2,1)S(1)}, bf16[128,768]{1,0:T(8,128)(2,1)S(1)}, u32[]{:S(2)}, u32[]{:S(2)}) %collective-permute-start.7) | collective-permute-done | bytes 196640 | tf_op jit(solution)/shard_map/ppermute | solution.py:35
  96.7 1.0 collective-permute-done.6.refs_1_
  97.7 7.4 %all-to-all-done.3.refs_5_ = bf16[8,160,128]{2,1,0:T(8,128)(2,1)S(1)} async-done(((bf16[8,160,128]{2,1,0:T(8,128)(2,1)}), bf16[8,160,128]{2,1,0:T(8,128)(2,1)S(1)}, u32[]{:S(2)}, u32[]{:S(2)}) %all-to-all-start.3) | async-done | bytes 327712 | tf_op jit(solution)/shard_map/all_to_all | solution.py:25
  105.0 3.0 %collective-permute-start.9 = (bf16[8,160,128]{2,1,0:T(8,128)(2,1)S(1)}, bf16[8,160,128]{2,1,0:T(8,128)(2,1)S(1)}, u32[]{:S(2)}, u32[]{:S(2)}) collective-permute-start(bf16[8,160,128]{2,1,0:T(8,128)(2,1)S(1)} %all-to-all-done.3.refs_5_), channel_id=1, source_target_pairs={{0,64},{64,0},{1,65},{65,1},{2,66},{66,2},{3,67},{67,3},{4,68},{68... | collective-permute-start | bytes 983048 | tf_op jit(solution)/shard_map/ppermute | solution.py:29
  108.0 3.7 %near.1 = (bf16[512,1024]{1,0:T(8,128)(2,1)S(1)}, f32[8,512,256]{2,1,0:T(8,128)S(1)}, f32[512,128]{1,0:T(8,128)S(1)}) custom-call(bf16[128,768]{1,0:T(8,128)(2,1)S(1)} %fusion.15.refs_0_, bf16[128,768]{1,0:T(8,128)(2,1)S(1)} %collective-permute-done.6.refs_1_, bf16[128,768]{1,0:T(8,128)(2,1)S(1)} %collective-permute-done.7.refs_2_, ...), custom_call_target="tpu_custom_call" | custom-call | flops 4499999744 | bytes 8000000 | tf_op jit(solution)/shard_map/near/pallas_call | solution.py:271
  111.7 6.3 %collective-permute-done.9.pack_ref = bf16[8,160,128]{2,1,0:T(8,128)(2,1)S(1)} collective-permute-done((bf16[8,160,128]{2,1,0:T(8,128)(2,1)S(1)}, bf16[8,160,128]{2,1,0:T(8,128)(2,1)S(1)}, u32[]{:S(2)}, u32[]{:S(2)}) %collective-permute-start.9) | collective-permute-done | bytes 327712 | tf_op jit(solution)/shard_map/ppermute | solution.py:29
  118.0 6.3 %far.1 = bf16[8,64,1664]{2,1,0:T(8,128)(2,1)} custom-call(s32[1]{0:T(128)} %bitcast.14.place_ref, bf16[512,1024]{1,0:T(8,128)(2,1)S(1)} %get-tuple-element.25.q_ref, f32[8,512,256]{2,1,0:T(8,128)S(1)} %get-tuple-element.26.o_ref, f32[512,128]{1,0:T(8,128)S(1)} %get-tuple-element.27.top_ref, bf16[8,160,128]{2,1,0:T(8,128)(2,1)S(1)} %collective-permute-done.9.pack_ref), custom_call_target="tpu_custom_call" | custom-call | flops 4499999744 | bytes 8000000 | tf_op jit(solution)/shard_map/far/pallas_call | solution.py:285
  124.3 4.2 %all-to-all-start.4 = ((bf16[8,64,1664]{2,1,0:T(8,128)(2,1)}), bf16[8,64,1664]{2,1,0:T(8,128)(2,1)S(1)}, u32[]{:S(2)}, u32[]{:S(2)}) async-start(bf16[8,64,1664]{2,1,0:T(8,128)(2,1)} %far.1), calls=%async_computation.4 | async-start | bytes 3407872 | tf_op jit(solution)/shard_map/all_to_all | solution.py:295
  129.2 21.4 %all-to-all-done.4.parts_ref = bf16[8,64,1664]{2,1,0:T(8,128)(2,1)S(1)} async-done(((bf16[8,64,1664]{2,1,0:T(8,128)(2,1)}), bf16[8,64,1664]{2,1,0:T(8,128)(2,1)S(1)}, u32[]{:S(2)}, u32[]{:S(2)}) %all-to-all-start.4) | async-done | bytes 1703968 | tf_op jit(solution)/shard_map/all_to_all | solution.py:295
  150.5 1.8 %combine.1 = bf16[64,1536]{1,0:T(8,128)(2,1)} custom-call(bf16[8,64,1664]{2,1,0:T(8,128)(2,1)S(1)} %all-to-all-done.4.parts_ref), custom_call_target="tpu_custom_call" | custom-call | tf_op jit(solution)/shard_map/combine/pallas_call | solution.py:296
  (53 shorter events, 6.0 us)
Async XLA Ops:
  0.6 41.9 %copy-start.1 = (bf16[64,768]{1,0:T(8,128)(2,1)S(1)}, bf16[64,768]{1,0:T(8,128)(2,1)}, u32[]{:S(2)}) copy-start(bf16[64,768]{1,0:T(8,128)(2,1)} %param.7) | copy-start | bytes 294916
  0.6 41.9 %copy-start.3 = (f32[768]{0:T(1024)S(1)}, f32[768]{0:T(1024)}, u32[]{:S(2)}) copy-start(f32[768]{0:T(1024)} %param.8) | copy-start | bytes 9220
  3.0 30.0 %all-to-all-start = ((bf16[8,48,128]{2,1,0:T(8,128)(2,1)}), bf16[8,48,128]{2,1,0:T(8,128)(2,1)S(1)}, u32[]{:S(2)}, u32[]{:S(2)}) async-start(bf16[8,48,128]{2,1,0:T(8,128)(2,1)} %broadcast_in_dim.10), calls=%async_computation | async-start | bytes 196608 | tf_op jit(solution)/shard_map/all_to_all | solution.py:25
  18.1 7.6 %collective-permute-start.2 = (bf16[64,768]{1,0:T(8,128)(2,1)}, bf16[64,768]{1,0:T(8,128)(2,1)S(1)}, u32[]{:S(2)}, u32[]{:S(2)}) collective-permute-start(bf16[64,768]{1,0:T(8,128)(2,1)} %param.7), channel_id=1, source_target_pairs={{0,384},{128,256},{256,128},{384,0},{1,385},{129,257},{257,129},{3... | collective-permute-start | bytes 294920 | tf_op jit(solution)/shard_map/ppermute | solution.py:35
  20.0 7.7 %collective-permute-start.1 = (bf16[64,768]{1,0:T(8,128)(2,1)}, bf16[64,768]{1,0:T(8,128)(2,1)S(1)}, u32[]{:S(2)}, u32[]{:S(2)}) collective-permute-start(bf16[64,768]{1,0:T(8,128)(2,1)} %param.7), channel_id=1, source_target_pairs={{0,256},{128,384},{256,0},{384,128},{1,257},{129,385},{257,1},{385... | collective-permute-start | bytes 294920 | tf_op jit(solution)/shard_map/ppermute | solution.py:35
  23.1 4.6 %collective-permute-start = (bf16[64,768]{1,0:T(8,128)(2,1)}, bf16[64,768]{1,0:T(8,128)(2,1)S(1)}, u32[]{:S(2)}, u32[]{:S(2)}) collective-permute-start(bf16[64,768]{1,0:T(8,128)(2,1)} %param.7), channel_id=1, source_target_pairs={{0,128},{128,0},{256,384},{384,256},{1,129},{129,1},{257,385},{385... | collective-permute-start | bytes 294920 | tf_op jit(solution)/shard_map/ppermute | solution.py:35
  35.1 25.7 %all-to-all-start.1 = ((bf16[8,8,48,128]{3,2,1,0:T(8,128)(2,1)}), bf16[8,8,48,128]{3,2,1,0:T(8,128)(2,1)S(1)}, u32[]{:S(2)}, u32[]{:S(2)}) async-start(bf16[8,8,48,128]{3,2,1,0:T(8,128)(2,1)} %broadcast_in_dim.12), calls=%async_computation.1 | async-start | bytes 1572864 | tf_op jit(solution)/shard_map/all_to_all | solution.py:25
  42.9 17.8 %collective-permute-start.3 = (bf16[5,64,768]{2,1,0:T(8,128)(2,1)S(1)}, bf16[5,64,768]{2,1,0:T(8,128)(2,1)S(1)}, u32[]{:S(2)}, u32[]{:S(2)}) collective-permute-start(bf16[5,64,768]{2,1,0:T(8,128)(2,1)S(1)} %pad_maximum_fusion), channel_id=1, source_target_pairs={{0,1},{1,0},{2,3},{3,2},{4,5},{5,4},{6,7},{7,6},{8,9},{9,8},{10,11... | collective-permute-start | bytes 1474568 | tf_op jit(solution)/shard_map/ppermute | solution.py:29
  46.1 12.0 %collective-permute-start.5 = (bf16[4,2,768]{2,1,0:T(2,128)(2,1)S(1)}, bf16[4,2,768]{2,1,0:T(2,128)(2,1)S(1)}, u32[]{:S(2)}, u32[]{:S(2)}) collective-permute-start(bf16[4,2,768]{2,1,0:T(2,128)(2,1)S(1)} %broadcast_select_fusion), channel_id=1, source_target_pairs={{1,3},{3,5},{5,7},{7,9},{9,11},{11,13},{13,15},{15,17},{17,19},{19... | collective-permute-start | bytes 36872 | tf_op jit(solution)/shard_map/ppermute | solution.py:229
  49.4 11.3 %collective-permute-start.4 = (bf16[4,2,768]{2,1,0:T(2,128)(2,1)S(1)}, bf16[4,2,768]{2,1,0:T(2,128)(2,1)S(1)}, u32[]{:S(2)}, u32[]{:S(2)}) collective-permute-start(bf16[4,2,768]{2,1,0:T(2,128)(2,1)S(1)} %broadcast_select_fusion), channel_id=1, source_target_pairs={{1,2},{3,4},{5,6},{7,8},{9,10},{11,12},{13,14},{15,16},{17,18},{19... | collective-permute-start | bytes 36872 | tf_op jit(solution)/shard_map/ppermute | solution.py:229
  60.7 7.7 %copy-start.2 = (bf16[768,128]{1,0:T(8,128)(2,1)S(1)}, bf16[768,128]{1,0:T(8,128)(2,1)}, u32[]{:S(2)}) copy-start(bf16[768,128]{1,0:T(8,128)(2,1)} %param.12) | copy-start | bytes 589828
  64.2 10.6 %all-to-all-start.2 = ((bf16[8,128,192]{1,2,0:T(8,128)(2,1)}), bf16[8,128,192]{1,2,0:T(8,128)(2,1)S(1)}, u32[]{:S(2)}, u32[]{:S(2)}) async-start(bf16[8,128,192]{1,2,0:T(8,128)(2,1)} %copy.12), calls=%async_computation.2 | async-start | bytes 786432 | tf_op jit(solution)/shard_map/all_to_all | solution.py:241
  75.0 0.8 copy-start.4
  75.1 1.0 copy-start.5
  75.5 32.5 %copy-start = (bf16[768,1024]{1,0:T(8,128)(2,1)S(1)}, bf16[768,1024]{1,0:T(8,128)(2,1)}, u32[]{:S(2)}) copy-start(bf16[768,1024]{1,0:T(8,128)(2,1)} %refs_4_.1) | copy-start | bytes 4718596
  77.2 27.8 %all-to-all-start.3 = ((bf16[8,160,128]{2,1,0:T(8,128)(2,1)}), bf16[8,160,128]{2,1,0:T(8,128)(2,1)S(1)}, u32[]{:S(2)}, u32[]{:S(2)}) async-start(bf16[8,160,128]{2,1,0:T(8,128)(2,1)} %broadcast_in_dim.14), calls=%async_computation.3 | async-start | bytes 655360 | tf_op jit(solution)/shard_map/all_to_all | solution.py:25
  80.9 13.2 %collective-permute-start.8 = (bf16[128,768]{1,0:T(8,128)(2,1)S(1)}, bf16[128,768]{1,0:T(8,128)(2,1)S(1)}, u32[]{:S(2)}, u32[]{:S(2)}) collective-permute-start(bf16[128,768]{1,0:T(8,128)(2,1)S(1)} %fusion.15.refs_0_), channel_id=1, source_target_pairs={{0,48},{16,32},{32,16},{48,0},{1,49},{17,33},{33,17},{49,1},{2,50}... | collective-permute-start | bytes 589832 | tf_op jit(solution)/shard_map/ppermute | solution.py:35
  85.5 11.2 %collective-permute-start.7 = (bf16[128,768]{1,0:T(8,128)(2,1)S(1)}, bf16[128,768]{1,0:T(8,128)(2,1)S(1)}, u32[]{:S(2)}, u32[]{:S(2)}) collective-permute-start(bf16[128,768]{1,0:T(8,128)(2,1)S(1)} %fusion.15.refs_0_), channel_id=1, source_target_pairs={{0,32},{16,48},{32,0},{48,16},{1,33},{17,49},{33,1},{49,17},{2,34}... | collective-permute-start | bytes 589832 | tf_op jit(solution)/shard_map/ppermute | solution.py:35
  88.2 9.4 %collective-permute-start.6 = (bf16[128,768]{1,0:T(8,128)(2,1)S(1)}, bf16[128,768]{1,0:T(8,128)(2,1)S(1)}, u32[]{:S(2)}, u32[]{:S(2)}) collective-permute-start(bf16[128,768]{1,0:T(8,128)(2,1)S(1)} %fusion.15.refs_0_), channel_id=1, source_target_pairs={{0,16},{16,0},{32,48},{48,32},{1,17},{17,1},{33,49},{49,33},{2,18}... | collective-permute-start | bytes 589832 | tf_op jit(solution)/shard_map/ppermute | solution.py:35
  105.0 13.0 %collective-permute-start.9 = (bf16[8,160,128]{2,1,0:T(8,128)(2,1)S(1)}, bf16[8,160,128]{2,1,0:T(8,128)(2,1)S(1)}, u32[]{:S(2)}, u32[]{:S(2)}) collective-permute-start(bf16[8,160,128]{2,1,0:T(8,128)(2,1)S(1)} %all-to-all-done.3.refs_5_), channel_id=1, source_target_pairs={{0,64},{64,0},{1,65},{65,1},{2,66},{66,2},{3,67},{67,3},{4,68},{68... | collective-permute-start | bytes 983048 | tf_op jit(solution)/shard_map/ppermute | solution.py:29
  124.3 26.2 %all-to-all-start.4 = ((bf16[8,64,1664]{2,1,0:T(8,128)(2,1)}), bf16[8,64,1664]{2,1,0:T(8,128)(2,1)S(1)}, u32[]{:S(2)}, u32[]{:S(2)}) async-start(bf16[8,64,1664]{2,1,0:T(8,128)(2,1)} %far.1), calls=%async_computation.4 | async-start | bytes 3407872 | tf_op jit(solution)/shard_map/all_to_all | solution.py:295

commit v3 on v2

--- a/solution.py
+++ b/solution.py
@@ -41,9 +41,34 @@
     return values * lax.rsqrt(mean_square + 1e-06) * gain
 
 
+def pack_kernel(w_ref, out_ref):
+    group = lax.axis_index(DP)
+    depth = w_ref.shape[0]
+    whole = w_ref[:, pl.ds(pl.multiple_of(group * 128, 128), 128)].astype(jnp.float32)
+    tile = w_ref[:, pl.ds(pl.multiple_of(512 + (group // 2) * 128, 128), 128)].astype(jnp.float32)
+    turned = pltpu.roll(tile, 64, 1)
+    odd = group % 2 == 1
+    left, right = jnp.where(odd, turned, tile), jnp.where(odd, tile, turned)
+    half = depth // 2
+    lane = lax.broadcasted_iota(jnp.int32, (half, 128), 1)
+    rest = jnp.where(lane < 64, left[:half], right[half:])
+    out = jnp.concatenate([whole, jnp.zeros((2, 128), jnp.float32), rest, jnp.zeros((1, 128), jnp.float32)])
+    out = out.astype(jnp.bfloat16)
+    for i in range(out_ref.shape[0]):
+        out_ref[i] = out
+
+
+def activate_kernel(*refs):
+    x_refs, (gain_ref, out_ref) = refs[:4], refs[4:]
+    for i, ref in enumerate(x_refs):
+        values = normalize(ref[...].astype(jnp.float32), gain_ref[...])
+        out_ref[i] = jax.nn.gelu(values, approximate=True).astype(jnp.bfloat16)
+
+
 def conv_kernel(place_ref, mine_ref, other_ref, end_ref, far_end_ref, w_ref, out_ref, wide_ref):
     group, zp = place_ref[0], place_ref[1]
-    parts, rows, width = mine_ref.shape
+    _, held, width = mine_ref.shape
+    rows = 2 * held
     count, depth = w_ref.shape[0], KW * width // 128
     wide_ref[...] = jnp.zeros_like(wide_ref)
     for side in range(2):
@@ -59,27 +84,64 @@
                 wide_ref[start + depth // 2 : start + depth, 128:] = pltpu.roll(tail, 64, 1)[: depth // 2]
 
     even = zp == 0
-    mine, other = mine_ref[...], other_ref[:parts]
+    mine, other = mine_ref[...], other_ref[...]
     first, second = jnp.where(even, mine, other), jnp.where(even, other, mine)
-    x = jnp.concatenate([first, second], axis=1).reshape(2 * parts * rows, width)
+    x = jnp.concatenate([first, second], axis=1).reshape(4 * rows, width)
     end, far_end = end_ref[...].astype(jnp.float32), far_end_ref[...].astype(jnp.float32)
     before, after = jnp.where(even, end, far_end), jnp.where(even, far_end, end)
-    ends = jnp.concatenate([before.reshape(2 * parts, width), after.reshape(2 * parts, width)]).astype(jnp.bfloat16)
-    sums = [None] * parts
+    ends = jnp.concatenate([before.reshape(8, width), after.reshape(8, width)]).astype(jnp.bfloat16)
+    sums = [None] * 4
     for offset in range(KW):
         w = wide_ref[offset * width : (offset + 1) * width, :].astype(jnp.bfloat16)
         y = jnp.dot(x, w, preferred_element_type=jnp.float32)
         z = jnp.dot(ends, w, preferred_element_type=jnp.float32)
-        for part in range(parts):
-            body = y[2 * part * rows : 2 * (part + 1) * rows]
-            before, after = z[2 * part : 2 * part + 2], z[2 * (parts + part) : 2 * (parts + part) + 2]
-            term = jnp.concatenate([before, body, after])[offset : offset + 2 * rows]
+        for part in range(4):
+            body = y[part * rows : (part + 1) * rows]
+            line = jnp.concatenate([z[2 * part : 2 * part + 2], body, z[8 + 2 * part : 10 + 2 * part]])
+            term = line[offset : offset + rows]
             sums[part] = term if offset == 0 else sums[part] + term
-    for part in range(parts):
+    lane = lax.broadcasted_iota(jnp.int32, (rows // 2, 128), 1)
+    for part in range(4):
         index = jnp.bitwise_xor(group, part)
-        value = sums[part][:, : out_ref.shape[2]].astype(jnp.bfloat16)
+        whole, rest = sums[part][:, :128], sums[part][:, 128:]
+        rest = jnp.where(lane < 64, rest[: rows // 2], pltpu.roll(rest, 64, 1)[rows // 2 :])
+        value = jnp.concatenate([whole, rest]).astype(jnp.bfloat16)
         out_ref[2 * index] = value
         out_ref[2 * index + 1] = value
+
+
+def stream_kernel(place_ref, parts_ref, mine_ref, beside_ref, gain_ref, kw_ref, vw_ref, stream_ref, in_ref, pack_ref):
+    even = place_ref[1] == 0
+    mine, beside = mine_ref[...].astype(jnp.float32), beside_ref[...].astype(jnp.float32)
+    rows = mine.shape[0]
+    lane = lax.broadcasted_iota(jnp.int32, (rows, 128), 1)
+    wholes, rests = [], []
+    for j in range(4):
+        total = parts_ref[2 * j].astype(jnp.float32) + parts_ref[2 * j + 1].astype(jnp.float32)
+        wholes.append(total[: 2 * rows])
+        rests.append((total[2 * rows :], pltpu.roll(total[2 * rows :], 64, 1)))
+    tiles = [
+        jnp.concatenate(
+            [
+                jnp.where(lane < 64, rests[j][0], rests[j + 1][1]),
+                jnp.where(lane < 64, rests[j][1], rests[j + 1][0]),
+            ]
+        )
+        for j in (0, 2)
+    ]
+    conv_out = jnp.concatenate(wholes + tiles, axis=1)
+    inputs = jnp.concatenate([jnp.where(even, mine, beside), jnp.where(even, beside, mine)])
+    stream = (inputs + conv_out).astype(jnp.bfloat16)
+    stream_ref[...] = jnp.where(even, stream[:rows], stream[rows:])
+    attn_in = normalize(stream.astype(jnp.float32), gain_ref[...]).astype(jnp.bfloat16)
+    in_ref[...] = attn_in
+    own = jnp.where(even, attn_in[:rows], attn_in[rows:])
+    keys = jnp.dot(own, kw_ref[...], preferred_element_type=jnp.float32)
+    values = jnp.dot(own, vw_ref[...], preferred_element_type=jnp.float32)
+    tail = jnp.concatenate([values[: rows // 2, 128:], values[rows // 2 :, 128:]], axis=1)
+    packed = jnp.concatenate([keys, values[:, :128], tail]).astype(jnp.bfloat16)
+    for i in range(pack_ref.shape[0]):
+        pack_ref[i] = packed
 
 
 def unpack(ref, k_ref, ve_ref, vo_ref):
@@ -206,57 +268,66 @@
     value_size = value_weight.shape[1]
     heads = query_weight.shape[1] // size
     zp = lax.axis_index("zp")
-    group = lax.axis_index(DP)
-    columns = width // 4
-
-    half = conv_weight.shape[0] // 2
-    whole = lax.dynamic_slice_in_dim(conv_weight, group * 128, 128, axis=1)
-    rest = lax.dynamic_slice_in_dim(conv_weight, 512 + group * 64, 64, axis=1)
-    rest = jnp.concatenate([rest[:half], rest[half:]], axis=1)
-    blocks = everyone(jnp.concatenate([jnp.pad(whole, ((0, 2), (0, 0))), jnp.pad(rest, ((0, 1), (0, 0)))]), "zt", 8)
+    place = jnp.stack([lax.axis_index(DP), zp])
+    in_smem = pl.BlockSpec(memory_space=pltpu.SMEM)
+    in_vmem = pl.BlockSpec(memory_space=pltpu.VMEM)
+    params = pltpu.CompilerParams(vmem_limit_bytes=32 * 1024 * 1024)
+
+    mine = pl.pallas_call(
+        pack_kernel,
+        out_shape=jax.ShapeDtypeStruct((8, 48, 128), jnp.bfloat16),
+        in_specs=[in_vmem],
+        out_specs=in_vmem,
+        compiler_params=params,
+        name="pack",
+    )(conv_weight)
+    blocks = lax.all_to_all(mine, "zt", 0, 0, tiled=True)
+
     shared = by_masks(features, DP)
-    blocks, *shared = lax.optimization_barrier((blocks, *shared))
-
-    shared = jnp.stack(shared).astype(jnp.float32)
-    activated = jax.nn.gelu(normalize(shared, conv_gain), approximate=True).astype(jnp.bfloat16)
+    beside = swapped(features, "zp")
+    blocks, beside, *shared = lax.optimization_barrier((blocks, beside, *shared))
+
     blocks = everyone(blocks, WEIGHT, 8).reshape(64, 48, 128)
+    activated = pl.pallas_call(
+        activate_kernel,
+        out_shape=jax.ShapeDtypeStruct((4, rows, width), jnp.bfloat16),
+        in_specs=[in_vmem] * 5,
+        out_specs=in_vmem,
+        compiler_params=params,
+        name="activate",
+    )(*shared, conv_gain[None])
     edge = jnp.where(zp == 0, activated[:, :2], activated[:, rows - 2 :])
     odd, even = range(1, 128, 2), range(0, 128, 2)
     steps = [
         [(i, i + step) for i in odd if i + step < 128] + [(i, i - step) for i in even if i - step >= 0]
         for step in (1, 2)
     ]
+    other = swapped(activated, "zp")
     end, far_end = (lax.ppermute(edge, SEQ, step) for step in steps)
-    other = swapped(jnp.concatenate([activated, features[None]]), "zp")
-    beside = other[4]
     partial = pl.pallas_call(
         conv_kernel,
-        out_shape=jax.ShapeDtypeStruct((8, 2 * rows, columns), jnp.bfloat16),
-        in_specs=[pl.BlockSpec(memory_space=pltpu.SMEM)] + [pl.BlockSpec(memory_space=pltpu.VMEM)] * 5,
-        out_specs=pl.BlockSpec(memory_space=pltpu.VMEM),
+        out_shape=jax.ShapeDtypeStruct((8, 3 * rows, 128), jnp.bfloat16),
+        in_specs=[in_smem] + [in_vmem] * 5,
+        out_specs=in_vmem,
         scratch_shapes=[pltpu.VMEM((KW * width, 256), jnp.float32)],
-        compiler_params=pltpu.CompilerParams(vmem_limit_bytes=32 * 1024 * 1024),
+        compiler_params=params,
         name="conv",
-    )(jnp.stack([group, zp]), activated, other, end, far_end, blocks)
-    partial = lax.all_to_all(partial, SHARE, 0, 0, tiled=True).astype(jnp.float32)
-    partial = partial.reshape(4, 2, 2 * rows, columns).sum(axis=1)
-    conv_out = jnp.concatenate(
-        [partial[i][:, :128] for i in range(4)] + [partial[i][:, 128:] for i in range(4)], axis=1
-    )
-    mine_first = jnp.concatenate([features, beside])
-    other_first = jnp.concatenate([beside, features])
-    inputs = jnp.where(zp == 0, mine_first, other_first).astype(jnp.float32)
-
-    wide_stream = (inputs + conv_out).astype(jnp.bfloat16)
-    stream = jnp.where(zp == 0, wide_stream[:rows], wide_stream[rows:])
-    wide_in = normalize(wide_stream.astype(jnp.float32), attn_gain).astype(jnp.bfloat16)
-    attn_in = jnp.where(zp == 0, wide_in[:rows], wide_in[rows:])
-    both = jnp.concatenate([key_weight, value_weight], axis=1)
-    pairs = jnp.dot(attn_in, both, preferred_element_type=jnp.float32).astype(jnp.bfloat16)
-    tail = pairs[:, 256:]
-    tail = jnp.concatenate([tail[: rows // 2], tail[rows // 2 :]], axis=1)
-    packed = jnp.concatenate([pairs[:, :128], pairs[:, 128:256], tail])
-    near = everyone(packed, "zt", 8)
+    )(place, activated, other, end, far_end, blocks)
+    partial = lax.all_to_all(partial, SHARE, 0, 0, tiled=True)
+
+    stream, wide_in, packed = pl.pallas_call(
+        stream_kernel,
+        out_shape=[
+            jax.ShapeDtypeStruct((rows, width), jnp.bfloat16),
+            jax.ShapeDtypeStruct((2 * rows, width), jnp.bfloat16),
+            jax.ShapeDtypeStruct((8, 5 * rows // 2, 128), jnp.bfloat16),
+        ],
+        in_specs=[in_smem] + [in_vmem] * 6,
+        out_specs=[in_vmem] * 3,
+        compiler_params=params,
+        name="stream",
+    )(place, partial, features, beside, attn_gain[None], key_weight, value_weight)
+    near = lax.all_to_all(packed, "zt", 0, 0, tiled=True)
     asked = by_masks(wide_in, COLUMN)
     near, *asked = lax.optimization_barrier((near, *asked))
     far = swapped(near, "xh")
@@ -265,9 +336,7 @@
         pltpu.VMEM((8 * rows, 256), jnp.bfloat16),
         pltpu.VMEM((8 * rows, 256), jnp.bfloat16),
     ]
-    in_vmem = pl.BlockSpec(memory_space=pltpu.VMEM)
     cost = pl.CostEstimate(flops=4_500_000_000, bytes_accessed=8_000_000, transcendentals=2_200_000)
-    params = pltpu.CompilerParams(vmem_limit_bytes=32 * 1024 * 1024)
     queries, weighted, tops = pl.pallas_call(
         functools.partial(near_kernel, heads, size),
         out_shape=[
@@ -285,7 +354,7 @@
     out = pl.pallas_call(
         functools.partial(far_kernel, heads, size),
         out_shape=jax.ShapeDtypeStruct((8, rows, heads * value_size + STATS), jnp.bfloat16),
-        in_specs=[pl.BlockSpec(memory_space=pltpu.SMEM)] + [in_vmem] * 4,
+        in_specs=[in_smem] + [in_vmem] * 4,
         out_specs=in_vmem,
         scratch_shapes=scratch,
         compiler_params=params,

time: 154 us -> 152 us (0.987)
  blocking collectives: 0 us -> 24.9 us
  waiting for transfers between devices: 58.2 us -> 37.7 us
  other arithmetic: 2.77 us -> 0.1 us
  local copies, waits for them, and re-layouts: 5.93 us -> 3.42 us
  Pallas kernels: 14.2 us -> 16.7 us
  starting transfers between devices: 69.9 us -> 67.5 us
    all_to_all x0 -> x1, blocking collectives: none -> 24.9 us  [local(): parts = lax.all_to_all(out, SPREAD, 0, 0, tiled=True)]
    all_to_all x3 -> x1, starting transfers between devices: 26.2 us -> 7.43 us  [everyone(): return lax.all_to_all(sent, axes, 0, 0, tiled=True)]
    all_to_all x2 -> x3, starting transfers between devices: 8.42 us -> 22.7 us  [the longest x1 15.1 us: local(): blocks = lax.all_to_all(mine, 'zt', 0, 0, tiled=True)]
    all_to_all x2 -> x3, waiting for transfers between devices: 27.6 us -> 14.1 us  [the longest x1 7.38 us: local(): near = lax.all_to_all(packed, 'zt', 0, 0, tiled=True)]
    all_to_all x3 -> x1, waiting for transfers between devices: 12.6 us -> 0.01 us  [everyone(): return lax.all_to_all(sent, axes, 0, 0, tiled=True)]
    ppermute x2, waiting for transfers between devices: 2.7 us -> 6.87 us  [local(): end, far_end = (lax.ppermute(edge, SEQ, step) for step in steps)]
    pallas_call x1 -> x4, Pallas kernels: 2.5 us -> 6.18 us  [the longest x1 3.31 us: local(): pl.pallas_call(conv_kernel, out_shape=jax.ShapeDtypeStruct((8, 3 * rows,...]
    ppermute x2 -> x3, waiting for transfers between devices: 6.33 us -> 9.69 us  [swapped(): return lax.ppermute(block, axis, [(0, 1), (1, 0)])]
  transfers between devices with their start and end apart: 15 -> 15, of which waited for: 10 -> 8; matrix products, arithmetic and copies ran while one was open for 1% -> 0% of each run, Pallas kernels for 2% -> 3%
where the time goes in v3:
time: 152 us; the launch traced here: 151 us
  starting transfers between devices  67.5 us (44%)
  waiting for transfers between devices  37.7 us (25%)
  blocking collectives  24.9 us (16%)
  Pallas kernels  16.7 us (11%)
  local copies, waits for them, and re-layouts  3.42 us (2%)
    all_to_all x1, blocking collectives, local(): parts = lax.all_to_all(out, SPREAD, 0, 0, tiled=True)  24.9 us
    ppermute x6, starting transfers between devices, by_masks(): lax.ppermute(block, axes, [(i, i ^ mask) for i in range(count)])  17.4 us
    all_to_all x1, starting transfers between devices, local(): blocks = lax.all_to_all(mine, 'zt', 0, 0, tiled=True)  15.1 us
    ppermute x2, starting transfers between devices, local(): end, far_end = (lax.ppermute(edge, SEQ, step) for step in steps)  11.8 us
    ppermute x3, waiting for transfers between devices, swapped(): return lax.ppermute(block, axis, [(0, 1), (1, 0)])  9.69 us
    ppermute x3, starting transfers between devices, swapped(): return lax.ppermute(block, axis, [(0, 1), (1, 0)])  8.19 us
    all_to_all x1, starting transfers between devices, everyone(): return lax.all_to_all(sent, axes, 0, 0, tiled=True)  7.43 us
    all_to_all x1, waiting for transfers between devices, local(): near = lax.all_to_all(packed, 'zt', 0, 0, tiled=True)  7.38 us
  transfers between devices with their start and end apart: 15, of which 8 were waited for; matrix products, arithmetic and copies ran while one was open for 0% of the time, Pallas kernels for 3%

profile of v3, /device:TPU:6, one launch (start us, length us, event | category | flops | bytes accessed | tf_op | source)
XLA Modules:
  0.0 151.2 jit_solution(11301681619188799397)
XLA Ops:
  0.7 0.8 copy-done.2
  1.5 0.7 pack.1
  2.2 15.1 %all-to-all-start = ((bf16[8,48,128]{2,1,0:T(8,128)(2,1)}), bf16[8,48,128]{2,1,0:T(8,128)(2,1)S(1)}, u32[]{:S(2)}, u32[]{:S(2)}) async-start(bf16[8,48,128]{2,1,0:T(8,128)(2,1)} %pack.1), calls=%async_computation | async-start | bytes 196608 | tf_op jit(solution)/shard_map/all_to_all | solution.py:284
  17.3 1.9 %collective-permute-start.3 = (bf16[64,768]{1,0:T(8,128)(2,1)}, bf16[64,768]{1,0:T(8,128)(2,1)S(1)}, u32[]{:S(2)}, u32[]{:S(2)}) collective-permute-start(bf16[64,768]{1,0:T(8,128)(2,1)} %mine_ref.1), channel_id=1, source_target_pairs={{0,384},{128,256},{256,128},{384,0},{1,385},{129,257},{257,129},{3... | collective-permute-start | bytes 294920 | tf_op jit(solution)/shard_map/ppermute | solution.py:35
  19.2 3.1 %collective-permute-start.2 = (bf16[64,768]{1,0:T(8,128)(2,1)}, bf16[64,768]{1,0:T(8,128)(2,1)S(1)}, u32[]{:S(2)}, u32[]{:S(2)}) collective-permute-start(bf16[64,768]{1,0:T(8,128)(2,1)} %mine_ref.1), channel_id=1, source_target_pairs={{0,256},{128,384},{256,0},{384,128},{1,257},{129,385},{257,1},{385... | collective-permute-start | bytes 294920 | tf_op jit(solution)/shard_map/ppermute | solution.py:35
  22.3 2.6 %collective-permute-start.1 = (bf16[64,768]{1,0:T(8,128)(2,1)}, bf16[64,768]{1,0:T(8,128)(2,1)S(1)}, u32[]{:S(2)}, u32[]{:S(2)}) collective-permute-start(bf16[64,768]{1,0:T(8,128)(2,1)} %mine_ref.1), channel_id=1, source_target_pairs={{0,128},{128,0},{256,384},{384,256},{1,129},{129,1},{257,385},{385... | collective-permute-start | bytes 294920 | tf_op jit(solution)/shard_map/ppermute | solution.py:35
  24.9 2.9 %collective-permute-start = (bf16[64,768]{1,0:T(8,128)(2,1)}, bf16[64,768]{1,0:T(8,128)(2,1)S(1)}, u32[]{:S(2)}, u32[]{:S(2)}) collective-permute-start(bf16[64,768]{1,0:T(8,128)(2,1)} %mine_ref.1), channel_id=1, source_target_pairs={{0,1},{1,0},{2,3},{3,2},{4,5},{5,4},{6,7},{7,6},{8,9},{9,8},{10,11... | collective-permute-start | bytes 294920 | tf_op jit(solution)/shard_map/ppermute | solution.py:29
  27.9 3.9 %collective-permute-done.beside_ref = bf16[64,768]{1,0:T(8,128)(2,1)S(1)} collective-permute-done((bf16[64,768]{1,0:T(8,128)(2,1)}, bf16[64,768]{1,0:T(8,128)(2,1)S(1)}, u32[]{:S(2)}, u32[]{:S(2)}) %collective-permute-start) | collective-permute-done | bytes 98336 | tf_op jit(solution)/shard_map/ppermute | solution.py:29
  32.2 1.0 broadcast_in_dim.16
  33.2 7.4 %all-to-all-start.1 = ((bf16[8,8,48,128]{3,2,1,0:T(8,128)(2,1)}), bf16[8,8,48,128]{3,2,1,0:T(8,128)(2,1)S(1)}, u32[]{:S(2)}, u32[]{:S(2)}) async-start(bf16[8,8,48,128]{3,2,1,0:T(8,128)(2,1)} %broadcast_in_dim.16), calls=%async_computation.1 | async-start | bytes 1572864 | tf_op jit(solution)/shard_map/all_to_all | solution.py:25
  41.1 3.2 %collective-permute-start.4 = (bf16[4,64,768]{2,1,0:T(8,128)(2,1)S(1)}, bf16[4,64,768]{2,1,0:T(8,128)(2,1)S(1)}, u32[]{:S(2)}, u32[]{:S(2)}) collective-permute-start(bf16[4,64,768]{2,1,0:T(8,128)(2,1)S(1)} %activate.1.mine_ref), channel_id=1, source_target_pairs={{0,1},{1,0},{2,3},{3,2},{4,5},{5,4},{6,7},{7,6},{8,9},{9,8},{10,11... | collective-permute-start | bytes 1179656 | tf_op jit(solution)/shard_map/ppermute | solution.py:29
  44.3 7.4 %collective-permute-start.6 = (bf16[4,2,768]{2,1,0:T(2,128)(2,1)S(1)}, bf16[4,2,768]{2,1,0:T(2,128)(2,1)S(1)}, u32[]{:S(2)}, u32[]{:S(2)}) collective-permute-start(bf16[4,2,768]{2,1,0:T(2,128)(2,1)S(1)} %broadcast_select_fusion), channel_id=1, source_target_pairs={{1,3},{3,5},{5,7},{7,9},{9,11},{11,13},{13,15},{15,17},{17,19},{19... | collective-permute-start | bytes 36872 | tf_op jit(solution)/shard_map/ppermute | solution.py:306
  51.7 4.4 %collective-permute-start.5 = (bf16[4,2,768]{2,1,0:T(2,128)(2,1)S(1)}, bf16[4,2,768]{2,1,0:T(2,128)(2,1)S(1)}, u32[]{:S(2)}, u32[]{:S(2)}) collective-permute-start(bf16[4,2,768]{2,1,0:T(2,128)(2,1)S(1)} %broadcast_select_fusion), channel_id=1, source_target_pairs={{1,2},{3,4},{5,6},{7,8},{9,10},{11,12},{13,14},{15,16},{17,18},{19... | collective-permute-start | bytes 36872 | tf_op jit(solution)/shard_map/ppermute | solution.py:306
  56.2 6.9 %collective-permute-done.5.end_ref = bf16[4,2,768]{2,1,0:T(2,128)(2,1)S(1)} collective-permute-done((bf16[4,2,768]{2,1,0:T(2,128)(2,1)S(1)}, bf16[4,2,768]{2,1,0:T(2,128)(2,1)S(1)}, u32[]{:S(2)}, u32[]{:S(2)}) %collective-permute-start.5) | collective-permute-done | bytes 12320 | tf_op jit(solution)/shard_map/ppermute | solution.py:306
  63.1 3.3 %conv.1 = bf16[8,192,128]{2,1,0:T(8,128)(2,1)} custom-call(s32[2]{0:T(128)S(1)} %pad_add_fusion.place_ref, bf16[4,64,768]{2,1,0:T(8,128)(2,1)S(1)} %activate.1.mine_ref, bf16[4,64,768]{2,1,0:T(8,128)(2,1)S(1)} %collective-permute-done.4.other_ref, bf16[4,2,768]{2,1,0:T(2,128)(2,1)S(1)} %collective-permute-done.5.end_ref, ...), custom_call_target="tpu_custom_call" | custom-call | tf_op jit(solution)/shard_map/conv/pallas_call | solution.py:307
  66.4 4.2 %all-to-all-start.2 = ((bf16[8,192,128]{2,1,0:T(8,128)(2,1)}), bf16[8,192,128]{2,1,0:T(8,128)(2,1)S(1)}, u32[]{:S(2)}, u32[]{:S(2)}) async-start(bf16[8,192,128]{2,1,0:T(8,128)(2,1)} %conv.1), calls=%async_computation.2 | async-start | bytes 786432 | tf_op jit(solution)/shard_map/all_to_all | solution.py:316
  70.8 6.2 %all-to-all-done.2.parts_ref = bf16[8,192,128]{2,1,0:T(8,128)(2,1)S(1)} async-done(((bf16[8,192,128]{2,1,0:T(8,128)(2,1)}), bf16[8,192,128]{2,1,0:T(8,128)(2,1)S(1)}, u32[]{:S(2)}, u32[]{:S(2)}) %all-to-all-start.2) | async-done | bytes 393248 | tf_op jit(solution)/shard_map/all_to_all | solution.py:316
  76.9 1.7 %stream.1 = (bf16[64,768]{1,0:T(8,128)(2,1)}, bf16[128,768]{1,0:T(8,128)(2,1)S(1)}, bf16[8,160,128]{2,1,0:T(8,128)(2,1)}) custom-call(s32[2]{0:T(128)S(1)} %pad_add_fusion.place_ref, bf16[8,192,128]{2,1,0:T(8,128)(2,1)S(1)} %all-to-all-done.2.parts_ref, bf16[64,768]{1,0:T(8,128)(2,1)S(1)} %copy-done, bf16[64,768]{1,0:T(8,128)(2,1)S(1)} %collective-permute-done.beside_ref, ...), custom_call_target="tpu_custom_call" | custom-call | tf_op jit(solution)/shard_map/stream/pallas_call | solution.py:318
  78.7 3.4 %all-to-all-start.3 = ((bf16[8,160,128]{2,1,0:T(8,128)(2,1)}), bf16[8,160,128]{2,1,0:T(8,128)(2,1)S(1)}, u32[]{:S(2)}, u32[]{:S(2)}) async-start(bf16[8,160,128]{2,1,0:T(8,128)(2,1)} %get-tuple-element.26), calls=%async_computation.3 | async-start | bytes 655360 | tf_op jit(solution)/shard_map/all_to_all | solution.py:330
  82.1 3.0 %collective-permute-start.9 = (bf16[128,768]{1,0:T(8,128)(2,1)S(1)}, bf16[128,768]{1,0:T(8,128)(2,1)S(1)}, u32[]{:S(2)}, u32[]{:S(2)}) collective-permute-start(bf16[128,768]{1,0:T(8,128)(2,1)S(1)} %get-tuple-element.28.refs_0_), channel_id=1, source_target_pairs={{0,48},{16,32},{32,16},{48,0},{1,49},{17,33},{33,17},{49,1},{2,50}... | collective-permute-start | bytes 589832 | tf_op jit(solution)/shard_map/ppermute | solution.py:35
  85.1 2.8 %collective-permute-start.8 = (bf16[128,768]{1,0:T(8,128)(2,1)S(1)}, bf16[128,768]{1,0:T(8,128)(2,1)S(1)}, u32[]{:S(2)}, u32[]{:S(2)}) collective-permute-start(bf16[128,768]{1,0:T(8,128)(2,1)S(1)} %get-tuple-element.28.refs_0_), channel_id=1, source_target_pairs={{0,32},{16,48},{32,0},{48,16},{1,33},{17,49},{33,1},{49,17},{2,34}... | collective-permute-start | bytes 589832 | tf_op jit(solution)/shard_map/ppermute | solution.py:35
  87.9 4.1 %collective-permute-start.7 = (bf16[128,768]{1,0:T(8,128)(2,1)S(1)}, bf16[128,768]{1,0:T(8,128)(2,1)S(1)}, u32[]{:S(2)}, u32[]{:S(2)}) collective-permute-start(bf16[128,768]{1,0:T(8,128)(2,1)S(1)} %get-tuple-element.28.refs_0_), channel_id=1, source_target_pairs={{0,16},{16,0},{32,48},{48,32},{1,17},{17,1},{33,49},{49,33},{2,18}... | collective-permute-start | bytes 589832 | tf_op jit(solution)/shard_map/ppermute | solution.py:35
  92.0 4.6 %collective-permute-done.9.refs_3_ = bf16[128,768]{1,0:T(8,128)(2,1)S(1)} collective-permute-done((bf16[128,768]{1,0:T(8,128)(2,1)S(1)}, bf16[128,768]{1,0:T(8,128)(2,1)S(1)}, u32[]{:S(2)}, u32[]{:S(2)}) %collective-permute-start.9) | collective-permute-done | bytes 196640 | tf_op jit(solution)/shard_map/ppermute | solution.py:35
  96.6 2.5 %collective-permute-done.7.refs_1_ = bf16[128,768]{1,0:T(8,128)(2,1)S(1)} collective-permute-done((bf16[128,768]{1,0:T(8,128)(2,1)S(1)}, bf16[128,768]{1,0:T(8,128)(2,1)S(1)}, u32[]{:S(2)}, u32[]{:S(2)}) %collective-permute-start.7) | collective-permute-done | bytes 196640 | tf_op jit(solution)/shard_map/ppermute | solution.py:35
  99.1 7.4 %all-to-all-done.3.refs_5_ = bf16[8,160,128]{2,1,0:T(8,128)(2,1)S(1)} async-done(((bf16[8,160,128]{2,1,0:T(8,128)(2,1)}), bf16[8,160,128]{2,1,0:T(8,128)(2,1)S(1)}, u32[]{:S(2)}, u32[]{:S(2)}) %all-to-all-start.3) | async-done | bytes 327712 | tf_op jit(solution)/shard_map/all_to_all | solution.py:330
  106.5 2.1 %collective-permute-start.10 = (bf16[8,160,128]{2,1,0:T(8,128)(2,1)S(1)}, bf16[8,160,128]{2,1,0:T(8,128)(2,1)S(1)}, u32[]{:S(2)}, u32[]{:S(2)}) collective-permute-start(bf16[8,160,128]{2,1,0:T(8,128)(2,1)S(1)} %all-to-all-done.3.refs_5_), channel_id=1, source_target_pairs={{0,64},{64,0},{1,65},{65,1},{2,66},{66,2},{3,67},{67,3},{4,68},{68... | collective-permute-start | bytes 983048 | tf_op jit(solution)/shard_map/ppermute | solution.py:29
  108.6 1.4 copy-done.3
  110.0 3.7 %near.1 = (bf16[512,1024]{1,0:T(8,128)(2,1)S(1)}, f32[8,512,256]{2,1,0:T(8,128)S(1)}, f32[512,128]{1,0:T(8,128)S(1)}) custom-call(bf16[128,768]{1,0:T(8,128)(2,1)S(1)} %get-tuple-element.28.refs_0_, bf16[128,768]{1,0:T(8,128)(2,1)S(1)} %collective-permute-done.7.refs_1_, bf16[128,768]{1,0:T(8,128)(2,1)S(1)} %collective-permute-done.8.refs_2_, ...), custom_call_target="tpu_custom_call" | custom-call | flops 4499999744 | bytes 8000000 | tf_op jit(solution)/shard_map/near/pallas_call | solution.py:340
  113.6 5.8 %collective-permute-done.10.pack_ref = bf16[8,160,128]{2,1,0:T(8,128)(2,1)S(1)} collective-permute-done((bf16[8,160,128]{2,1,0:T(8,128)(2,1)S(1)}, bf16[8,160,128]{2,1,0:T(8,128)(2,1)S(1)}, u32[]{:S(2)}, u32[]{:S(2)}) %collective-permute-start.10) | collective-permute-done | bytes 327712 | tf_op jit(solution)/shard_map/ppermute | solution.py:29
  119.5 5.1 %far.1 = bf16[8,64,1664]{2,1,0:T(8,128)(2,1)S(1)} custom-call(s32[1]{0:T(128)} %bitcast.3.place_ref, bf16[512,1024]{1,0:T(8,128)(2,1)S(1)} %get-tuple-element.33.q_ref, f32[8,512,256]{2,1,0:T(8,128)S(1)} %get-tuple-element.34.o_ref, f32[512,128]{1,0:T(8,128)S(1)} %get-tuple-element.35.top_ref, bf16[8,160,128]{2,1,0:T(8,128)(2,1)S(1)} %collective-permute-done.10.pack_ref), custom_call_target="tpu_custom_call" | custom-call | flops 4499999744 | bytes 8000000 | tf_op jit(solution)/shard_map/far/pallas_call | solution.py:354
  124.6 24.9 %all_to_all.25.parts_ref = bf16[8,64,1664]{2,1,0:T(8,128)(2,1)S(1)} all-to-all(bf16[8,64,1664]{2,1,0:T(8,128)(2,1)S(1)} %far.1), channel_id=1, replica_groups=mesh['xl'=2,'co'=2,'xh'=2,'y1'=2,'y0'=2,'zt'=8,'zp'=2] {'y1','y0','zp'}, dimensions={0} | all-to-all | bytes 3407872 | tf_op jit(solution)/shard_map/all_to_all | solution.py:364
  149.5 1.8 %combine.1 = bf16[64,1536]{1,0:T(8,128)(2,1)} custom-call(bf16[8,64,1664]{2,1,0:T(8,128)(2,1)S(1)} %all_to_all.25.parts_ref), custom_call_target="tpu_custom_call" | custom-call | tf_op jit(solution)/shard_map/combine/pallas_call | solution.py:365
  (26 shorter events, 1.2 us)
Async XLA Ops:
  0.6 40.0 %copy-start = (bf16[64,768]{1,0:T(8,128)(2,1)S(1)}, bf16[64,768]{1,0:T(8,128)(2,1)}, u32[]{:S(2)}) copy-start(bf16[64,768]{1,0:T(8,128)(2,1)} %mine_ref.1) | copy-start | bytes 294916
  0.6 0.8 copy-start.2
  1.5 39.2 %copy-start.5 = (f32[768]{0:T(1024)S(1)}, f32[768]{0:T(1024)}, u32[]{:S(2)}) copy-start(f32[768]{0:T(1024)} %param.8) | copy-start | bytes 9220
  2.2 30.0 %all-to-all-start = ((bf16[8,48,128]{2,1,0:T(8,128)(2,1)}), bf16[8,48,128]{2,1,0:T(8,128)(2,1)S(1)}, u32[]{:S(2)}, u32[]{:S(2)}) async-start(bf16[8,48,128]{2,1,0:T(8,128)(2,1)} %pack.1), calls=%async_computation | async-start | bytes 196608 | tf_op jit(solution)/shard_map/all_to_all | solution.py:284
  17.3 10.5 %collective-permute-start.3 = (bf16[64,768]{1,0:T(8,128)(2,1)}, bf16[64,768]{1,0:T(8,128)(2,1)S(1)}, u32[]{:S(2)}, u32[]{:S(2)}) collective-permute-start(bf16[64,768]{1,0:T(8,128)(2,1)} %mine_ref.1), channel_id=1, source_target_pairs={{0,384},{128,256},{256,128},{384,0},{1,385},{129,257},{257,129},{3... | collective-permute-start | bytes 294920 | tf_op jit(solution)/shard_map/ppermute | solution.py:35
  19.2 8.6 %collective-permute-start.2 = (bf16[64,768]{1,0:T(8,128)(2,1)}, bf16[64,768]{1,0:T(8,128)(2,1)S(1)}, u32[]{:S(2)}, u32[]{:S(2)}) collective-permute-start(bf16[64,768]{1,0:T(8,128)(2,1)} %mine_ref.1), channel_id=1, source_target_pairs={{0,256},{128,384},{256,0},{384,128},{1,257},{129,385},{257,1},{385... | collective-permute-start | bytes 294920 | tf_op jit(solution)/shard_map/ppermute | solution.py:35
  22.3 5.6 %collective-permute-start.1 = (bf16[64,768]{1,0:T(8,128)(2,1)}, bf16[64,768]{1,0:T(8,128)(2,1)S(1)}, u32[]{:S(2)}, u32[]{:S(2)}) collective-permute-start(bf16[64,768]{1,0:T(8,128)(2,1)} %mine_ref.1), channel_id=1, source_target_pairs={{0,128},{128,0},{256,384},{384,256},{1,129},{129,1},{257,385},{385... | collective-permute-start | bytes 294920 | tf_op jit(solution)/shard_map/ppermute | solution.py:35
  24.9 6.8 %collective-permute-start = (bf16[64,768]{1,0:T(8,128)(2,1)}, bf16[64,768]{1,0:T(8,128)(2,1)S(1)}, u32[]{:S(2)}, u32[]{:S(2)}) collective-permute-start(bf16[64,768]{1,0:T(8,128)(2,1)} %mine_ref.1), channel_id=1, source_target_pairs={{0,1},{1,0},{2,3},{3,2},{4,5},{5,4},{6,7},{7,6},{8,9},{9,8},{10,11... | collective-permute-start | bytes 294920 | tf_op jit(solution)/shard_map/ppermute | solution.py:29
  33.2 29.8 %all-to-all-start.1 = ((bf16[8,8,48,128]{3,2,1,0:T(8,128)(2,1)}), bf16[8,8,48,128]{3,2,1,0:T(8,128)(2,1)S(1)}, u32[]{:S(2)}, u32[]{:S(2)}) async-start(bf16[8,8,48,128]{3,2,1,0:T(8,128)(2,1)} %broadcast_in_dim.16), calls=%async_computation.1 | async-start | bytes 1572864 | tf_op jit(solution)/shard_map/all_to_all | solution.py:25
  40.7 29.9 %copy-start.6 = (f32[768]{0:T(1024)S(1)}, f32[768]{0:T(1024)}, u32[]{:S(2)}) copy-start(f32[768]{0:T(1024)} %param.10) | copy-start | bytes 9220
  40.7 29.9 %copy-start.4 = (bf16[768,192]{0,1:T(8,128)(2,1)S(1)}, bf16[768,192]{0,1:T(8,128)(2,1)}, u32[]{:S(2)}) copy-start(bf16[768,192]{0,1:T(8,128)(2,1)} %param.13) | copy-start | bytes 884740
  41.1 22.0 %collective-permute-start.4 = (bf16[4,64,768]{2,1,0:T(8,128)(2,1)S(1)}, bf16[4,64,768]{2,1,0:T(8,128)(2,1)S(1)}, u32[]{:S(2)}, u32[]{:S(2)}) collective-permute-start(bf16[4,64,768]{2,1,0:T(8,128)(2,1)S(1)} %activate.1.mine_ref), channel_id=1, source_target_pairs={{0,1},{1,0},{2,3},{3,2},{4,5},{5,4},{6,7},{7,6},{8,9},{9,8},{10,11... | collective-permute-start | bytes 1179656 | tf_op jit(solution)/shard_map/ppermute | solution.py:29
  44.3 11.9 %collective-permute-start.6 = (bf16[4,2,768]{2,1,0:T(2,128)(2,1)S(1)}, bf16[4,2,768]{2,1,0:T(2,128)(2,1)S(1)}, u32[]{:S(2)}, u32[]{:S(2)}) collective-permute-start(bf16[4,2,768]{2,1,0:T(2,128)(2,1)S(1)} %broadcast_select_fusion), channel_id=1, source_target_pairs={{1,3},{3,5},{5,7},{7,9},{9,11},{11,13},{13,15},{15,17},{17,19},{19... | collective-permute-start | bytes 36872 | tf_op jit(solution)/shard_map/ppermute | solution.py:306
  51.7 11.3 %collective-permute-start.5 = (bf16[4,2,768]{2,1,0:T(2,128)(2,1)S(1)}, bf16[4,2,768]{2,1,0:T(2,128)(2,1)S(1)}, u32[]{:S(2)}, u32[]{:S(2)}) collective-permute-start(bf16[4,2,768]{2,1,0:T(2,128)(2,1)S(1)} %broadcast_select_fusion), channel_id=1, source_target_pairs={{1,2},{3,4},{5,6},{7,8},{9,10},{11,12},{13,14},{15,16},{17,18},{19... | collective-permute-start | bytes 36872 | tf_op jit(solution)/shard_map/ppermute | solution.py:306
  63.1 13.9 %copy-start.1 = (bf16[768,128]{1,0:T(8,128)(2,1)S(1)}, bf16[768,128]{1,0:T(8,128)(2,1)}, u32[]{:S(2)}) copy-start(bf16[768,128]{1,0:T(8,128)(2,1)} %kw_ref.1) | copy-start | bytes 589828
  66.4 10.6 %all-to-all-start.2 = ((bf16[8,192,128]{2,1,0:T(8,128)(2,1)}), bf16[8,192,128]{2,1,0:T(8,128)(2,1)S(1)}, u32[]{:S(2)}, u32[]{:S(2)}) async-start(bf16[8,192,128]{2,1,0:T(8,128)(2,1)} %conv.1), calls=%async_computation.2 | async-start | bytes 786432 | tf_op jit(solution)/shard_map/all_to_all | solution.py:316
  78.7 27.8 %all-to-all-start.3 = ((bf16[8,160,128]{2,1,0:T(8,128)(2,1)}), bf16[8,160,128]{2,1,0:T(8,128)(2,1)S(1)}, u32[]{:S(2)}, u32[]{:S(2)}) async-start(bf16[8,160,128]{2,1,0:T(8,128)(2,1)} %get-tuple-element.26), calls=%async_computation.3 | async-start | bytes 655360 | tf_op jit(solution)/shard_map/all_to_all | solution.py:330
  82.1 14.4 %collective-permute-start.9 = (bf16[128,768]{1,0:T(8,128)(2,1)S(1)}, bf16[128,768]{1,0:T(8,128)(2,1)S(1)}, u32[]{:S(2)}, u32[]{:S(2)}) collective-permute-start(bf16[128,768]{1,0:T(8,128)(2,1)S(1)} %get-tuple-element.28.refs_0_), channel_id=1, source_target_pairs={{0,48},{16,32},{32,16},{48,0},{1,49},{17,33},{33,17},{49,1},{2,50}... | collective-permute-start | bytes 589832 | tf_op jit(solution)/shard_map/ppermute | solution.py:35
  85.1 11.5 %collective-permute-start.8 = (bf16[128,768]{1,0:T(8,128)(2,1)S(1)}, bf16[128,768]{1,0:T(8,128)(2,1)S(1)}, u32[]{:S(2)}, u32[]{:S(2)}) collective-permute-start(bf16[128,768]{1,0:T(8,128)(2,1)S(1)} %get-tuple-element.28.refs_0_), channel_id=1, source_target_pairs={{0,32},{16,48},{32,0},{48,16},{1,33},{17,49},{33,1},{49,17},{2,34}... | collective-permute-start | bytes 589832 | tf_op jit(solution)/shard_map/ppermute | solution.py:35
  87.9 11.2 %collective-permute-start.7 = (bf16[128,768]{1,0:T(8,128)(2,1)S(1)}, bf16[128,768]{1,0:T(8,128)(2,1)S(1)}, u32[]{:S(2)}, u32[]{:S(2)}) collective-permute-start(bf16[128,768]{1,0:T(8,128)(2,1)S(1)} %get-tuple-element.28.refs_0_), channel_id=1, source_target_pairs={{0,16},{16,0},{32,48},{48,32},{1,17},{17,1},{33,49},{49,33},{2,18}... | collective-permute-start | bytes 589832 | tf_op jit(solution)/shard_map/ppermute | solution.py:35
  106.5 13.0 %collective-permute-start.10 = (bf16[8,160,128]{2,1,0:T(8,128)(2,1)S(1)}, bf16[8,160,128]{2,1,0:T(8,128)(2,1)S(1)}, u32[]{:S(2)}, u32[]{:S(2)}) collective-permute-start(bf16[8,160,128]{2,1,0:T(8,128)(2,1)S(1)} %all-to-all-done.3.refs_5_), channel_id=1, source_target_pairs={{0,64},{64,0},{1,65},{65,1},{2,66},{66,2},{3,67},{67,3},{4,68},{68... | collective-permute-start | bytes 983048 | tf_op jit(solution)/shard_map/ppermute | solution.py:29
  108.6 1.4 copy-start.3

commit v4 on v3

--- a/solution.py
+++ b/solution.py
@@ -14,9 +14,8 @@
 AXES = DP + SEQ
 SIZES = (2, 2, 2, 2, 2, 8, 2)
 SHARE = ("xl", "co", "zp")
-WEIGHT = ("xh", "y1", "y0")
-COLUMN = ("y1", "y0")
-SPREAD = COLUMN + ("zp",)
+SPREAD = ("xh", "y1", "y0")
+COLUMN = ("zt", "zp")
 STATS = 128
 
 
@@ -100,26 +99,26 @@
             line = jnp.concatenate([z[2 * part : 2 * part + 2], body, z[8 + 2 * part : 10 + 2 * part]])
             term = line[offset : offset + rows]
             sums[part] = term if offset == 0 else sums[part] + term
-    lane = lax.broadcasted_iota(jnp.int32, (rows // 2, 128), 1)
+    lane = lax.broadcasted_iota(jnp.int32, (held // 2, 128), 1)
     for part in range(4):
         index = jnp.bitwise_xor(group, part)
-        whole, rest = sums[part][:, :128], sums[part][:, 128:]
-        rest = jnp.where(lane < 64, rest[: rows // 2], pltpu.roll(rest, 64, 1)[rows // 2 :])
-        value = jnp.concatenate([whole, rest]).astype(jnp.bfloat16)
-        out_ref[2 * index] = value
-        out_ref[2 * index + 1] = value
-
-
-def stream_kernel(place_ref, parts_ref, mine_ref, beside_ref, gain_ref, kw_ref, vw_ref, stream_ref, in_ref, pack_ref):
-    even = place_ref[1] == 0
-    mine, beside = mine_ref[...].astype(jnp.float32), beside_ref[...].astype(jnp.float32)
-    rows = mine.shape[0]
-    lane = lax.broadcasted_iota(jnp.int32, (rows, 128), 1)
+        rest = sums[part][:, 128:]
+        turned = pltpu.roll(rest, 64, 1)
+        for half in range(2):
+            low, middle, high = half * held, half * held + held // 2, (half + 1) * held
+            value = [sums[part][low:high, :128], jnp.where(lane < 64, rest[low:middle], turned[middle:high])]
+            out_ref[2 * index + half] = jnp.concatenate(value).astype(jnp.bfloat16)
+
+
+def stream_kernel(parts_ref, mine_ref, gain_ref, kw_ref, vw_ref, stream_ref, in_ref, pack_ref):
+    inputs = mine_ref[...].astype(jnp.float32)
+    rows = inputs.shape[0]
+    lane = lax.broadcasted_iota(jnp.int32, (rows // 2, 128), 1)
     wholes, rests = [], []
     for j in range(4):
         total = parts_ref[2 * j].astype(jnp.float32) + parts_ref[2 * j + 1].astype(jnp.float32)
-        wholes.append(total[: 2 * rows])
-        rests.append((total[2 * rows :], pltpu.roll(total[2 * rows :], 64, 1)))
+        wholes.append(total[:rows])
+        rests.append((total[rows:], pltpu.roll(total[rows:], 64, 1)))
     tiles = [
         jnp.concatenate(
             [
@@ -130,18 +129,15 @@
         for j in (0, 2)
     ]
     conv_out = jnp.concatenate(wholes + tiles, axis=1)
-    inputs = jnp.concatenate([jnp.where(even, mine, beside), jnp.where(even, beside, mine)])
     stream = (inputs + conv_out).astype(jnp.bfloat16)
-    stream_ref[...] = jnp.where(even, stream[:rows], stream[rows:])
+    stream_ref[...] = stream
     attn_in = normalize(stream.astype(jnp.float32), gain_ref[...]).astype(jnp.bfloat16)
-    in_ref[...] = attn_in
-    own = jnp.where(even, attn_in[:rows], attn_in[rows:])
-    keys = jnp.dot(own, kw_ref[...], preferred_element_type=jnp.float32)
-    values = jnp.dot(own, vw_ref[...], preferred_element_type=jnp.float32)
+    for i in range(in_ref.shape[0]):
+        in_ref[i] = attn_in
+    keys = jnp.dot(attn_in, kw_ref[...], preferred_element_type=jnp.float32)
+    values = jnp.dot(attn_in, vw_ref[...], preferred_element_type=jnp.float32)
     tail = jnp.concatenate([values[: rows // 2, 128:], values[rows // 2 :, 128:]], axis=1)
-    packed = jnp.concatenate([keys, values[:, :128], tail]).astype(jnp.bfloat16)
-    for i in range(pack_ref.shape[0]):
-        pack_ref[i] = packed
+    pack_ref[...] = jnp.concatenate([keys, values[:, :128], tail]).astype(jnp.bfloat16)
 
 
 def unpack(ref, k_ref, ve_ref, vo_ref):
@@ -165,43 +161,20 @@
             vo_ref[here, 128:256] = jnp.where(lane < 64, shifted, right).astype(jnp.bfloat16)
 
 
-def near_kernel(heads, size, *refs):
-    x_refs, (qw_ref, pack_ref, q_ref, o_ref, top_ref, k_ref, ve_ref, vo_ref) = refs[:4], refs[4:]
+def attend_kernel(heads, size, x_ref, qw_ref, pack_ref, out_ref, q_ref, k_ref, ve_ref, vo_ref):
     unpack(pack_ref, k_ref, ve_ref, vo_ref)
-    x = jnp.concatenate([ref[...] for ref in x_refs])
-    q = jnp.dot(x, qw_ref[...], preferred_element_type=jnp.float32) * size ** (-0.5)
+    blocks, block, width = x_ref.shape
+    rows, chunk = blocks * block, 256
+    q = jnp.dot(x_ref[...].reshape(rows, width), qw_ref[...], preferred_element_type=jnp.float32) * size ** (-0.5)
     q_ref[...] = q.astype(jnp.bfloat16)
-    rows, chunk = x.shape[0], 256
     lane = lax.broadcasted_iota(jnp.int32, (chunk, 128), 1)
     for start in range(0, rows, chunk):
         part = slice(start, start + chunk)
-        tops = jnp.zeros((chunk, 128), jnp.float32)
-        for head in range(heads):
-            q = q_ref[part, head * size : (head + 1) * size]
-            s = jnp.dot(q, k_ref[...], preferred_element_type=jnp.float32)
-            top = jnp.max(s, axis=-1, keepdims=True)
-            p = jnp.exp(s - top).astype(jnp.bfloat16)
-            v_ref = vo_ref if head % 2 else ve_ref
-            o_ref[head, part, :] = jnp.dot(p, v_ref[...], preferred_element_type=jnp.float32)
-            tops = jnp.where(lane == head, top, tops)
-        top_ref[part, :] = tops
-
-
-def far_kernel(heads, size, place_ref, q_ref, o_ref, top_ref, pack_ref, out_ref, k_ref, ve_ref, vo_ref):
-    unpack(pack_ref, k_ref, ve_ref, vo_ref)
-    place = place_ref[0]
-    rows, chunk, block = q_ref.shape[0], 256, out_ref.shape[1]
-    lane = lax.broadcasted_iota(jnp.int32, (chunk, 128), 1)
-    for start in range(0, rows, chunk):
-        part = slice(start, start + chunk)
-        tops = top_ref[part, :]
 
         def put(low, value):
             value = value.astype(jnp.bfloat16)
             for i in range(chunk // block):
-                at = start // block + i
-                index = 2 * jnp.bitwise_xor(place, at // 2) + at % 2
-                out_ref[index, :, low : low + 128] = value[i * block : (i + 1) * block]
+                out_ref[start // block + i, :, low : low + 128] = value[i * block : (i + 1) * block]
 
         stats = jnp.zeros((chunk, STATS), jnp.float32)
         for pair in range(heads // 2):
@@ -210,12 +183,10 @@
                 head = 2 * pair + odd
                 q = q_ref[part, head * size : (head + 1) * size]
                 s = jnp.dot(q, k_ref[...], preferred_element_type=jnp.float32)
-                old = tops[:, head : head + 1]
-                peak = jnp.maximum(jnp.max(s, axis=-1, keepdims=True), old)
+                peak = jnp.max(s, axis=-1, keepdims=True)
                 p = jnp.exp(s - peak).astype(jnp.bfloat16)
                 v_ref = vo_ref if odd else ve_ref
                 o = jnp.dot(p, v_ref[...], preferred_element_type=jnp.float32)
-                o = o + o_ref[head, part, :] * jnp.exp(old - peak)
                 halves.append(o)
                 if odd:
                     stats = jnp.where(lane == head, o[:, :128], stats)
@@ -284,10 +255,9 @@
     blocks = lax.all_to_all(mine, "zt", 0, 0, tiled=True)
 
     shared = by_masks(features, DP)
-    beside = swapped(features, "zp")
-    blocks, beside, *shared = lax.optimization_barrier((blocks, beside, *shared))
-
-    blocks = everyone(blocks, WEIGHT, 8).reshape(64, 48, 128)
+    blocks, *shared = lax.optimization_barrier((blocks, *shared))
+
+    blocks = everyone(blocks, SPREAD, 8).reshape(64, 48, 128)
     activated = pl.pallas_call(
         activate_kernel,
         out_shape=jax.ShapeDtypeStruct((4, rows, width), jnp.bfloat16),
@@ -306,7 +276,7 @@
     end, far_end = (lax.ppermute(edge, SEQ, step) for step in steps)
     partial = pl.pallas_call(
         conv_kernel,
-        out_shape=jax.ShapeDtypeStruct((8, 3 * rows, 128), jnp.bfloat16),
+        out_shape=jax.ShapeDtypeStruct((8, 3 * rows // 2, 128), jnp.bfloat16),
         in_specs=[in_smem] + [in_vmem] * 5,
         out_specs=in_vmem,
         scratch_shapes=[pltpu.VMEM((KW * width, 256), jnp.float32)],
@@ -315,52 +285,34 @@
     )(place, activated, other, end, far_end, blocks)
     partial = lax.all_to_all(partial, SHARE, 0, 0, tiled=True)
 
-    stream, wide_in, packed = pl.pallas_call(
+    stream, attn_in, packed = pl.pallas_call(
         stream_kernel,
         out_shape=[
             jax.ShapeDtypeStruct((rows, width), jnp.bfloat16),
-            jax.ShapeDtypeStruct((2 * rows, width), jnp.bfloat16),
-            jax.ShapeDtypeStruct((8, 5 * rows // 2, 128), jnp.bfloat16),
+            jax.ShapeDtypeStruct((8, rows, width), jnp.bfloat16),
+            jax.ShapeDtypeStruct((5 * rows // 2, 128), jnp.bfloat16),
         ],
-        in_specs=[in_smem] + [in_vmem] * 6,
+        in_specs=[in_vmem] * 5,
         out_specs=[in_vmem] * 3,
         compiler_params=params,
         name="stream",
-    )(place, partial, features, beside, attn_gain[None], key_weight, value_weight)
-    near = lax.all_to_all(packed, "zt", 0, 0, tiled=True)
-    asked = by_masks(wide_in, COLUMN)
-    near, *asked = lax.optimization_barrier((near, *asked))
-    far = swapped(near, "xh")
-    scratch = [
-        pltpu.VMEM((size, 8 * rows), jnp.bfloat16),
-        pltpu.VMEM((8 * rows, 256), jnp.bfloat16),
-        pltpu.VMEM((8 * rows, 256), jnp.bfloat16),
-    ]
-    cost = pl.CostEstimate(flops=4_500_000_000, bytes_accessed=8_000_000, transcendentals=2_200_000)
-    queries, weighted, tops = pl.pallas_call(
-        functools.partial(near_kernel, heads, size),
-        out_shape=[
-            jax.ShapeDtypeStruct((8 * rows, heads * size), jnp.bfloat16),
-            jax.ShapeDtypeStruct((heads, 8 * rows, 256), jnp.float32),
-            jax.ShapeDtypeStruct((8 * rows, 128), jnp.float32),
+    )(partial, features, attn_gain[None], key_weight, value_weight)
+    asked = lax.all_to_all(attn_in, SPREAD, 0, 0, tiled=True)
+    pairs = lax.all_gather(packed, COLUMN, axis=0)
+    out = pl.pallas_call(
+        functools.partial(attend_kernel, heads, size),
+        out_shape=jax.ShapeDtypeStruct((8, rows, heads * value_size + STATS), jnp.bfloat16),
+        in_specs=[in_vmem] * 3,
+        out_specs=in_vmem,
+        scratch_shapes=[
+            pltpu.VMEM((8 * rows, heads * size), jnp.bfloat16),
+            pltpu.VMEM((size, 16 * rows), jnp.bfloat16),
+            pltpu.VMEM((16 * rows, 256), jnp.bfloat16),
+            pltpu.VMEM((16 * rows, 256), jnp.bfloat16),
         ],
-        in_specs=[in_vmem] * 6,
-        out_specs=[in_vmem] * 3,
-        scratch_shapes=scratch,
-        compiler_params=params,
-        cost_estimate=cost,
-        name="near",
-    )(*asked, query_weight, near)
-    out = pl.pallas_call(
-        functools.partial(far_kernel, heads, size),
-        out_shape=jax.ShapeDtypeStruct((8, rows, heads * value_size + STATS), jnp.bfloat16),
-        in_specs=[in_smem] + [in_vmem] * 4,
-        out_specs=in_vmem,
-        scratch_shapes=scratch,
-        compiler_params=params,
-        cost_estimate=cost,
-        name="far",
-    )(lax.axis_index(COLUMN)[None], queries, weighted, tops, far)
+        compiler_params=params,
+        name="attend",
+    )(asked, query_weight, pairs)
     parts = lax.all_to_all(out, SPREAD, 0, 0, tiled=True)
     attended = pl.pallas_call(
         functools.partial(combine_kernel, heads),

time: 152 us -> 142 us (0.934)
  blocking collectives: 24.9 us -> 55.2 us
  waiting for transfers between devices: 37.7 us -> 14.1 us
  starting transfers between devices: 67.5 us -> 54 us
  Pallas kernels: 16.7 us -> 13.7 us
    all_gather x0 -> x1, blocking collectives: none -> 33.4 us  [local(): pairs = lax.all_gather(packed, COLUMN, axis=0)]
    ppermute x6 -> x3, starting transfers between devices: 17.4 us -> 7.58 us  [by_masks(): lax.ppermute(block, axes, [(i, i ^ mask) for i in range(count)])]
    ppermute x3 -> x1, waiting for transfers between devices: 9.69 us -> 0.01 us  [swapped(): return lax.ppermute(block, axis, [(0, 1), (1, 0)])]
    all_to_all x1, waiting for transfers between devices: 7.38 us -> 0.01 us  [local(): asked = lax.all_to_all(attn_in, SPREAD, 0, 0, tiled=True)]
    ppermute x3 -> x1, starting transfers between devices: 8.19 us -> 3.07 us  [swapped(): return lax.ppermute(block, axis, [(0, 1), (1, 0)])]
    ppermute x6 -> x3, waiting for transfers between devices: 7.1 us -> 2.05 us  [by_masks(): lax.ppermute(block, axes, [(i, i ^ mask) for i in range(count)])]
    all_to_all x1, waiting for transfers between devices: 0.5 us -> 5.26 us  [local(): blocks = lax.all_to_all(mine, 'zt', 0, 0, tiled=True)]
    ppermute x2, waiting for transfers between devices: 6.87 us -> 2.7 us  [local(): end, far_end = (lax.ppermute(edge, SEQ, step) for step in steps)]
  transfers between devices with their start and end apart: 15 -> 10, of which waited for: 8 -> 4; matrix products, arithmetic and copies ran while one was open for 0% -> 0% of each run, Pallas kernels for 3% -> 0%
where the time goes in v4:
time: 142 us; the launch traced here: 140 us
  blocking collectives  55.2 us (39%)
  starting transfers between devices  54 us (38%)
  waiting for transfers between devices  14.1 us (10%)
  Pallas kernels  13.7 us (10%)
  local copies, waits for them, and re-layouts  2.01 us (1%)
    all_gather x1, blocking collectives, local(): pairs = lax.all_gather(packed, COLUMN, axis=0)  33.4 us
    all_to_all x1, blocking collectives, local(): parts = lax.all_to_all(out, SPREAD, 0, 0, tiled=True)  21.8 us
    all_to_all x1, starting transfers between devices, local(): blocks = lax.all_to_all(mine, 'zt', 0, 0, tiled=True)  15.1 us
    ppermute x2, starting transfers between devices, local(): end, far_end = (lax.ppermute(edge, SEQ, step) for step in steps)  11.9 us
    ppermute x3, starting transfers between devices, by_masks(): lax.ppermute(block, axes, [(i, i ^ mask) for i in range(count)])  7.58 us
    all_to_all x1, starting transfers between devices, everyone(): return lax.all_to_all(sent, axes, 0, 0, tiled=True)  7.43 us
    pallas_call x1, Pallas kernels, local(): pl.pallas_call(functools.partial(attend_kernel, heads, size), out_shape=j...  6.45 us
    all_to_all x1, waiting for transfers between devices, local(): blocks = lax.all_to_all(mine, 'zt', 0, 0, tiled=True)  5.26 us
  transfers between devices with their start and end apart: 10, of which 4 were waited for; matrix products, arithmetic and copies ran while one was open for 0% of the time, Pallas kernels for 0%

profile of v4, /device:TPU:6, one launch (start us, length us, event | category | flops | bytes accessed | tf_op | source)
XLA Modules:
  0.0 139.9 jit_solution(10354119312756327914)
XLA Ops:
  0.6 0.0 copy-start.1
  0.7 0.8 copy-done.3
  1.5 0.7 pack.1
  2.2 15.1 %all-to-all-start = ((bf16[8,48,128]{2,1,0:T(8,128)(2,1)}), bf16[8,48,128]{2,1,0:T(8,128)(2,1)S(1)}, u32[]{:S(2)}, u32[]{:S(2)}) async-start(bf16[8,48,128]{2,1,0:T(8,128)(2,1)} %pack.1), calls=%async_computation | async-start | bytes 196608 | tf_op jit(solution)/shard_map/all_to_all | solution.py:255
  17.3 1.9 %collective-permute-start.2 = (bf16[64,768]{1,0:T(8,128)(2,1)}, bf16[64,768]{1,0:T(8,128)(2,1)S(1)}, u32[]{:S(2)}, u32[]{:S(2)}) collective-permute-start(bf16[64,768]{1,0:T(8,128)(2,1)} %mine_ref.1), channel_id=1, source_target_pairs={{0,384},{128,256},{256,128},{384,0},{1,385},{129,257},{257,129},{3... | collective-permute-start | bytes 294920 | tf_op jit(solution)/shard_map/ppermute | solution.py:34
  19.2 3.1 %collective-permute-start.1 = (bf16[64,768]{1,0:T(8,128)(2,1)}, bf16[64,768]{1,0:T(8,128)(2,1)S(1)}, u32[]{:S(2)}, u32[]{:S(2)}) collective-permute-start(bf16[64,768]{1,0:T(8,128)(2,1)} %mine_ref.1), channel_id=1, source_target_pairs={{0,256},{128,384},{256,0},{384,128},{1,257},{129,385},{257,1},{385... | collective-permute-start | bytes 294920 | tf_op jit(solution)/shard_map/ppermute | solution.py:34
  22.3 2.6 %collective-permute-start = (bf16[64,768]{1,0:T(8,128)(2,1)}, bf16[64,768]{1,0:T(8,128)(2,1)S(1)}, u32[]{:S(2)}, u32[]{:S(2)}) collective-permute-start(bf16[64,768]{1,0:T(8,128)(2,1)} %mine_ref.1), channel_id=1, source_target_pairs={{0,128},{128,0},{256,384},{384,256},{1,129},{129,1},{257,385},{385... | collective-permute-start | bytes 294920 | tf_op jit(solution)/shard_map/ppermute | solution.py:34
  24.9 2.0 %collective-permute-done.1.refs_2_ = bf16[64,768]{1,0:T(8,128)(2,1)S(1)} collective-permute-done((bf16[64,768]{1,0:T(8,128)(2,1)}, bf16[64,768]{1,0:T(8,128)(2,1)S(1)}, u32[]{:S(2)}, u32[]{:S(2)}) %collective-permute-start.1) | collective-permute-done | bytes 98336 | tf_op jit(solution)/shard_map/ppermute | solution.py:34
  26.9 0.0 collective-permute-done.refs_1_
  27.0 5.3 %all-to-all-done = bf16[8,48,128]{2,1,0:T(8,128)(2,1)S(1)} async-done(((bf16[8,48,128]{2,1,0:T(8,128)(2,1)}), bf16[8,48,128]{2,1,0:T(8,128)(2,1)S(1)}, u32[]{:S(2)}, u32[]{:S(2)}) %all-to-all-start) | async-done | bytes 98336 | tf_op jit(solution)/shard_map/all_to_all | solution.py:255
  32.2 1.0 broadcast_in_dim.13
  33.2 7.4 %all-to-all-start.1 = ((bf16[8,8,48,128]{3,2,1,0:T(8,128)(2,1)}), bf16[8,8,48,128]{3,2,1,0:T(8,128)(2,1)S(1)}, u32[]{:S(2)}, u32[]{:S(2)}) async-start(bf16[8,8,48,128]{3,2,1,0:T(8,128)(2,1)} %broadcast_in_dim.13), calls=%async_computation.1 | async-start | bytes 1572864 | tf_op jit(solution)/shard_map/all_to_all | solution.py:24
  40.7 0.0 copy-start.2
  40.7 0.4 activate.1.mine_ref
  41.1 3.1 %collective-permute-start.3 = (bf16[4,64,768]{2,1,0:T(8,128)(2,1)S(1)}, bf16[4,64,768]{2,1,0:T(8,128)(2,1)S(1)}, u32[]{:S(2)}, u32[]{:S(2)}) collective-permute-start(bf16[4,64,768]{2,1,0:T(8,128)(2,1)S(1)} %activate.1.mine_ref), channel_id=1, source_target_pairs={{0,1},{1,0},{2,3},{3,2},{4,5},{5,4},{6,7},{7,6},{8,9},{9,8},{10,11... | collective-permute-start | bytes 1179656 | tf_op jit(solution)/shard_map/ppermute | solution.py:28
  44.2 3.3 %collective-permute-start.5 = (bf16[4,2,768]{2,1,0:T(2,128)(2,1)S(1)}, bf16[4,2,768]{2,1,0:T(2,128)(2,1)S(1)}, u32[]{:S(2)}, u32[]{:S(2)}) collective-permute-start(bf16[4,2,768]{2,1,0:T(2,128)(2,1)S(1)} %broadcast_select_fusion), channel_id=1, source_target_pairs={{1,3},{3,5},{5,7},{7,9},{9,11},{11,13},{13,15},{15,17},{17,19},{19... | collective-permute-start | bytes 36872 | tf_op jit(solution)/shard_map/ppermute | solution.py:276
  47.6 8.5 %collective-permute-start.4 = (bf16[4,2,768]{2,1,0:T(2,128)(2,1)S(1)}, bf16[4,2,768]{2,1,0:T(2,128)(2,1)S(1)}, u32[]{:S(2)}, u32[]{:S(2)}) collective-permute-start(bf16[4,2,768]{2,1,0:T(2,128)(2,1)S(1)} %broadcast_select_fusion), channel_id=1, source_target_pairs={{1,2},{3,4},{5,6},{7,8},{9,10},{11,12},{13,14},{15,16},{17,18},{19... | collective-permute-start | bytes 36872 | tf_op jit(solution)/shard_map/ppermute | solution.py:276
  56.1 0.1 pad_add_fusion.place_ref
  56.2 2.7 %collective-permute-done.4.end_ref = bf16[4,2,768]{2,1,0:T(2,128)(2,1)S(1)} collective-permute-done((bf16[4,2,768]{2,1,0:T(2,128)(2,1)S(1)}, bf16[4,2,768]{2,1,0:T(2,128)(2,1)S(1)}, u32[]{:S(2)}, u32[]{:S(2)}) %collective-permute-start.4) | collective-permute-done | bytes 12320 | tf_op jit(solution)/shard_map/ppermute | solution.py:276
  58.9 0.0 collective-permute-done.3.other_ref
  58.9 0.0 all-to-all-done.1
  58.9 3.2 %conv.1 = bf16[8,96,128]{2,1,0:T(8,128)(2,1)} custom-call(s32[2]{0:T(128)S(1)} %pad_add_fusion.place_ref, bf16[4,64,768]{2,1,0:T(8,128)(2,1)S(1)} %activate.1.mine_ref, bf16[4,64,768]{2,1,0:T(8,128)(2,1)S(1)} %collective-permute-done.3.other_ref, bf16[4,2,768]{2,1,0:T(2,128)(2,1)S(1)} %collective-permute-done.4.end_ref, ...), custom_call_target="tpu_custom_call" | custom-call | tf_op jit(solution)/shard_map/conv/pallas_call | solution.py:277
  62.1 4.1 %all-to-all-start.2 = ((bf16[8,96,128]{2,1,0:T(8,128)(2,1)}), bf16[8,96,128]{2,1,0:T(8,128)(2,1)S(1)}, u32[]{:S(2)}, u32[]{:S(2)}) async-start(bf16[8,96,128]{2,1,0:T(8,128)(2,1)} %conv.1), calls=%async_computation.2 | async-start | bytes 393216 | tf_op jit(solution)/shard_map/all_to_all | solution.py:286
  66.3 0.2 copy.9.vw_ref
  66.4 0.0 copy-start
  66.5 4.1 %all-to-all-done.2.parts_ref = bf16[8,96,128]{2,1,0:T(8,128)(2,1)S(1)} async-done(((bf16[8,96,128]{2,1,0:T(8,128)(2,1)}), bf16[8,96,128]{2,1,0:T(8,128)(2,1)S(1)}, u32[]{:S(2)}, u32[]{:S(2)}) %all-to-all-start.2) | async-done | bytes 196640 | tf_op jit(solution)/shard_map/all_to_all | solution.py:286
  70.5 1.1 stream.1
  71.6 4.8 %all-to-all-start.3 = ((bf16[8,64,768]{2,1,0:T(8,128)(2,1)}), bf16[8,64,768]{2,1,0:T(8,128)(2,1)S(1)}, u32[]{:S(2)}, u32[]{:S(2)}) async-start(bf16[8,64,768]{2,1,0:T(8,128)(2,1)} %get-tuple-element.16), calls=%async_computation.3 | async-start | bytes 1572864 | tf_op jit(solution)/shard_map/all_to_all | solution.py:300
  76.4 33.4 %all-gather = bf16[2560,128]{1,0:T(8,128)(2,1)S(1)} all-gather(bf16[160,128]{1,0:T(8,128)(2,1)S(1)} %get-tuple-element.17), channel_id=2, replica_groups=mesh['xl'=2,'co'=2,'xh'=2,'y1'=2,'y0'=2,'zt'=8,'zp'=2] {'zt','zp'}, dimensions={0}, use_global_device_ids=true | all-gather | bytes 696320 | tf_op jit(solution)/shard_map/all_gather | solution.py:301
  109.9 6.5 %attend.1 = bf16[8,64,1664]{2,1,0:T(8,128)(2,1)S(1)} custom-call(bf16[8,64,768]{2,1,0:T(8,128)(2,1)S(1)} %all-to-all-done.3.x_ref, bf16[768,1024]{1,0:T(8,128)(2,1)S(1)} %copy-done, bf16[16,160,128]{2,1,0:T(8,128)(2,1)S(1)} %bitcast.5), custom_call_target="tpu_custom_call" | custom-call | tf_op jit(solution)/shard_map/attend/pallas_call | solution.py:302
  116.3 21.8 %all_to_all.25.parts_ref = bf16[8,64,1664]{2,1,0:T(8,128)(2,1)S(1)} all-to-all(bf16[8,64,1664]{2,1,0:T(8,128)(2,1)S(1)} %attend.1), channel_id=1, replica_groups=mesh['xl'=2,'co'=2,'xh'=2,'y1'=2,'y0'=2,'zt'=8,'zp'=2] {'xh','y1','y0'}, dimensions={0} | all-to-all | bytes 3407872 | tf_op jit(solution)/shard_map/all_to_all | solution.py:316
  138.1 1.8 %combine.1 = bf16[64,1536]{1,0:T(8,128)(2,1)} custom-call(bf16[8,64,1664]{2,1,0:T(8,128)(2,1)S(1)} %all_to_all.25.parts_ref), custom_call_target="tpu_custom_call" | custom-call | tf_op jit(solution)/shard_map/combine/pallas_call | solution.py:317
  (16 shorter events, 0.1 us)
Async XLA Ops:
  0.6 40.0 %copy-start.1 = (bf16[64,768]{1,0:T(8,128)(2,1)S(1)}, bf16[64,768]{1,0:T(8,128)(2,1)}, u32[]{:S(2)}) copy-start(bf16[64,768]{1,0:T(8,128)(2,1)} %mine_ref.1) | copy-start | bytes 294916
  0.6 0.8 copy-start.3
  1.5 39.2 %copy-start.5 = (f32[768]{0:T(1024)S(1)}, f32[768]{0:T(1024)}, u32[]{:S(2)}) copy-start(f32[768]{0:T(1024)} %param.8) | copy-start | bytes 9220
  2.2 30.0 %all-to-all-start = ((bf16[8,48,128]{2,1,0:T(8,128)(2,1)}), bf16[8,48,128]{2,1,0:T(8,128)(2,1)S(1)}, u32[]{:S(2)}, u32[]{:S(2)}) async-start(bf16[8,48,128]{2,1,0:T(8,128)(2,1)} %pack.1), calls=%async_computation | async-start | bytes 196608 | tf_op jit(solution)/shard_map/all_to_all | solution.py:255
  17.3 7.6 %collective-permute-start.2 = (bf16[64,768]{1,0:T(8,128)(2,1)}, bf16[64,768]{1,0:T(8,128)(2,1)S(1)}, u32[]{:S(2)}, u32[]{:S(2)}) collective-permute-start(bf16[64,768]{1,0:T(8,128)(2,1)} %mine_ref.1), channel_id=1, source_target_pairs={{0,384},{128,256},{256,128},{384,0},{1,385},{129,257},{257,129},{3... | collective-permute-start | bytes 294920 | tf_op jit(solution)/shard_map/ppermute | solution.py:34
  19.2 7.7 %collective-permute-start.1 = (bf16[64,768]{1,0:T(8,128)(2,1)}, bf16[64,768]{1,0:T(8,128)(2,1)S(1)}, u32[]{:S(2)}, u32[]{:S(2)}) collective-permute-start(bf16[64,768]{1,0:T(8,128)(2,1)} %mine_ref.1), channel_id=1, source_target_pairs={{0,256},{128,384},{256,0},{384,128},{1,257},{129,385},{257,1},{385... | collective-permute-start | bytes 294920 | tf_op jit(solution)/shard_map/ppermute | solution.py:34
  22.3 4.6 %collective-permute-start = (bf16[64,768]{1,0:T(8,128)(2,1)}, bf16[64,768]{1,0:T(8,128)(2,1)S(1)}, u32[]{:S(2)}, u32[]{:S(2)}) collective-permute-start(bf16[64,768]{1,0:T(8,128)(2,1)} %mine_ref.1), channel_id=1, source_target_pairs={{0,128},{128,0},{256,384},{384,256},{1,129},{129,1},{257,385},{385... | collective-permute-start | bytes 294920 | tf_op jit(solution)/shard_map/ppermute | solution.py:34
  33.2 25.7 %all-to-all-start.1 = ((bf16[8,8,48,128]{3,2,1,0:T(8,128)(2,1)}), bf16[8,8,48,128]{3,2,1,0:T(8,128)(2,1)S(1)}, u32[]{:S(2)}, u32[]{:S(2)}) async-start(bf16[8,8,48,128]{3,2,1,0:T(8,128)(2,1)} %broadcast_in_dim.13), calls=%async_computation.1 | async-start | bytes 1572864 | tf_op jit(solution)/shard_map/all_to_all | solution.py:24
  40.6 25.6 %copy-start.6 = (f32[768]{0:T(1024)S(1)}, f32[768]{0:T(1024)}, u32[]{:S(2)}) copy-start(f32[768]{0:T(1024)} %param.10) | copy-start | bytes 9220
  40.6 25.6 %copy-start.4 = (bf16[768,192]{0,1:T(8,128)(2,1)S(1)}, bf16[768,192]{0,1:T(8,128)(2,1)}, u32[]{:S(2)}) copy-start(bf16[768,192]{0,1:T(8,128)(2,1)} %param.13) | copy-start | bytes 884740
  40.7 29.9 %copy-start.2 = (bf16[768,128]{1,0:T(8,128)(2,1)S(1)}, bf16[768,128]{1,0:T(8,128)(2,1)}, u32[]{:S(2)}) copy-start(bf16[768,128]{1,0:T(8,128)(2,1)} %kw_ref.1) | copy-start | bytes 589828
  41.1 17.8 %collective-permute-start.3 = (bf16[4,64,768]{2,1,0:T(8,128)(2,1)S(1)}, bf16[4,64,768]{2,1,0:T(8,128)(2,1)S(1)}, u32[]{:S(2)}, u32[]{:S(2)}) collective-permute-start(bf16[4,64,768]{2,1,0:T(8,128)(2,1)S(1)} %activate.1.mine_ref), channel_id=1, source_target_pairs={{0,1},{1,0},{2,3},{3,2},{4,5},{5,4},{6,7},{7,6},{8,9},{9,8},{10,11... | collective-permute-start | bytes 1179656 | tf_op jit(solution)/shard_map/ppermute | solution.py:28
  44.2 12.0 %collective-permute-start.5 = (bf16[4,2,768]{2,1,0:T(2,128)(2,1)S(1)}, bf16[4,2,768]{2,1,0:T(2,128)(2,1)S(1)}, u32[]{:S(2)}, u32[]{:S(2)}) collective-permute-start(bf16[4,2,768]{2,1,0:T(2,128)(2,1)S(1)} %broadcast_select_fusion), channel_id=1, source_target_pairs={{1,3},{3,5},{5,7},{7,9},{9,11},{11,13},{13,15},{15,17},{17,19},{19... | collective-permute-start | bytes 36872 | tf_op jit(solution)/shard_map/ppermute | solution.py:276
  47.6 11.3 %collective-permute-start.4 = (bf16[4,2,768]{2,1,0:T(2,128)(2,1)S(1)}, bf16[4,2,768]{2,1,0:T(2,128)(2,1)S(1)}, u32[]{:S(2)}, u32[]{:S(2)}) collective-permute-start(bf16[4,2,768]{2,1,0:T(2,128)(2,1)S(1)} %broadcast_select_fusion), channel_id=1, source_target_pairs={{1,2},{3,4},{5,6},{7,8},{9,10},{11,12},{13,14},{15,16},{17,18},{19... | collective-permute-start | bytes 36872 | tf_op jit(solution)/shard_map/ppermute | solution.py:276
  62.1 8.4 %all-to-all-start.2 = ((bf16[8,96,128]{2,1,0:T(8,128)(2,1)}), bf16[8,96,128]{2,1,0:T(8,128)(2,1)S(1)}, u32[]{:S(2)}, u32[]{:S(2)}) async-start(bf16[8,96,128]{2,1,0:T(8,128)(2,1)} %conv.1), calls=%async_computation.2 | async-start | bytes 393216 | tf_op jit(solution)/shard_map/all_to_all | solution.py:286
  66.4 43.4 %copy-start = (bf16[768,1024]{1,0:T(8,128)(2,1)S(1)}, bf16[768,1024]{1,0:T(8,128)(2,1)}, u32[]{:S(2)}) copy-start(bf16[768,1024]{1,0:T(8,128)(2,1)} %qw_ref.1) | copy-start | bytes 4718596
  71.6 38.2 %all-to-all-start.3 = ((bf16[8,64,768]{2,1,0:T(8,128)(2,1)}), bf16[8,64,768]{2,1,0:T(8,128)(2,1)S(1)}, u32[]{:S(2)}, u32[]{:S(2)}) async-start(bf16[8,64,768]{2,1,0:T(8,128)(2,1)} %get-tuple-element.16), calls=%async_computation.3 | async-start | bytes 1572864 | tf_op jit(solution)/shard_map/all_to_all | solution.py:300

commit v5 on v4

--- a/solution.py
+++ b/solution.py
@@ -64,11 +64,10 @@
         out_ref[i] = jax.nn.gelu(values, approximate=True).astype(jnp.bfloat16)
 
 
-def conv_kernel(place_ref, mine_ref, other_ref, end_ref, far_end_ref, w_ref, out_ref, wide_ref):
-    group, zp = place_ref[0], place_ref[1]
-    _, held, width = mine_ref.shape
-    rows = 2 * held
-    count, depth = w_ref.shape[0], KW * width // 128
+def expand_kernel(place_ref, w_ref, out_ref, wide_ref):
+    zp = place_ref[1]
+    count = w_ref.shape[0]
+    depth = out_ref.shape[0] // (2 * count)
     wide_ref[...] = jnp.zeros_like(wide_ref)
     for side in range(2):
 
@@ -82,6 +81,13 @@
                 wide_ref[start : start + depth // 2, 128:] = tail[: depth // 2]
                 wide_ref[start + depth // 2 : start + depth, 128:] = pltpu.roll(tail, 64, 1)[: depth // 2]
 
+    out_ref[...] = wide_ref[...].astype(jnp.bfloat16)
+
+
+def conv_kernel(place_ref, mine_ref, other_ref, end_ref, far_end_ref, wide_ref, out_ref):
+    group, zp = place_ref[0], place_ref[1]
+    _, held, width = mine_ref.shape
+    rows = 2 * held
     even = zp == 0
     mine, other = mine_ref[...], other_ref[...]
     first, second = jnp.where(even, mine, other), jnp.where(even, other, mine)
@@ -91,7 +97,7 @@
     ends = jnp.concatenate([before.reshape(8, width), after.reshape(8, width)]).astype(jnp.bfloat16)
     sums = [None] * 4
     for offset in range(KW):
-        w = wide_ref[offset * width : (offset + 1) * width, :].astype(jnp.bfloat16)
+        w = wide_ref[offset * width : (offset + 1) * width, :]
         y = jnp.dot(x, w, preferred_element_type=jnp.float32)
         z = jnp.dot(ends, w, preferred_element_type=jnp.float32)
         for part in range(4):
@@ -168,41 +174,43 @@
     q = jnp.dot(x_ref[...].reshape(rows, width), qw_ref[...], preferred_element_type=jnp.float32) * size ** (-0.5)
     q_ref[...] = q.astype(jnp.bfloat16)
     lane = lax.broadcasted_iota(jnp.int32, (chunk, 128), 1)
-    for start in range(0, rows, chunk):
-        part = slice(start, start + chunk)
-
-        def put(low, value):
-            value = value.astype(jnp.bfloat16)
-            for i in range(chunk // block):
-                out_ref[start // block + i, :, low : low + 128] = value[i * block : (i + 1) * block]
-
-        stats = jnp.zeros((chunk, STATS), jnp.float32)
-        for pair in range(heads // 2):
-            halves = []
-            for odd in range(2):
-                head = 2 * pair + odd
-                q = q_ref[part, head * size : (head + 1) * size]
-                s = jnp.dot(q, k_ref[...], preferred_element_type=jnp.float32)
-                peak = jnp.max(s, axis=-1, keepdims=True)
-                p = jnp.exp(s - peak).astype(jnp.bfloat16)
-                v_ref = vo_ref if odd else ve_ref
-                o = jnp.dot(p, v_ref[...], preferred_element_type=jnp.float32)
-                halves.append(o)
-                if odd:
-                    stats = jnp.where(lane == head, o[:, :128], stats)
-                else:
-                    stats = jnp.where(lane == 64 + head, o[:, 128:], stats)
-                stats = jnp.where(lane == 16 + head, peak, stats)
-            even, odd = halves
-            base = pair * 384
-            put(base, even[:, :128])
-            put(base + 128, jnp.where(lane < 64, even[:, 128:], odd[:, :128]))
-            put(base + 256, odd[:, 128:])
-        first = stats.astype(jnp.bfloat16).astype(jnp.float32)
-        rest = stats - first
-        second = rest.astype(jnp.bfloat16).astype(jnp.float32)
-        third = rest - second
-        put(heads * 192, first + pltpu.roll(second, 8, 1) + pltpu.roll(third, 32, 1))
+    def scores(start, head):
+        q = q_ref[start : start + chunk, head * size : (head + 1) * size]
+        return jnp.dot(q, k_ref[...], preferred_element_type=jnp.float32)
+
+    def put(start, low, value):
+        value = value.astype(jnp.bfloat16)
+        for i in range(chunk // block):
+            out_ref[start // block + i, :, low : low + 128] = value[i * block : (i + 1) * block]
+
+    steps = [(start, head) for start in range(0, rows, chunk) for head in range(heads)]
+    following = scores(*steps[0])
+    for step, (start, head) in enumerate(steps):
+        s = following
+        if step + 1 < len(steps):
+            following = scores(*steps[step + 1])
+        peak = jnp.max(s, axis=-1, keepdims=True)
+        p = jnp.exp(s - peak).astype(jnp.bfloat16)
+        if head == 0:
+            stats = jnp.zeros((chunk, STATS), jnp.float32)
+        base = head // 2 * 384
+        if head % 2 == 0:
+            even = jnp.dot(p, ve_ref[...], preferred_element_type=jnp.float32)
+            stats = jnp.where(lane == 72 + head, even[:, 128:], stats)
+            stats = jnp.where(lane == 64 + head, peak, stats)
+            put(start, base, even[:, :128])
+        else:
+            odd = jnp.dot(p, vo_ref[...], preferred_element_type=jnp.float32)
+            stats = jnp.where(lane == 8 + head, odd[:, :128], stats)
+            stats = jnp.where(lane == head, peak, stats)
+            put(start, base + 128, jnp.where(lane < 64, even[:, 128:], odd[:, :128]))
+            put(start, base + 256, odd[:, 128:])
+        if head == heads - 1:
+            first = stats.astype(jnp.bfloat16).astype(jnp.float32)
+            rest = stats - first
+            second = rest.astype(jnp.bfloat16).astype(jnp.float32)
+            third = rest - second
+            put(start, heads * 192, first + pltpu.roll(second, 16, 1) + pltpu.roll(third, 32, 1))
 
 
 def combine_kernel(heads, parts_ref, out_ref):
@@ -212,16 +220,16 @@
     parts = []
     for i in range(count):
         stats = parts_ref[i, :, base:].astype(jnp.float32)
-        parts.append(stats + pltpu.roll(stats, STATS - 8, 1) + pltpu.roll(stats, STATS - 32, 1))
+        parts.append(stats + pltpu.roll(stats, STATS - 16, 1) + pltpu.roll(stats, STATS - 32, 1))
+    top = functools.reduce(jnp.maximum, parts)
+    scales = [jnp.exp(part - top) for part in parts]
+    terms = [scale * pltpu.roll(part, STATS - 8, 1) for part, scale in zip(parts, scales)]
+    inverse = 1.0 / functools.reduce(jnp.add, terms)
+    shares = [scale * inverse for scale in scales]
     weights = []
     for head in range(heads):
-        sum_lane = head if head % 2 else 64 + head
-        peaks = [part[:, 16 + head : 17 + head] for part in parts]
-        top = functools.reduce(jnp.maximum, peaks)
-        scales = [jnp.exp(peak - top) for peak in peaks]
-        terms = [part[:, sum_lane : sum_lane + 1] * scale for part, scale in zip(parts, scales)]
-        inverse = 1.0 / functools.reduce(jnp.add, terms)
-        weights.append([scale * inverse for scale in scales])
+        at = head if head % 2 else 64 + head
+        weights.append([share[:, at : at + 1] for share in shares])
     for tile in range(heads * 192 // 128):
         low, high = tile * 128 // 192, (tile * 128 + 127) // 192
         total = jnp.zeros((rows, 128), jnp.float32)
@@ -274,15 +282,23 @@
     ]
     other = swapped(activated, "zp")
     end, far_end = (lax.ppermute(edge, SEQ, step) for step in steps)
+    wide = pl.pallas_call(
+        expand_kernel,
+        out_shape=jax.ShapeDtypeStruct((KW * width, 256), jnp.bfloat16),
+        in_specs=[in_smem, in_vmem],
+        out_specs=in_vmem,
+        scratch_shapes=[pltpu.VMEM((KW * width, 256), jnp.float32)],
+        compiler_params=params,
+        name="expand",
+    )(place, blocks)
     partial = pl.pallas_call(
         conv_kernel,
         out_shape=jax.ShapeDtypeStruct((8, 3 * rows // 2, 128), jnp.bfloat16),
         in_specs=[in_smem] + [in_vmem] * 5,
         out_specs=in_vmem,
-        scratch_shapes=[pltpu.VMEM((KW * width, 256), jnp.float32)],
         compiler_params=params,
         name="conv",
-    )(place, activated, other, end, far_end, blocks)
+    )(place, activated, other, end, far_end, wide)
     partial = lax.all_to_all(partial, SHARE, 0, 0, tiled=True)
 
     stream, attn_in, packed = pl.pallas_call(

time: 142 us -> 139 us (0.979)
    ppermute x2, starting transfers between devices: 11.9 us -> 8.46 us  [local(): end, far_end = (lax.ppermute(edge, SEQ, step) for step in steps)]
    all_to_all x1, starting transfers between devices: 4.14 us -> 6.44 us  [local(): partial = lax.all_to_all(partial, SHARE, 0, 0, tiled=True)]
    ppermute x3, waiting for transfers between devices: 2.05 us -> 3.94 us  [by_masks(): lax.ppermute(block, axes, [(i, i ^ mask) for i in range(count)])]
    all_to_all x1, waiting for transfers between devices: 5.26 us -> 3.37 us  [local(): blocks = lax.all_to_all(mine, 'zt', 0, 0, tiled=True)]
  transfers between devices with their start and end apart: 10 -> 10, of which waited for: 4 -> 5; matrix products, arithmetic and copies ran while one was open for 0% -> 0% of each run, Pallas kernels for 0% -> 1%
where the time goes in v5:
time: 139 us; the launch traced here: 137 us
  blocking collectives  54.6 us (39%)
  starting transfers between devices  52.9 us (38%)
  Pallas kernels  13.9 us (10%)
  waiting for transfers between devices  12.9 us (9%)
  local copies, waits for them, and re-layouts  2.02 us (1%)
    all_gather x1, blocking collectives, local(): pairs = lax.all_gather(packed, COLUMN, axis=0)  33.1 us
    all_to_all x1, blocking collectives, local(): parts = lax.all_to_all(out, SPREAD, 0, 0, tiled=True)  21.5 us
    all_to_all x1, starting transfers between devices, local(): blocks = lax.all_to_all(mine, 'zt', 0, 0, tiled=True)  15.1 us
    ppermute x2, starting transfers between devices, local(): end, far_end = (lax.ppermute(edge, SEQ, step) for step in steps)  8.46 us
    ppermute x3, starting transfers between devices, by_masks(): lax.ppermute(block, axes, [(i, i ^ mask) for i in range(count)])  7.58 us
    all_to_all x1, starting transfers between devices, everyone(): return lax.all_to_all(sent, axes, 0, 0, tiled=True)  7.43 us
    all_to_all x1, starting transfers between devices, local(): partial = lax.all_to_all(partial, SHARE, 0, 0, tiled=True)  6.44 us
    pallas_call x1, Pallas kernels, local(): pl.pallas_call(functools.partial(attend_kernel, heads, size), out_shape=j...  6.09 us
  transfers between devices with their start and end apart: 10, of which 5 were waited for; matrix products, arithmetic and copies ran while one was open for 0% of the time, Pallas kernels for 1%

profile of v5, /device:TPU:6, one launch (start us, length us, event | category | flops | bytes accessed | tf_op | source)
XLA Modules:
  0.0 137.2 jit_solution(15754971239799788990)
XLA Ops:
  0.6 0.0 copy-start.1
  0.7 0.8 copy-done.3
  1.5 0.7 pack.1
  2.2 15.1 %all-to-all-start = ((bf16[8,48,128]{2,1,0:T(8,128)(2,1)}), bf16[8,48,128]{2,1,0:T(8,128)(2,1)S(1)}, u32[]{:S(2)}, u32[]{:S(2)}) async-start(bf16[8,48,128]{2,1,0:T(8,128)(2,1)} %pack.1), calls=%async_computation | async-start | bytes 196608 | tf_op jit(solution)/shard_map/all_to_all | solution.py:263
  17.3 1.9 %collective-permute-start = (bf16[64,768]{1,0:T(8,128)(2,1)}, bf16[64,768]{1,0:T(8,128)(2,1)S(1)}, u32[]{:S(2)}, u32[]{:S(2)}) collective-permute-start(bf16[64,768]{1,0:T(8,128)(2,1)} %mine_ref.1), channel_id=1, source_target_pairs={{0,128},{128,0},{256,384},{384,256},{1,129},{129,1},{257,385},{385... | collective-permute-start | bytes 294920 | tf_op jit(solution)/shard_map/ppermute | solution.py:34
  19.2 2.7 %collective-permute-start.1 = (bf16[64,768]{1,0:T(8,128)(2,1)}, bf16[64,768]{1,0:T(8,128)(2,1)S(1)}, u32[]{:S(2)}, u32[]{:S(2)}) collective-permute-start(bf16[64,768]{1,0:T(8,128)(2,1)} %mine_ref.1), channel_id=1, source_target_pairs={{0,256},{128,384},{256,0},{384,128},{1,257},{129,385},{257,1},{385... | collective-permute-start | bytes 294920 | tf_op jit(solution)/shard_map/ppermute | solution.py:34
  22.0 2.9 %collective-permute-start.2 = (bf16[64,768]{1,0:T(8,128)(2,1)}, bf16[64,768]{1,0:T(8,128)(2,1)S(1)}, u32[]{:S(2)}, u32[]{:S(2)}) collective-permute-start(bf16[64,768]{1,0:T(8,128)(2,1)} %mine_ref.1), channel_id=1, source_target_pairs={{0,384},{128,256},{256,128},{384,0},{1,385},{129,257},{257,129},{3... | collective-permute-start | bytes 294920 | tf_op jit(solution)/shard_map/ppermute | solution.py:34
  24.9 1.6 %collective-permute-done.1.refs_2_ = bf16[64,768]{1,0:T(8,128)(2,1)S(1)} collective-permute-done((bf16[64,768]{1,0:T(8,128)(2,1)}, bf16[64,768]{1,0:T(8,128)(2,1)S(1)}, u32[]{:S(2)}, u32[]{:S(2)}) %collective-permute-start.1) | collective-permute-done | bytes 98336 | tf_op jit(solution)/shard_map/ppermute | solution.py:34
  26.5 2.3 %collective-permute-done.2.refs_3_ = bf16[64,768]{1,0:T(8,128)(2,1)S(1)} collective-permute-done((bf16[64,768]{1,0:T(8,128)(2,1)}, bf16[64,768]{1,0:T(8,128)(2,1)S(1)}, u32[]{:S(2)}, u32[]{:S(2)}) %collective-permute-start.2) | collective-permute-done | bytes 98336 | tf_op jit(solution)/shard_map/ppermute | solution.py:34
  28.8 3.4 %all-to-all-done = bf16[8,48,128]{2,1,0:T(8,128)(2,1)S(1)} async-done(((bf16[8,48,128]{2,1,0:T(8,128)(2,1)}), bf16[8,48,128]{2,1,0:T(8,128)(2,1)S(1)}, u32[]{:S(2)}, u32[]{:S(2)}) %all-to-all-start) | async-done | bytes 98336 | tf_op jit(solution)/shard_map/all_to_all | solution.py:263
  32.2 1.0 broadcast_in_dim.13
  33.2 7.4 %all-to-all-start.1 = ((bf16[8,8,48,128]{3,2,1,0:T(8,128)(2,1)}), bf16[8,8,48,128]{3,2,1,0:T(8,128)(2,1)S(1)}, u32[]{:S(2)}, u32[]{:S(2)}) async-start(bf16[8,8,48,128]{3,2,1,0:T(8,128)(2,1)} %broadcast_in_dim.13), calls=%async_computation.1 | async-start | bytes 1572864 | tf_op jit(solution)/shard_map/all_to_all | solution.py:24
  40.6 0.4 activate.1.mine_ref
  41.1 3.1 %collective-permute-start.3 = (bf16[4,64,768]{2,1,0:T(8,128)(2,1)S(1)}, bf16[4,64,768]{2,1,0:T(8,128)(2,1)S(1)}, u32[]{:S(2)}, u32[]{:S(2)}) collective-permute-start(bf16[4,64,768]{2,1,0:T(8,128)(2,1)S(1)} %activate.1.mine_ref), channel_id=1, source_target_pairs={{0,1},{1,0},{2,3},{3,2},{4,5},{5,4},{6,7},{7,6},{8,9},{9,8},{10,11... | collective-permute-start | bytes 1179656 | tf_op jit(solution)/shard_map/ppermute | solution.py:28
  44.2 4.2 %collective-permute-start.4 = (bf16[4,2,768]{2,1,0:T(2,128)(2,1)S(1)}, bf16[4,2,768]{2,1,0:T(2,128)(2,1)S(1)}, u32[]{:S(2)}, u32[]{:S(2)}) collective-permute-start(bf16[4,2,768]{2,1,0:T(2,128)(2,1)S(1)} %broadcast_select_fusion), channel_id=1, source_target_pairs={{1,2},{3,4},{5,6},{7,8},{9,10},{11,12},{13,14},{15,16},{17,18},{19... | collective-permute-start | bytes 36872 | tf_op jit(solution)/shard_map/ppermute | solution.py:284
  48.4 4.3 %collective-permute-start.5 = (bf16[4,2,768]{2,1,0:T(2,128)(2,1)S(1)}, bf16[4,2,768]{2,1,0:T(2,128)(2,1)S(1)}, u32[]{:S(2)}, u32[]{:S(2)}) collective-permute-start(bf16[4,2,768]{2,1,0:T(2,128)(2,1)S(1)} %broadcast_select_fusion), channel_id=1, source_target_pairs={{1,3},{3,5},{5,7},{7,9},{9,11},{11,13},{13,15},{15,17},{17,19},{19... | collective-permute-start | bytes 36872 | tf_op jit(solution)/shard_map/ppermute | solution.py:284
  52.7 0.1 pad_add_fusion.place_ref
  52.7 1.2 expand.1.wide_ref
  53.9 0.0 copy-start.4
  53.9 0.0 copy-start.6
  53.9 0.0 copy-start.2
  54.0 1.5 %collective-permute-done.4.end_ref = bf16[4,2,768]{2,1,0:T(2,128)(2,1)S(1)} collective-permute-done((bf16[4,2,768]{2,1,0:T(2,128)(2,1)S(1)}, bf16[4,2,768]{2,1,0:T(2,128)(2,1)S(1)}, u32[]{:S(2)}, u32[]{:S(2)}) %collective-permute-start.4) | collective-permute-done | bytes 12320 | tf_op jit(solution)/shard_map/ppermute | solution.py:284
  55.5 2.8 %conv.1 = bf16[8,96,128]{2,1,0:T(8,128)(2,1)} custom-call(s32[2]{0:T(128)S(1)} %pad_add_fusion.place_ref, bf16[4,64,768]{2,1,0:T(8,128)(2,1)S(1)} %activate.1.mine_ref, bf16[4,64,768]{2,1,0:T(8,128)(2,1)S(1)} %collective-permute-done.3.other_ref, bf16[4,2,768]{2,1,0:T(2,128)(2,1)S(1)} %collective-permute-done.4.end_ref, ...), custom_call_target="tpu_custom_call" | custom-call | tf_op jit(solution)/shard_map/conv/pallas_call | solution.py:294
  58.3 6.4 %all-to-all-start.2 = ((bf16[8,96,128]{2,1,0:T(8,128)(2,1)}), bf16[8,96,128]{2,1,0:T(8,128)(2,1)S(1)}, u32[]{:S(2)}, u32[]{:S(2)}) async-start(bf16[8,96,128]{2,1,0:T(8,128)(2,1)} %conv.1), calls=%async_computation.2 | async-start | bytes 393216 | tf_op jit(solution)/shard_map/all_to_all | solution.py:302
  64.7 0.2 copy.9.vw_ref
  64.9 4.1 %all-to-all-done.2.parts_ref = bf16[8,96,128]{2,1,0:T(8,128)(2,1)S(1)} async-done(((bf16[8,96,128]{2,1,0:T(8,128)(2,1)}), bf16[8,96,128]{2,1,0:T(8,128)(2,1)S(1)}, u32[]{:S(2)}, u32[]{:S(2)}) %all-to-all-start.2) | async-done | bytes 196640 | tf_op jit(solution)/shard_map/all_to_all | solution.py:302
  69.0 1.1 stream.1
  70.1 4.8 %all-to-all-start.3 = ((bf16[8,64,768]{2,1,0:T(8,128)(2,1)}), bf16[8,64,768]{2,1,0:T(8,128)(2,1)S(1)}, u32[]{:S(2)}, u32[]{:S(2)}) async-start(bf16[8,64,768]{2,1,0:T(8,128)(2,1)} %get-tuple-element.16), calls=%async_computation.3 | async-start | bytes 1572864 | tf_op jit(solution)/shard_map/all_to_all | solution.py:316
  74.9 33.1 %all-gather = bf16[2560,128]{1,0:T(8,128)(2,1)S(1)} all-gather(bf16[160,128]{1,0:T(8,128)(2,1)S(1)} %get-tuple-element.17), channel_id=2, replica_groups=mesh['xl'=2,'co'=2,'xh'=2,'y1'=2,'y0'=2,'zt'=8,'zp'=2] {'zt','zp'}, dimensions={0}, use_global_device_ids=true | all-gather | bytes 696320 | tf_op jit(solution)/shard_map/all_gather | solution.py:317
  108.0 6.1 %attend.1 = bf16[8,64,1664]{2,1,0:T(8,128)(2,1)S(1)} custom-call(bf16[8,64,768]{2,1,0:T(8,128)(2,1)S(1)} %all-to-all-done.3.x_ref, bf16[768,1024]{1,0:T(8,128)(2,1)S(1)} %copy-done, bf16[16,160,128]{2,1,0:T(8,128)(2,1)S(1)} %bitcast.5), custom_call_target="tpu_custom_call" | custom-call | tf_op jit(solution)/shard_map/attend/pallas_call | solution.py:318
  114.1 21.5 %all_to_all.25.parts_ref = bf16[8,64,1664]{2,1,0:T(8,128)(2,1)S(1)} all-to-all(bf16[8,64,1664]{2,1,0:T(8,128)(2,1)S(1)} %attend.1), channel_id=1, replica_groups=mesh['xl'=2,'co'=2,'xh'=2,'y1'=2,'y0'=2,'zt'=8,'zp'=2] {'xh','y1','y0'}, dimensions={0} | all-to-all | bytes 3407872 | tf_op jit(solution)/shard_map/all_to_all | solution.py:332
  135.6 1.6 %combine.1 = bf16[64,1536]{1,0:T(8,128)(2,1)} custom-call(bf16[8,64,1664]{2,1,0:T(8,128)(2,1)S(1)} %all_to_all.25.parts_ref), custom_call_target="tpu_custom_call" | custom-call | tf_op jit(solution)/shard_map/combine/pallas_call | solution.py:333
  (17 shorter events, 0.1 us)
Async XLA Ops:
  0.6 40.0 %copy-start.1 = (bf16[64,768]{1,0:T(8,128)(2,1)S(1)}, bf16[64,768]{1,0:T(8,128)(2,1)}, u32[]{:S(2)}) copy-start(bf16[64,768]{1,0:T(8,128)(2,1)} %mine_ref.1) | copy-start | bytes 294916
  0.6 0.8 copy-start.3
  1.5 39.2 %copy-start.5 = (f32[768]{0:T(1024)S(1)}, f32[768]{0:T(1024)}, u32[]{:S(2)}) copy-start(f32[768]{0:T(1024)} %param.8) | copy-start | bytes 9220
  2.2 30.0 %all-to-all-start = ((bf16[8,48,128]{2,1,0:T(8,128)(2,1)}), bf16[8,48,128]{2,1,0:T(8,128)(2,1)S(1)}, u32[]{:S(2)}, u32[]{:S(2)}) async-start(bf16[8,48,128]{2,1,0:T(8,128)(2,1)} %pack.1), calls=%async_computation | async-start | bytes 196608 | tf_op jit(solution)/shard_map/all_to_all | solution.py:263
  17.3 7.6 %collective-permute-start = (bf16[64,768]{1,0:T(8,128)(2,1)}, bf16[64,768]{1,0:T(8,128)(2,1)S(1)}, u32[]{:S(2)}, u32[]{:S(2)}) collective-permute-start(bf16[64,768]{1,0:T(8,128)(2,1)} %mine_ref.1), channel_id=1, source_target_pairs={{0,128},{128,0},{256,384},{384,256},{1,129},{129,1},{257,385},{385... | collective-permute-start | bytes 294920 | tf_op jit(solution)/shard_map/ppermute | solution.py:34
  19.2 7.3 %collective-permute-start.1 = (bf16[64,768]{1,0:T(8,128)(2,1)}, bf16[64,768]{1,0:T(8,128)(2,1)S(1)}, u32[]{:S(2)}, u32[]{:S(2)}) collective-permute-start(bf16[64,768]{1,0:T(8,128)(2,1)} %mine_ref.1), channel_id=1, source_target_pairs={{0,256},{128,384},{256,0},{384,128},{1,257},{129,385},{257,1},{385... | collective-permute-start | bytes 294920 | tf_op jit(solution)/shard_map/ppermute | solution.py:34
  22.0 6.9 %collective-permute-start.2 = (bf16[64,768]{1,0:T(8,128)(2,1)}, bf16[64,768]{1,0:T(8,128)(2,1)S(1)}, u32[]{:S(2)}, u32[]{:S(2)}) collective-permute-start(bf16[64,768]{1,0:T(8,128)(2,1)} %mine_ref.1), channel_id=1, source_target_pairs={{0,384},{128,256},{256,128},{384,0},{1,385},{129,257},{257,129},{3... | collective-permute-start | bytes 294920 | tf_op jit(solution)/shard_map/ppermute | solution.py:34
  33.2 19.5 %all-to-all-start.1 = ((bf16[8,8,48,128]{3,2,1,0:T(8,128)(2,1)}), bf16[8,8,48,128]{3,2,1,0:T(8,128)(2,1)S(1)}, u32[]{:S(2)}, u32[]{:S(2)}) async-start(bf16[8,8,48,128]{3,2,1,0:T(8,128)(2,1)} %broadcast_in_dim.13), calls=%async_computation.1 | async-start | bytes 1572864 | tf_op jit(solution)/shard_map/all_to_all | solution.py:24
  41.1 14.4 %collective-permute-start.3 = (bf16[4,64,768]{2,1,0:T(8,128)(2,1)S(1)}, bf16[4,64,768]{2,1,0:T(8,128)(2,1)S(1)}, u32[]{:S(2)}, u32[]{:S(2)}) collective-permute-start(bf16[4,64,768]{2,1,0:T(8,128)(2,1)S(1)} %activate.1.mine_ref), channel_id=1, source_target_pairs={{0,1},{1,0},{2,3},{3,2},{4,5},{5,4},{6,7},{7,6},{8,9},{9,8},{10,11... | collective-permute-start | bytes 1179656 | tf_op jit(solution)/shard_map/ppermute | solution.py:28
  44.2 11.3 %collective-permute-start.4 = (bf16[4,2,768]{2,1,0:T(2,128)(2,1)S(1)}, bf16[4,2,768]{2,1,0:T(2,128)(2,1)S(1)}, u32[]{:S(2)}, u32[]{:S(2)}) collective-permute-start(bf16[4,2,768]{2,1,0:T(2,128)(2,1)S(1)} %broadcast_select_fusion), channel_id=1, source_target_pairs={{1,2},{3,4},{5,6},{7,8},{9,10},{11,12},{13,14},{15,16},{17,18},{19... | collective-permute-start | bytes 36872 | tf_op jit(solution)/shard_map/ppermute | solution.py:284
  48.4 7.1 %collective-permute-start.5 = (bf16[4,2,768]{2,1,0:T(2,128)(2,1)S(1)}, bf16[4,2,768]{2,1,0:T(2,128)(2,1)S(1)}, u32[]{:S(2)}, u32[]{:S(2)}) collective-permute-start(bf16[4,2,768]{2,1,0:T(2,128)(2,1)S(1)} %broadcast_select_fusion), channel_id=1, source_target_pairs={{1,3},{3,5},{5,7},{7,9},{9,11},{11,13},{13,15},{15,17},{17,19},{19... | collective-permute-start | bytes 36872 | tf_op jit(solution)/shard_map/ppermute | solution.py:284
  53.9 10.8 %copy-start.4 = (bf16[768,192]{0,1:T(8,128)(2,1)S(1)}, bf16[768,192]{0,1:T(8,128)(2,1)}, u32[]{:S(2)}) copy-start(bf16[768,192]{0,1:T(8,128)(2,1)} %param.13) | copy-start | bytes 884740
  53.9 11.0 %copy-start.6 = (f32[768]{0:T(1024)S(1)}, f32[768]{0:T(1024)}, u32[]{:S(2)}) copy-start(f32[768]{0:T(1024)} %param.10) | copy-start | bytes 9220
  53.9 15.1 %copy-start.2 = (bf16[768,128]{1,0:T(8,128)(2,1)S(1)}, bf16[768,128]{1,0:T(8,128)(2,1)}, u32[]{:S(2)}) copy-start(bf16[768,128]{1,0:T(8,128)(2,1)} %kw_ref.1) | copy-start | bytes 589828
  58.3 10.7 %all-to-all-start.2 = ((bf16[8,96,128]{2,1,0:T(8,128)(2,1)}), bf16[8,96,128]{2,1,0:T(8,128)(2,1)S(1)}, u32[]{:S(2)}, u32[]{:S(2)}) async-start(bf16[8,96,128]{2,1,0:T(8,128)(2,1)} %conv.1), calls=%async_computation.2 | async-start | bytes 393216 | tf_op jit(solution)/shard_map/all_to_all | solution.py:302
  64.9 43.1 %copy-start = (bf16[768,1024]{1,0:T(8,128)(2,1)S(1)}, bf16[768,1024]{1,0:T(8,128)(2,1)}, u32[]{:S(2)}) copy-start(bf16[768,1024]{1,0:T(8,128)(2,1)} %qw_ref.1) | copy-start | bytes 4718596
  70.1 37.9 %all-to-all-start.3 = ((bf16[8,64,768]{2,1,0:T(8,128)(2,1)}), bf16[8,64,768]{2,1,0:T(8,128)(2,1)S(1)}, u32[]{:S(2)}, u32[]{:S(2)}) async-start(bf16[8,64,768]{2,1,0:T(8,128)(2,1)} %get-tuple-element.16), calls=%async_computation.3 | async-start | bytes 1572864 | tf_op jit(solution)/shard_map/all_to_all | solution.py:316

commit v6 on v5

--- a/solution.py
+++ b/solution.py
@@ -57,10 +57,9 @@
         out_ref[i] = out
 
 
-def activate_kernel(*refs):
-    x_refs, (gain_ref, out_ref) = refs[:4], refs[4:]
-    for i, ref in enumerate(x_refs):
-        values = normalize(ref[...].astype(jnp.float32), gain_ref[...])
+def activate_kernel(x_ref, gain_ref, out_ref):
+    for i in range(x_ref.shape[0]):
+        values = normalize(x_ref[i].astype(jnp.float32), gain_ref[...])
         out_ref[i] = jax.nn.gelu(values, approximate=True).astype(jnp.bfloat16)
 
 
@@ -85,7 +84,7 @@
 
 
 def conv_kernel(place_ref, mine_ref, other_ref, end_ref, far_end_ref, wide_ref, out_ref):
-    group, zp = place_ref[0], place_ref[1]
+    zp = place_ref[1]
     _, held, width = mine_ref.shape
     rows = 2 * held
     even = zp == 0
@@ -107,13 +106,12 @@
             sums[part] = term if offset == 0 else sums[part] + term
     lane = lax.broadcasted_iota(jnp.int32, (held // 2, 128), 1)
     for part in range(4):
-        index = jnp.bitwise_xor(group, part)
         rest = sums[part][:, 128:]
         turned = pltpu.roll(rest, 64, 1)
         for half in range(2):
             low, middle, high = half * held, half * held + held // 2, (half + 1) * held
             value = [sums[part][low:high, :128], jnp.where(lane < 64, rest[low:middle], turned[middle:high])]
-            out_ref[2 * index + half] = jnp.concatenate(value).astype(jnp.bfloat16)
+            out_ref[2 * part + half] = jnp.concatenate(value).astype(jnp.bfloat16)
 
 
 def stream_kernel(parts_ref, mine_ref, gain_ref, kw_ref, vw_ref, stream_ref, in_ref, pack_ref):
@@ -262,18 +260,18 @@
     )(conv_weight)
     blocks = lax.all_to_all(mine, "zt", 0, 0, tiled=True)
 
-    shared = by_masks(features, DP)
-    blocks, *shared = lax.optimization_barrier((blocks, *shared))
+    shared = lax.all_gather(features, DP, axis=0)
+    blocks, shared = lax.optimization_barrier((blocks, shared))
 
     blocks = everyone(blocks, SPREAD, 8).reshape(64, 48, 128)
     activated = pl.pallas_call(
         activate_kernel,
         out_shape=jax.ShapeDtypeStruct((4, rows, width), jnp.bfloat16),
-        in_specs=[in_vmem] * 5,
+        in_specs=[in_vmem] * 2,
         out_specs=in_vmem,
         compiler_params=params,
         name="activate",
-    )(*shared, conv_gain[None])
+    )(shared, conv_gain[None])
     edge = jnp.where(zp == 0, activated[:, :2], activated[:, rows - 2 :])
     odd, even = range(1, 128, 2), range(0, 128, 2)
     steps = [

time: 139 us -> 138 us (level)
  starting transfers between devices: 52.9 us -> 42.7 us
  blocking collectives: 54.6 us -> 58.9 us
  waiting for transfers between devices: 12.9 us -> 16.8 us
    ppermute x3 -> x0, starting transfers between devices: 7.58 us -> none  [by_masks(): lax.ppermute(block, axes, [(i, i ^ mask) for i in range(count)])]
    all_gather x0 -> x1, blocking collectives: none -> 6.35 us  [local(): shared = lax.all_gather(features, DP, axis=0)]
    all_to_all x1, waiting for transfers between devices: 3.37 us -> 8.58 us  [local(): blocks = lax.all_to_all(mine, 'zt', 0, 0, tiled=True)]
    ppermute x3 -> x0, waiting for transfers between devices: 3.94 us -> none  [by_masks(): lax.ppermute(block, axes, [(i, i ^ mask) for i in range(count)])]
    ppermute x2, starting transfers between devices: 8.46 us -> 5.82 us  [local(): end, far_end = (lax.ppermute(edge, SEQ, step) for step in steps)]
    ppermute x2, waiting for transfers between devices: 1.53 us -> 4.16 us  [local(): end, far_end = (lax.ppermute(edge, SEQ, step) for step in steps)]
    all_gather x1, blocking collectives: 33.1 us -> 30.6 us  [local(): pairs = lax.all_gather(packed, COLUMN, axis=0)]
  transfers between devices with their start and end apart: 10 -> 7, of which waited for: 5 -> 3; matrix products, arithmetic and copies ran while one was open for 0% -> 0% of each run, Pallas kernels for 1% -> 1%
where the time goes in v6:
time: 138 us; the launch traced here: 135 us
  blocking collectives  58.9 us (43%)
  starting transfers between devices  42.7 us (31%)
  waiting for transfers between devices  16.8 us (12%)
  Pallas kernels  13.9 us (10%)
  local copies, waits for them, and re-layouts  2 us (1%)
    all_gather x1, blocking collectives, local(): pairs = lax.all_gather(packed, COLUMN, axis=0)  30.6 us
    all_to_all x1, blocking collectives, local(): parts = lax.all_to_all(out, SPREAD, 0, 0, tiled=True)  21.9 us
    all_to_all x1, starting transfers between devices, local(): blocks = lax.all_to_all(mine, 'zt', 0, 0, tiled=True)  15.1 us
    all_to_all x1, waiting for transfers between devices, local(): blocks = lax.all_to_all(mine, 'zt', 0, 0, tiled=True)  8.58 us
    all_to_all x1, starting transfers between devices, everyone(): return lax.all_to_all(sent, axes, 0, 0, tiled=True)  7.43 us
    all_to_all x1, starting transfers between devices, local(): partial = lax.all_to_all(partial, SHARE, 0, 0, tiled=True)  6.44 us
    all_gather x1, blocking collectives, local(): shared = lax.all_gather(features, DP, axis=0)  6.35 us
    pallas_call x1, Pallas kernels, local(): pl.pallas_call(functools.partial(attend_kernel, heads, size), out_shape=j...  6.09 us
  transfers between devices with their start and end apart: 7, of which 3 were waited for; matrix products, arithmetic and copies ran while one was open for 0% of the time, Pallas kernels for 1%

profile of v6, /device:TPU:6, one launch (start us, length us, event | category | flops | bytes accessed | tf_op | source)
XLA Modules:
  0.0 135.1 jit_solution(12313721136886018545)
XLA Ops:
  0.6 0.8 copy-done.3
  1.4 0.7 pack.1
  2.2 15.1 %all-to-all-start = ((bf16[8,48,128]{2,1,0:T(8,128)(2,1)}), bf16[8,48,128]{2,1,0:T(8,128)(2,1)S(1)}, u32[]{:S(2)}, u32[]{:S(2)}) async-start(bf16[8,48,128]{2,1,0:T(8,128)(2,1)} %pack.1), calls=%async_computation | async-start | bytes 196608 | tf_op jit(solution)/shard_map/all_to_all | solution.py:261
  17.2 6.3 %all-gather = bf16[256,768]{1,0:T(8,128)(2,1)S(1)} all-gather(bf16[64,768]{1,0:T(8,128)(2,1)} %mine_ref.1), channel_id=2, replica_groups=mesh['xl'=2,'co'=2,'xh'=2,'y1'=2,'y0'=2,'zt'=8,'zp'=2] {'xl','co'}, dimensions={0}, use_global_device_ids=true | all-gather | bytes 491520 | tf_op jit(solution)/shard_map/all_gather | solution.py:263
  23.6 8.6 %all-to-all-done = bf16[8,48,128]{2,1,0:T(8,128)(2,1)S(1)} async-done(((bf16[8,48,128]{2,1,0:T(8,128)(2,1)}), bf16[8,48,128]{2,1,0:T(8,128)(2,1)S(1)}, u32[]{:S(2)}, u32[]{:S(2)}) %all-to-all-start) | async-done | bytes 98336 | tf_op jit(solution)/shard_map/all_to_all | solution.py:261
  32.2 1.0 broadcast_in_dim.13
  33.2 7.4 %all-to-all-start.1 = ((bf16[8,8,48,128]{3,2,1,0:T(8,128)(2,1)}), bf16[8,8,48,128]{3,2,1,0:T(8,128)(2,1)S(1)}, u32[]{:S(2)}, u32[]{:S(2)}) async-start(bf16[8,8,48,128]{3,2,1,0:T(8,128)(2,1)} %broadcast_in_dim.13), calls=%async_computation.1 | async-start | bytes 1572864 | tf_op jit(solution)/shard_map/all_to_all | solution.py:24
  40.6 0.4 activate.1.mine_ref
  41.0 3.1 %collective-permute-start = (bf16[4,64,768]{2,1,0:T(8,128)(2,1)S(1)}, bf16[4,64,768]{2,1,0:T(8,128)(2,1)S(1)}, u32[]{:S(2)}, u32[]{:S(2)}) collective-permute-start(bf16[4,64,768]{2,1,0:T(8,128)(2,1)S(1)} %activate.1.mine_ref), channel_id=1, source_target_pairs={{0,1},{1,0},{2,3},{3,2},{4,5},{5,4},{6,7},{7,6},{8,9},{9,8},{10,11... | collective-permute-start | bytes 1179656 | tf_op jit(solution)/shard_map/ppermute | solution.py:28
  44.1 3.9 %collective-permute-start.1 = (bf16[4,2,768]{2,1,0:T(2,128)(2,1)S(1)}, bf16[4,2,768]{2,1,0:T(2,128)(2,1)S(1)}, u32[]{:S(2)}, u32[]{:S(2)}) collective-permute-start(bf16[4,2,768]{2,1,0:T(2,128)(2,1)S(1)} %broadcast_select_fusion), channel_id=1, source_target_pairs={{1,2},{3,4},{5,6},{7,8},{9,10},{11,12},{13,14},{15,16},{17,18},{19... | collective-permute-start | bytes 36872 | tf_op jit(solution)/shard_map/ppermute | solution.py:282
  48.0 1.9 %collective-permute-start.2 = (bf16[4,2,768]{2,1,0:T(2,128)(2,1)S(1)}, bf16[4,2,768]{2,1,0:T(2,128)(2,1)S(1)}, u32[]{:S(2)}, u32[]{:S(2)}) collective-permute-start(bf16[4,2,768]{2,1,0:T(2,128)(2,1)S(1)} %broadcast_select_fusion), channel_id=1, source_target_pairs={{1,3},{3,5},{5,7},{7,9},{9,11},{11,13},{13,15},{15,17},{17,19},{19... | collective-permute-start | bytes 36872 | tf_op jit(solution)/shard_map/ppermute | solution.py:282
  50.0 0.1 pad_add_fusion.place_ref
  50.0 0.0 all-to-all-done.1
  50.1 1.2 expand.1.wide_ref
  51.2 0.0 copy-start.4
  51.3 0.0 copy-start.6
  51.3 0.0 copy-start.1
  51.3 0.0 copy-start.2
  51.3 4.2 %collective-permute-done.1.end_ref = bf16[4,2,768]{2,1,0:T(2,128)(2,1)S(1)} collective-permute-done((bf16[4,2,768]{2,1,0:T(2,128)(2,1)S(1)}, bf16[4,2,768]{2,1,0:T(2,128)(2,1)S(1)}, u32[]{:S(2)}, u32[]{:S(2)}) %collective-permute-start.1) | collective-permute-done | bytes 12320 | tf_op jit(solution)/shard_map/ppermute | solution.py:282
  55.4 0.0 collective-permute-done.2.far_end_ref
  55.4 0.0 collective-permute-done.other_ref
  55.5 2.8 %conv.1 = bf16[8,96,128]{2,1,0:T(8,128)(2,1)} custom-call(s32[2]{0:T(128)S(1)} %pad_add_fusion.place_ref, bf16[4,64,768]{2,1,0:T(8,128)(2,1)S(1)} %activate.1.mine_ref, bf16[4,64,768]{2,1,0:T(8,128)(2,1)S(1)} %collective-permute-done.other_ref, bf16[4,2,768]{2,1,0:T(2,128)(2,1)S(1)} %collective-permute-done.1.end_ref, ...), custom_call_target="tpu_custom_call" | custom-call | tf_op jit(solution)/shard_map/conv/pallas_call | solution.py:292
  58.2 6.4 %all-to-all-start.2 = ((bf16[8,96,128]{2,1,0:T(8,128)(2,1)}), bf16[8,96,128]{2,1,0:T(8,128)(2,1)S(1)}, u32[]{:S(2)}, u32[]{:S(2)}) async-start(bf16[8,96,128]{2,1,0:T(8,128)(2,1)} %conv.1), calls=%async_computation.2 | async-start | bytes 393216 | tf_op jit(solution)/shard_map/all_to_all | solution.py:300
  64.7 0.2 copy.9.vw_ref
  64.9 0.0 copy-start
  64.9 4.1 %all-to-all-done.2.parts_ref = bf16[8,96,128]{2,1,0:T(8,128)(2,1)S(1)} async-done(((bf16[8,96,128]{2,1,0:T(8,128)(2,1)}), bf16[8,96,128]{2,1,0:T(8,128)(2,1)S(1)}, u32[]{:S(2)}, u32[]{:S(2)}) %all-to-all-start.2) | async-done | bytes 196640 | tf_op jit(solution)/shard_map/all_to_all | solution.py:300
  69.0 1.1 stream.1
  70.1 4.8 %all-to-all-start.3 = ((bf16[8,64,768]{2,1,0:T(8,128)(2,1)}), bf16[8,64,768]{2,1,0:T(8,128)(2,1)S(1)}, u32[]{:S(2)}, u32[]{:S(2)}) async-start(bf16[8,64,768]{2,1,0:T(8,128)(2,1)} %get-tuple-element.10), calls=%async_computation.3 | async-start | bytes 1572864 | tf_op jit(solution)/shard_map/all_to_all | solution.py:314
  74.9 30.6 %all-gather.1 = bf16[2560,128]{1,0:T(8,128)(2,1)S(1)} all-gather(bf16[160,128]{1,0:T(8,128)(2,1)S(1)} %get-tuple-element.11), channel_id=3, replica_groups=mesh['xl'=2,'co'=2,'xh'=2,'y1'=2,'y0'=2,'zt'=8,'zp'=2] {'zt','zp'}, dimensions={0}, use_global_device_ids=true | all-gather | bytes 696320 | tf_op jit(solution)/shard_map/all_gather | solution.py:315
  105.5 6.1 %attend.1 = bf16[8,64,1664]{2,1,0:T(8,128)(2,1)S(1)} custom-call(bf16[8,64,768]{2,1,0:T(8,128)(2,1)S(1)} %all-to-all-done.3.x_ref, bf16[768,1024]{1,0:T(8,128)(2,1)S(1)} %copy-done, bf16[16,160,128]{2,1,0:T(8,128)(2,1)S(1)} %bitcast.6), custom_call_target="tpu_custom_call" | custom-call | tf_op jit(solution)/shard_map/attend/pallas_call | solution.py:316
  111.6 21.9 %all_to_all.25.parts_ref = bf16[8,64,1664]{2,1,0:T(8,128)(2,1)S(1)} all-to-all(bf16[8,64,1664]{2,1,0:T(8,128)(2,1)S(1)} %attend.1), channel_id=1, replica_groups=mesh['xl'=2,'co'=2,'xh'=2,'y1'=2,'y0'=2,'zt'=8,'zp'=2] {'xh','y1','y0'}, dimensions={0} | all-to-all | bytes 3407872 | tf_op jit(solution)/shard_map/all_to_all | solution.py:330
  133.5 1.6 %combine.1 = bf16[64,1536]{1,0:T(8,128)(2,1)} custom-call(bf16[8,64,1664]{2,1,0:T(8,128)(2,1)S(1)} %all_to_all.25.parts_ref), custom_call_target="tpu_custom_call" | custom-call | tf_op jit(solution)/shard_map/combine/pallas_call | solution.py:331
  (12 shorter events, 0.1 us)
Async XLA Ops:
  0.6 0.8 copy-start.3
  1.4 39.2 %copy-start.5 = (f32[768]{0:T(1024)S(1)}, f32[768]{0:T(1024)}, u32[]{:S(2)}) copy-start(f32[768]{0:T(1024)} %param.8) | copy-start | bytes 9220
  2.2 30.0 %all-to-all-start = ((bf16[8,48,128]{2,1,0:T(8,128)(2,1)}), bf16[8,48,128]{2,1,0:T(8,128)(2,1)S(1)}, u32[]{:S(2)}, u32[]{:S(2)}) async-start(bf16[8,48,128]{2,1,0:T(8,128)(2,1)} %pack.1), calls=%async_computation | async-start | bytes 196608 | tf_op jit(solution)/shard_map/all_to_all | solution.py:261
  33.2 16.9 %all-to-all-start.1 = ((bf16[8,8,48,128]{3,2,1,0:T(8,128)(2,1)}), bf16[8,8,48,128]{3,2,1,0:T(8,128)(2,1)S(1)}, u32[]{:S(2)}, u32[]{:S(2)}) async-start(bf16[8,8,48,128]{3,2,1,0:T(8,128)(2,1)} %broadcast_in_dim.13), calls=%async_computation.1 | async-start | bytes 1572864 | tf_op jit(solution)/shard_map/all_to_all | solution.py:24
  41.0 14.4 %collective-permute-start = (bf16[4,64,768]{2,1,0:T(8,128)(2,1)S(1)}, bf16[4,64,768]{2,1,0:T(8,128)(2,1)S(1)}, u32[]{:S(2)}, u32[]{:S(2)}) collective-permute-start(bf16[4,64,768]{2,1,0:T(8,128)(2,1)S(1)} %activate.1.mine_ref), channel_id=1, source_target_pairs={{0,1},{1,0},{2,3},{3,2},{4,5},{5,4},{6,7},{7,6},{8,9},{9,8},{10,11... | collective-permute-start | bytes 1179656 | tf_op jit(solution)/shard_map/ppermute | solution.py:28
  44.1 11.3 %collective-permute-start.1 = (bf16[4,2,768]{2,1,0:T(2,128)(2,1)S(1)}, bf16[4,2,768]{2,1,0:T(2,128)(2,1)S(1)}, u32[]{:S(2)}, u32[]{:S(2)}) collective-permute-start(bf16[4,2,768]{2,1,0:T(2,128)(2,1)S(1)} %broadcast_select_fusion), channel_id=1, source_target_pairs={{1,2},{3,4},{5,6},{7,8},{9,10},{11,12},{13,14},{15,16},{17,18},{19... | collective-permute-start | bytes 36872 | tf_op jit(solution)/shard_map/ppermute | solution.py:282
  48.0 7.4 %collective-permute-start.2 = (bf16[4,2,768]{2,1,0:T(2,128)(2,1)S(1)}, bf16[4,2,768]{2,1,0:T(2,128)(2,1)S(1)}, u32[]{:S(2)}, u32[]{:S(2)}) collective-permute-start(bf16[4,2,768]{2,1,0:T(2,128)(2,1)S(1)} %broadcast_select_fusion), channel_id=1, source_target_pairs={{1,3},{3,5},{5,7},{7,9},{9,11},{11,13},{13,15},{15,17},{17,19},{19... | collective-permute-start | bytes 36872 | tf_op jit(solution)/shard_map/ppermute | solution.py:282
  51.2 13.4 %copy-start.4 = (bf16[768,192]{0,1:T(8,128)(2,1)S(1)}, bf16[768,192]{0,1:T(8,128)(2,1)}, u32[]{:S(2)}) copy-start(bf16[768,192]{0,1:T(8,128)(2,1)} %param.13) | copy-start | bytes 884740
  51.3 13.6 %copy-start.6 = (f32[768]{0:T(1024)S(1)}, f32[768]{0:T(1024)}, u32[]{:S(2)}) copy-start(f32[768]{0:T(1024)} %param.10) | copy-start | bytes 9220
  51.3 17.7 %copy-start.1 = (bf16[64,768]{1,0:T(8,128)(2,1)S(1)}, bf16[64,768]{1,0:T(8,128)(2,1)}, u32[]{:S(2)}) copy-start(bf16[64,768]{1,0:T(8,128)(2,1)} %mine_ref.1) | copy-start | bytes 294916
  51.3 17.7 %copy-start.2 = (bf16[768,128]{1,0:T(8,128)(2,1)S(1)}, bf16[768,128]{1,0:T(8,128)(2,1)}, u32[]{:S(2)}) copy-start(bf16[768,128]{1,0:T(8,128)(2,1)} %kw_ref.1) | copy-start | bytes 589828
  58.2 10.7 %all-to-all-start.2 = ((bf16[8,96,128]{2,1,0:T(8,128)(2,1)}), bf16[8,96,128]{2,1,0:T(8,128)(2,1)S(1)}, u32[]{:S(2)}, u32[]{:S(2)}) async-start(bf16[8,96,128]{2,1,0:T(8,128)(2,1)} %conv.1), calls=%async_computation.2 | async-start | bytes 393216 | tf_op jit(solution)/shard_map/all_to_all | solution.py:300
  64.9 40.7 %copy-start = (bf16[768,1024]{1,0:T(8,128)(2,1)S(1)}, bf16[768,1024]{1,0:T(8,128)(2,1)}, u32[]{:S(2)}) copy-start(bf16[768,1024]{1,0:T(8,128)(2,1)} %qw_ref.1) | copy-start | bytes 4718596
  70.1 35.4 %all-to-all-start.3 = ((bf16[8,64,768]{2,1,0:T(8,128)(2,1)}), bf16[8,64,768]{2,1,0:T(8,128)(2,1)S(1)}, u32[]{:S(2)}, u32[]{:S(2)}) async-start(bf16[8,64,768]{2,1,0:T(8,128)(2,1)} %get-tuple-element.10), calls=%async_computation.3 | async-start | bytes 1572864 | tf_op jit(solution)/shard_map/all_to_all | solution.py:314

commit v7 on v6

--- a/solution.py
+++ b/solution.py
@@ -63,11 +63,11 @@
         out_ref[i] = jax.nn.gelu(values, approximate=True).astype(jnp.bfloat16)
 
 
-def expand_kernel(place_ref, w_ref, out_ref, wide_ref):
+def expand_kernel(place_ref, w_ref, out_ref):
     zp = place_ref[1]
     count = w_ref.shape[0]
     depth = out_ref.shape[0] // (2 * count)
-    wide_ref[...] = jnp.zeros_like(wide_ref)
+    out_ref[...] = jnp.zeros_like(out_ref)
     for side in range(2):
 
         @pl.when(zp == side)
@@ -76,21 +76,19 @@
                 start = (2 * i + side) * depth
                 block = w_ref[i].astype(jnp.float32)
                 tail = block[32:48]
-                wide_ref[start : start + depth, :128] = block[:depth]
-                wide_ref[start : start + depth // 2, 128:] = tail[: depth // 2]
-                wide_ref[start + depth // 2 : start + depth, 128:] = pltpu.roll(tail, 64, 1)[: depth // 2]
-
-    out_ref[...] = wide_ref[...].astype(jnp.bfloat16)
-
-
-def conv_kernel(place_ref, mine_ref, other_ref, end_ref, far_end_ref, wide_ref, out_ref):
+                rest = jnp.concatenate([tail[: depth // 2], pltpu.roll(tail, 64, 1)[: depth // 2]])
+                out_ref[start : start + depth, :128] = block[:depth].astype(jnp.bfloat16)
+                out_ref[start : start + depth, 128:] = rest.astype(jnp.bfloat16)
+
+
+def conv_kernel(place_ref, mine_ref, other_ref, end_ref, far_end_ref, wide_ref, out_ref, x_ref):
     zp = place_ref[1]
     _, held, width = mine_ref.shape
     rows = 2 * held
     even = zp == 0
-    mine, other = mine_ref[...], other_ref[...]
-    first, second = jnp.where(even, mine, other), jnp.where(even, other, mine)
-    x = jnp.concatenate([first, second], axis=1).reshape(4 * rows, width)
+    x_ref[:, pl.ds(pl.multiple_of(zp * held, held), held), :] = mine_ref[...]
+    x_ref[:, pl.ds(pl.multiple_of((1 - zp) * held, held), held), :] = other_ref[...]
+    x = x_ref[...].reshape(4 * rows, width)
     end, far_end = end_ref[...].astype(jnp.float32), far_end_ref[...].astype(jnp.float32)
     before, after = jnp.where(even, end, far_end), jnp.where(even, far_end, end)
     ends = jnp.concatenate([before.reshape(8, width), after.reshape(8, width)]).astype(jnp.bfloat16)
@@ -261,9 +259,7 @@
     blocks = lax.all_to_all(mine, "zt", 0, 0, tiled=True)
 
     shared = lax.all_gather(features, DP, axis=0)
-    blocks, shared = lax.optimization_barrier((blocks, shared))
-
-    blocks = everyone(blocks, SPREAD, 8).reshape(64, 48, 128)
+
     activated = pl.pallas_call(
         activate_kernel,
         out_shape=jax.ShapeDtypeStruct((4, rows, width), jnp.bfloat16),
@@ -272,20 +268,21 @@
         compiler_params=params,
         name="activate",
     )(shared, conv_gain[None])
+    blocks, activated = lax.optimization_barrier((blocks, activated))
+    blocks = everyone(blocks, SPREAD, 8).reshape(64, 48, 128)
     edge = jnp.where(zp == 0, activated[:, :2], activated[:, rows - 2 :])
     odd, even = range(1, 128, 2), range(0, 128, 2)
     steps = [
         [(i, i + step) for i in odd if i + step < 128] + [(i, i - step) for i in even if i - step >= 0]
-        for step in (1, 2)
+        for step in (2, 1)
     ]
     other = swapped(activated, "zp")
-    end, far_end = (lax.ppermute(edge, SEQ, step) for step in steps)
+    far_end, end = (lax.ppermute(edge, SEQ, step) for step in steps)
     wide = pl.pallas_call(
         expand_kernel,
         out_shape=jax.ShapeDtypeStruct((KW * width, 256), jnp.bfloat16),
         in_specs=[in_smem, in_vmem],
         out_specs=in_vmem,
-        scratch_shapes=[pltpu.VMEM((KW * width, 256), jnp.float32)],
         compiler_params=params,
         name="expand",
     )(place, blocks)
@@ -294,6 +291,7 @@
         out_shape=jax.ShapeDtypeStruct((8, 3 * rows // 2, 128), jnp.bfloat16),
         in_specs=[in_smem] + [in_vmem] * 5,
         out_specs=in_vmem,
+        scratch_shapes=[pltpu.VMEM((4, 2 * rows, width), jnp.bfloat16)],
         compiler_params=params,
         name="conv",
     )(place, activated, other, end, far_end, wide)

time: 138 us -> 137 us (level)
  transfers between devices with their start and end apart: 7 -> 7, of which waited for: 3 -> 3; matrix products, arithmetic and copies ran while one was open for 0% -> 1% of each run, Pallas kernels for 1% -> 1%
where the time goes in v7:
time: 137 us; the launch traced here: 135 us
  blocking collectives  58.9 us (43%)
  starting transfers between devices  42.6 us (31%)
  waiting for transfers between devices  15.9 us (12%)
  Pallas kernels  13.7 us (10%)
  local copies, waits for them, and re-layouts  2.68 us (2%)
    all_gather x1, blocking collectives, local(): pairs = lax.all_gather(packed, COLUMN, axis=0)  30.6 us
    all_to_all x1, blocking collectives, local(): parts = lax.all_to_all(out, SPREAD, 0, 0, tiled=True)  21.9 us
    all_to_all x1, starting transfers between devices, local(): blocks = lax.all_to_all(mine, 'zt', 0, 0, tiled=True)  15.1 us
    all_to_all x1, waiting for transfers between devices, local(): blocks = lax.all_to_all(mine, 'zt', 0, 0, tiled=True)  7.48 us
    all_to_all x1, starting transfers between devices, everyone(): return lax.all_to_all(sent, axes, 0, 0, tiled=True)  7.43 us
    all_to_all x1, starting transfers between devices, local(): partial = lax.all_to_all(partial, SHARE, 0, 0, tiled=True)  6.44 us
    all_gather x1, blocking collectives, local(): shared = lax.all_gather(features, DP, axis=0)  6.35 us
    pallas_call x1, Pallas kernels, local(): pl.pallas_call(functools.partial(attend_kernel, heads, size), out_shape=j...  6.09 us
  transfers between devices with their start and end apart: 7, of which 3 were waited for; matrix products, arithmetic and copies ran while one was open for 1% of the time, Pallas kernels for 1%

profile of v7, /device:TPU:6, one launch (start us, length us, event | category | flops | bytes accessed | tf_op | source)
XLA Modules:
  0.0 134.7 jit_solution(982543988434625512)
XLA Ops:
  0.6 0.8 copy-done.3
  1.4 0.7 pack.1
  2.2 15.1 %all-to-all-start = ((bf16[8,48,128]{2,1,0:T(8,128)(2,1)}), bf16[8,48,128]{2,1,0:T(8,128)(2,1)S(1)}, u32[]{:S(2)}, u32[]{:S(2)}) async-start(bf16[8,48,128]{2,1,0:T(8,128)(2,1)} %pack.1), calls=%async_computation | async-start | bytes 196608 | tf_op jit(solution)/shard_map/all_to_all | solution.py:259
  17.2 0.7 broadcast_in_dim.12.gain_ref
  17.9 6.3 %all-gather = bf16[256,768]{1,0:T(8,128)(2,1)S(1)} all-gather(bf16[64,768]{1,0:T(8,128)(2,1)} %mine_ref.1), channel_id=2, replica_groups=mesh['xl'=2,'co'=2,'xh'=2,'y1'=2,'y0'=2,'zt'=8,'zp'=2] {'xl','co'}, dimensions={0}, use_global_device_ids=true | all-gather | bytes 491520 | tf_op jit(solution)/shard_map/all_gather | solution.py:261
  24.3 0.4 activate.1.mine_ref
  24.7 7.5 %all-to-all-done = bf16[8,48,128]{2,1,0:T(8,128)(2,1)S(1)} async-done(((bf16[8,48,128]{2,1,0:T(8,128)(2,1)}), bf16[8,48,128]{2,1,0:T(8,128)(2,1)S(1)}, u32[]{:S(2)}, u32[]{:S(2)}) %all-to-all-start) | async-done | bytes 98336 | tf_op jit(solution)/shard_map/all_to_all | solution.py:259
  32.2 1.0 broadcast_in_dim.13
  33.2 7.4 %all-to-all-start.1 = ((bf16[8,8,48,128]{3,2,1,0:T(8,128)(2,1)}), bf16[8,8,48,128]{3,2,1,0:T(8,128)(2,1)S(1)}, u32[]{:S(2)}, u32[]{:S(2)}) async-start(bf16[8,8,48,128]{3,2,1,0:T(8,128)(2,1)} %broadcast_in_dim.13), calls=%async_computation.1 | async-start | bytes 1572864 | tf_op jit(solution)/shard_map/all_to_all | solution.py:24
  40.6 3.1 %collective-permute-start = (bf16[4,64,768]{2,1,0:T(8,128)(2,1)S(1)}, bf16[4,64,768]{2,1,0:T(8,128)(2,1)S(1)}, u32[]{:S(2)}, u32[]{:S(2)}) collective-permute-start(bf16[4,64,768]{2,1,0:T(8,128)(2,1)S(1)} %activate.1.mine_ref), channel_id=1, source_target_pairs={{0,1},{1,0},{2,3},{3,2},{4,5},{5,4},{6,7},{7,6},{8,9},{9,8},{10,11... | collective-permute-start | bytes 1179656 | tf_op jit(solution)/shard_map/ppermute | solution.py:28
  43.7 3.9 %collective-permute-start.1 = (bf16[4,2,768]{2,1,0:T(2,128)(2,1)S(1)}, bf16[4,2,768]{2,1,0:T(2,128)(2,1)S(1)}, u32[]{:S(2)}, u32[]{:S(2)}) collective-permute-start(bf16[4,2,768]{2,1,0:T(2,128)(2,1)S(1)} %broadcast_select_fusion), channel_id=1, source_target_pairs={{1,2},{3,4},{5,6},{7,8},{9,10},{11,12},{13,14},{15,16},{17,18},{19... | collective-permute-start | bytes 36872 | tf_op jit(solution)/shard_map/ppermute | solution.py:280
  47.6 1.9 %collective-permute-start.2 = (bf16[4,2,768]{2,1,0:T(2,128)(2,1)S(1)}, bf16[4,2,768]{2,1,0:T(2,128)(2,1)S(1)}, u32[]{:S(2)}, u32[]{:S(2)}) collective-permute-start(bf16[4,2,768]{2,1,0:T(2,128)(2,1)S(1)} %broadcast_select_fusion), channel_id=1, source_target_pairs={{1,3},{3,5},{5,7},{7,9},{9,11},{11,13},{13,15},{15,17},{17,19},{19... | collective-permute-start | bytes 36872 | tf_op jit(solution)/shard_map/ppermute | solution.py:280
  49.5 0.1 pad_add_fusion.place_ref
  49.6 0.0 all-to-all-done.1
  49.6 1.0 expand.1.wide_ref
  50.6 0.0 copy-start.4
  50.6 0.0 copy-start.5
  50.6 0.0 copy-start.1
  50.6 0.0 copy-start.2
  50.6 4.4 %collective-permute-done.1.end_ref = bf16[4,2,768]{2,1,0:T(2,128)(2,1)S(1)} collective-permute-done((bf16[4,2,768]{2,1,0:T(2,128)(2,1)S(1)}, bf16[4,2,768]{2,1,0:T(2,128)(2,1)S(1)}, u32[]{:S(2)}, u32[]{:S(2)}) %collective-permute-start.1) | collective-permute-done | bytes 12320 | tf_op jit(solution)/shard_map/ppermute | solution.py:280
  55.0 0.0 collective-permute-done.2.far_end_ref
  55.0 2.8 %conv.1 = bf16[8,96,128]{2,1,0:T(8,128)(2,1)} custom-call(s32[2]{0:T(128)S(1)} %pad_add_fusion.place_ref, bf16[4,64,768]{2,1,0:T(8,128)(2,1)S(1)} %activate.1.mine_ref, bf16[4,64,768]{2,1,0:T(8,128)(2,1)S(1)} %collective-permute-done.other_ref, bf16[4,2,768]{2,1,0:T(2,128)(2,1)S(1)} %collective-permute-done.1.end_ref, ...), custom_call_target="tpu_custom_call" | custom-call | tf_op jit(solution)/shard_map/conv/pallas_call | solution.py:289
  57.8 6.4 %all-to-all-start.2 = ((bf16[8,96,128]{2,1,0:T(8,128)(2,1)}), bf16[8,96,128]{2,1,0:T(8,128)(2,1)S(1)}, u32[]{:S(2)}, u32[]{:S(2)}) async-start(bf16[8,96,128]{2,1,0:T(8,128)(2,1)} %conv.1), calls=%async_computation.2 | async-start | bytes 393216 | tf_op jit(solution)/shard_map/all_to_all | solution.py:298
  64.3 0.2 copy.9.vw_ref
  64.5 0.0 copy-start
  64.5 4.1 %all-to-all-done.2.parts_ref = bf16[8,96,128]{2,1,0:T(8,128)(2,1)S(1)} async-done(((bf16[8,96,128]{2,1,0:T(8,128)(2,1)}), bf16[8,96,128]{2,1,0:T(8,128)(2,1)S(1)}, u32[]{:S(2)}, u32[]{:S(2)}) %all-to-all-start.2) | async-done | bytes 196640 | tf_op jit(solution)/shard_map/all_to_all | solution.py:298
  68.6 1.1 stream.1
  69.7 4.8 %all-to-all-start.3 = ((bf16[8,64,768]{2,1,0:T(8,128)(2,1)}), bf16[8,64,768]{2,1,0:T(8,128)(2,1)S(1)}, u32[]{:S(2)}, u32[]{:S(2)}) async-start(bf16[8,64,768]{2,1,0:T(8,128)(2,1)} %get-tuple-element.10), calls=%async_computation.3 | async-start | bytes 1572864 | tf_op jit(solution)/shard_map/all_to_all | solution.py:312
  74.5 30.6 %all-gather.1 = bf16[2560,128]{1,0:T(8,128)(2,1)S(1)} all-gather(bf16[160,128]{1,0:T(8,128)(2,1)S(1)} %get-tuple-element.11), channel_id=3, replica_groups=mesh['xl'=2,'co'=2,'xh'=2,'y1'=2,'y0'=2,'zt'=8,'zp'=2] {'zt','zp'}, dimensions={0}, use_global_device_ids=true | all-gather | bytes 696320 | tf_op jit(solution)/shard_map/all_gather | solution.py:313
  105.1 6.1 %attend.1 = bf16[8,64,1664]{2,1,0:T(8,128)(2,1)S(1)} custom-call(bf16[8,64,768]{2,1,0:T(8,128)(2,1)S(1)} %all-to-all-done.3.x_ref, bf16[768,1024]{1,0:T(8,128)(2,1)S(1)} %copy-done, bf16[16,160,128]{2,1,0:T(8,128)(2,1)S(1)} %bitcast.6), custom_call_target="tpu_custom_call" | custom-call | tf_op jit(solution)/shard_map/attend/pallas_call | solution.py:314
  111.2 21.9 %all_to_all.25.parts_ref = bf16[8,64,1664]{2,1,0:T(8,128)(2,1)S(1)} all-to-all(bf16[8,64,1664]{2,1,0:T(8,128)(2,1)S(1)} %attend.1), channel_id=1, replica_groups=mesh['xl'=2,'co'=2,'xh'=2,'y1'=2,'y0'=2,'zt'=8,'zp'=2] {'xh','y1','y0'}, dimensions={0} | all-to-all | bytes 3407872 | tf_op jit(solution)/shard_map/all_to_all | solution.py:328
  133.1 1.6 %combine.1 = bf16[64,1536]{1,0:T(8,128)(2,1)} custom-call(bf16[8,64,1664]{2,1,0:T(8,128)(2,1)S(1)} %all_to_all.25.parts_ref), custom_call_target="tpu_custom_call" | custom-call | tf_op jit(solution)/shard_map/combine/pallas_call | solution.py:329
  (10 shorter events, 0.0 us)
Async XLA Ops:
  0.6 0.8 copy-start.3
  2.2 30.0 %all-to-all-start = ((bf16[8,48,128]{2,1,0:T(8,128)(2,1)}), bf16[8,48,128]{2,1,0:T(8,128)(2,1)S(1)}, u32[]{:S(2)}, u32[]{:S(2)}) async-start(bf16[8,48,128]{2,1,0:T(8,128)(2,1)} %pack.1), calls=%async_computation | async-start | bytes 196608 | tf_op jit(solution)/shard_map/all_to_all | solution.py:259
  33.2 16.5 %all-to-all-start.1 = ((bf16[8,8,48,128]{3,2,1,0:T(8,128)(2,1)}), bf16[8,8,48,128]{3,2,1,0:T(8,128)(2,1)S(1)}, u32[]{:S(2)}, u32[]{:S(2)}) async-start(bf16[8,8,48,128]{3,2,1,0:T(8,128)(2,1)} %broadcast_in_dim.13), calls=%async_computation.1 | async-start | bytes 1572864 | tf_op jit(solution)/shard_map/all_to_all | solution.py:24
  40.6 14.4 %collective-permute-start = (bf16[4,64,768]{2,1,0:T(8,128)(2,1)S(1)}, bf16[4,64,768]{2,1,0:T(8,128)(2,1)S(1)}, u32[]{:S(2)}, u32[]{:S(2)}) collective-permute-start(bf16[4,64,768]{2,1,0:T(8,128)(2,1)S(1)} %activate.1.mine_ref), channel_id=1, source_target_pairs={{0,1},{1,0},{2,3},{3,2},{4,5},{5,4},{6,7},{7,6},{8,9},{9,8},{10,11... | collective-permute-start | bytes 1179656 | tf_op jit(solution)/shard_map/ppermute | solution.py:28
  43.7 11.3 %collective-permute-start.1 = (bf16[4,2,768]{2,1,0:T(2,128)(2,1)S(1)}, bf16[4,2,768]{2,1,0:T(2,128)(2,1)S(1)}, u32[]{:S(2)}, u32[]{:S(2)}) collective-permute-start(bf16[4,2,768]{2,1,0:T(2,128)(2,1)S(1)} %broadcast_select_fusion), channel_id=1, source_target_pairs={{1,2},{3,4},{5,6},{7,8},{9,10},{11,12},{13,14},{15,16},{17,18},{19... | collective-permute-start | bytes 36872 | tf_op jit(solution)/shard_map/ppermute | solution.py:280
  47.6 7.4 %collective-permute-start.2 = (bf16[4,2,768]{2,1,0:T(2,128)(2,1)S(1)}, bf16[4,2,768]{2,1,0:T(2,128)(2,1)S(1)}, u32[]{:S(2)}, u32[]{:S(2)}) collective-permute-start(bf16[4,2,768]{2,1,0:T(2,128)(2,1)S(1)} %broadcast_select_fusion), channel_id=1, source_target_pairs={{1,3},{3,5},{5,7},{7,9},{9,11},{11,13},{13,15},{15,17},{17,19},{19... | collective-permute-start | bytes 36872 | tf_op jit(solution)/shard_map/ppermute | solution.py:280
  50.6 13.7 %copy-start.4 = (bf16[768,192]{0,1:T(8,128)(2,1)S(1)}, bf16[768,192]{0,1:T(8,128)(2,1)}, u32[]{:S(2)}) copy-start(bf16[768,192]{0,1:T(8,128)(2,1)} %param.13) | copy-start | bytes 884740
  50.6 13.8 %copy-start.5 = (f32[768]{0:T(1024)S(1)}, f32[768]{0:T(1024)}, u32[]{:S(2)}) copy-start(f32[768]{0:T(1024)} %param.10) | copy-start | bytes 9220
  50.6 17.9 %copy-start.1 = (bf16[64,768]{1,0:T(8,128)(2,1)S(1)}, bf16[64,768]{1,0:T(8,128)(2,1)}, u32[]{:S(2)}) copy-start(bf16[64,768]{1,0:T(8,128)(2,1)} %mine_ref.1) | copy-start | bytes 294916
  50.6 17.9 %copy-start.2 = (bf16[768,128]{1,0:T(8,128)(2,1)S(1)}, bf16[768,128]{1,0:T(8,128)(2,1)}, u32[]{:S(2)}) copy-start(bf16[768,128]{1,0:T(8,128)(2,1)} %kw_ref.1) | copy-start | bytes 589828
  57.8 10.7 %all-to-all-start.2 = ((bf16[8,96,128]{2,1,0:T(8,128)(2,1)}), bf16[8,96,128]{2,1,0:T(8,128)(2,1)S(1)}, u32[]{:S(2)}, u32[]{:S(2)}) async-start(bf16[8,96,128]{2,1,0:T(8,128)(2,1)} %conv.1), calls=%async_computation.2 | async-start | bytes 393216 | tf_op jit(solution)/shard_map/all_to_all | solution.py:298
  64.5 40.7 %copy-start = (bf16[768,1024]{1,0:T(8,128)(2,1)S(1)}, bf16[768,1024]{1,0:T(8,128)(2,1)}, u32[]{:S(2)}) copy-start(bf16[768,1024]{1,0:T(8,128)(2,1)} %qw_ref.1) | copy-start | bytes 4718596
  69.7 35.4 %all-to-all-start.3 = ((bf16[8,64,768]{2,1,0:T(8,128)(2,1)}), bf16[8,64,768]{2,1,0:T(8,128)(2,1)S(1)}, u32[]{:S(2)}, u32[]{:S(2)}) async-start(bf16[8,64,768]{2,1,0:T(8,128)(2,1)} %get-tuple-element.10), calls=%async_computation.3 | async-start | bytes 1572864 | tf_op jit(solution)/shard_map/all_to_all | solution.py:312

commit v8 on v7

--- a/solution.py
+++ b/solution.py
@@ -86,17 +86,19 @@
     _, held, width = mine_ref.shape
     rows = 2 * held
     even = zp == 0
-    x_ref[:, pl.ds(pl.multiple_of(zp * held, held), held), :] = mine_ref[...]
-    x_ref[:, pl.ds(pl.multiple_of((1 - zp) * held, held), held), :] = other_ref[...]
-    x = x_ref[...].reshape(4 * rows, width)
+    for part in range(4):
+        x_ref[pl.ds(pl.multiple_of(part * rows + zp * held, held), held), :] = mine_ref[part]
+        x_ref[pl.ds(pl.multiple_of(part * rows + (1 - zp) * held, held), held), :] = other_ref[part]
     end, far_end = end_ref[...].astype(jnp.float32), far_end_ref[...].astype(jnp.float32)
     before, after = jnp.where(even, end, far_end), jnp.where(even, far_end, end)
     ends = jnp.concatenate([before.reshape(8, width), after.reshape(8, width)]).astype(jnp.bfloat16)
+    x_ref[4 * rows :, :] = ends
+    x = x_ref[...]
     sums = [None] * 4
     for offset in range(KW):
         w = wide_ref[offset * width : (offset + 1) * width, :]
         y = jnp.dot(x, w, preferred_element_type=jnp.float32)
-        z = jnp.dot(ends, w, preferred_element_type=jnp.float32)
+        z = y[4 * rows :]
         for part in range(4):
             body = y[part * rows : (part + 1) * rows]
             line = jnp.concatenate([z[2 * part : 2 * part + 2], body, z[8 + 2 * part : 10 + 2 * part]])
@@ -291,7 +293,7 @@
         out_shape=jax.ShapeDtypeStruct((8, 3 * rows // 2, 128), jnp.bfloat16),
         in_specs=[in_smem] + [in_vmem] * 5,
         out_specs=in_vmem,
-        scratch_shapes=[pltpu.VMEM((4, 2 * rows, width), jnp.bfloat16)],
+        scratch_shapes=[pltpu.VMEM((8 * rows + 16, width), jnp.bfloat16)],
         compiler_params=params,
         name="conv",
     )(place, activated, other, end, far_end, wide)

time: 137 us -> 137 us (level)
  no operation moved by 1% of the time
where the time goes in v8:
time: 137 us; the launch traced here: 135 us
  blocking collectives  58.9 us (43%)
  starting transfers between devices  42.6 us (31%)
  waiting for transfers between devices  15.9 us (12%)
  Pallas kernels  13.5 us (10%)
  local copies, waits for them, and re-layouts  2.68 us (2%)
    all_gather x1, blocking collectives, local(): pairs = lax.all_gather(packed, COLUMN, axis=0)  30.6 us
    all_to_all x1, blocking collectives, local(): parts = lax.all_to_all(out, SPREAD, 0, 0, tiled=True)  21.9 us
    all_to_all x1, starting transfers between devices, local(): blocks = lax.all_to_all(mine, 'zt', 0, 0, tiled=True)  15.1 us
    all_to_all x1, waiting for transfers between devices, local(): blocks = lax.all_to_all(mine, 'zt', 0, 0, tiled=True)  7.48 us
    all_to_all x1, starting transfers between devices, everyone(): return lax.all_to_all(sent, axes, 0, 0, tiled=True)  7.43 us
    all_to_all x1, starting transfers between devices, local(): partial = lax.all_to_all(partial, SHARE, 0, 0, tiled=True)  6.44 us
    all_gather x1, blocking collectives, local(): shared = lax.all_gather(features, DP, axis=0)  6.35 us
    pallas_call x1, Pallas kernels, local(): pl.pallas_call(functools.partial(attend_kernel, heads, size), out_shape=j...  6.09 us
  transfers between devices with their start and end apart: 7, of which 3 were waited for; matrix products, arithmetic and copies ran while one was open for 1% of the time, Pallas kernels for 1%

profile of v8, /device:TPU:6, one launch (start us, length us, event | category | flops | bytes accessed | tf_op | source)
XLA Modules:
  0.0 134.5 jit_solution(10084884698912941091)
XLA Ops:
  0.6 0.8 copy-done.3
  1.4 0.7 pack.1
  2.2 15.1 %all-to-all-start = ((bf16[8,48,128]{2,1,0:T(8,128)(2,1)}), bf16[8,48,128]{2,1,0:T(8,128)(2,1)S(1)}, u32[]{:S(2)}, u32[]{:S(2)}) async-start(bf16[8,48,128]{2,1,0:T(8,128)(2,1)} %pack.1), calls=%async_computation | async-start | bytes 196608 | tf_op jit(solution)/shard_map/all_to_all | solution.py:261
  17.2 0.7 broadcast_in_dim.12.gain_ref
  17.9 6.3 %all-gather = bf16[256,768]{1,0:T(8,128)(2,1)S(1)} all-gather(bf16[64,768]{1,0:T(8,128)(2,1)} %mine_ref.1), channel_id=2, replica_groups=mesh['xl'=2,'co'=2,'xh'=2,'y1'=2,'y0'=2,'zt'=8,'zp'=2] {'xl','co'}, dimensions={0}, use_global_device_ids=true | all-gather | bytes 491520 | tf_op jit(solution)/shard_map/all_gather | solution.py:263
  24.3 0.4 activate.1.mine_ref
  24.7 7.5 %all-to-all-done = bf16[8,48,128]{2,1,0:T(8,128)(2,1)S(1)} async-done(((bf16[8,48,128]{2,1,0:T(8,128)(2,1)}), bf16[8,48,128]{2,1,0:T(8,128)(2,1)S(1)}, u32[]{:S(2)}, u32[]{:S(2)}) %all-to-all-start) | async-done | bytes 98336 | tf_op jit(solution)/shard_map/all_to_all | solution.py:261
  32.2 1.0 broadcast_in_dim.13
  33.2 7.4 %all-to-all-start.1 = ((bf16[8,8,48,128]{3,2,1,0:T(8,128)(2,1)}), bf16[8,8,48,128]{3,2,1,0:T(8,128)(2,1)S(1)}, u32[]{:S(2)}, u32[]{:S(2)}) async-start(bf16[8,8,48,128]{3,2,1,0:T(8,128)(2,1)} %broadcast_in_dim.13), calls=%async_computation.1 | async-start | bytes 1572864 | tf_op jit(solution)/shard_map/all_to_all | solution.py:24
  40.6 3.1 %collective-permute-start = (bf16[4,64,768]{2,1,0:T(8,128)(2,1)S(1)}, bf16[4,64,768]{2,1,0:T(8,128)(2,1)S(1)}, u32[]{:S(2)}, u32[]{:S(2)}) collective-permute-start(bf16[4,64,768]{2,1,0:T(8,128)(2,1)S(1)} %activate.1.mine_ref), channel_id=1, source_target_pairs={{0,1},{1,0},{2,3},{3,2},{4,5},{5,4},{6,7},{7,6},{8,9},{9,8},{10,11... | collective-permute-start | bytes 1179656 | tf_op jit(solution)/shard_map/ppermute | solution.py:28
  43.7 3.9 %collective-permute-start.1 = (bf16[4,2,768]{2,1,0:T(2,128)(2,1)S(1)}, bf16[4,2,768]{2,1,0:T(2,128)(2,1)S(1)}, u32[]{:S(2)}, u32[]{:S(2)}) collective-permute-start(bf16[4,2,768]{2,1,0:T(2,128)(2,1)S(1)} %broadcast_select_fusion), channel_id=1, source_target_pairs={{1,2},{3,4},{5,6},{7,8},{9,10},{11,12},{13,14},{15,16},{17,18},{19... | collective-permute-start | bytes 36872 | tf_op jit(solution)/shard_map/ppermute | solution.py:282
  47.6 1.9 %collective-permute-start.2 = (bf16[4,2,768]{2,1,0:T(2,128)(2,1)S(1)}, bf16[4,2,768]{2,1,0:T(2,128)(2,1)S(1)}, u32[]{:S(2)}, u32[]{:S(2)}) collective-permute-start(bf16[4,2,768]{2,1,0:T(2,128)(2,1)S(1)} %broadcast_select_fusion), channel_id=1, source_target_pairs={{1,3},{3,5},{5,7},{7,9},{9,11},{11,13},{13,15},{15,17},{17,19},{19... | collective-permute-start | bytes 36872 | tf_op jit(solution)/shard_map/ppermute | solution.py:282
  49.5 0.1 pad_add_fusion.place_ref
  49.6 1.0 expand.1.wide_ref
  50.6 0.0 copy-start.4
  50.6 0.0 copy-start.5
  50.6 0.0 copy-start.1
  50.6 0.0 copy-start.2
  50.6 4.4 %collective-permute-done.1.end_ref = bf16[4,2,768]{2,1,0:T(2,128)(2,1)S(1)} collective-permute-done((bf16[4,2,768]{2,1,0:T(2,128)(2,1)S(1)}, bf16[4,2,768]{2,1,0:T(2,128)(2,1)S(1)}, u32[]{:S(2)}, u32[]{:S(2)}) %collective-permute-start.1) | collective-permute-done | bytes 12320 | tf_op jit(solution)/shard_map/ppermute | solution.py:282
  55.0 0.0 collective-permute-done.2.far_end_ref
  55.0 2.6 %conv.1 = bf16[8,96,128]{2,1,0:T(8,128)(2,1)} custom-call(s32[2]{0:T(128)S(1)} %pad_add_fusion.place_ref, bf16[4,64,768]{2,1,0:T(8,128)(2,1)S(1)} %activate.1.mine_ref, bf16[4,64,768]{2,1,0:T(8,128)(2,1)S(1)} %collective-permute-done.other_ref, bf16[4,2,768]{2,1,0:T(2,128)(2,1)S(1)} %collective-permute-done.1.end_ref, ...), custom_call_target="tpu_custom_call" | custom-call | tf_op jit(solution)/shard_map/conv/pallas_call | solution.py:291
  57.7 6.4 %all-to-all-start.2 = ((bf16[8,96,128]{2,1,0:T(8,128)(2,1)}), bf16[8,96,128]{2,1,0:T(8,128)(2,1)S(1)}, u32[]{:S(2)}, u32[]{:S(2)}) async-start(bf16[8,96,128]{2,1,0:T(8,128)(2,1)} %conv.1), calls=%async_computation.2 | async-start | bytes 393216 | tf_op jit(solution)/shard_map/all_to_all | solution.py:300
  64.1 0.2 copy.9.vw_ref
  64.3 0.0 copy-start
  64.3 4.1 %all-to-all-done.2.parts_ref = bf16[8,96,128]{2,1,0:T(8,128)(2,1)S(1)} async-done(((bf16[8,96,128]{2,1,0:T(8,128)(2,1)}), bf16[8,96,128]{2,1,0:T(8,128)(2,1)S(1)}, u32[]{:S(2)}, u32[]{:S(2)}) %all-to-all-start.2) | async-done | bytes 196640 | tf_op jit(solution)/shard_map/all_to_all | solution.py:300
  68.4 1.1 stream.1
  69.5 4.8 %all-to-all-start.3 = ((bf16[8,64,768]{2,1,0:T(8,128)(2,1)}), bf16[8,64,768]{2,1,0:T(8,128)(2,1)S(1)}, u32[]{:S(2)}, u32[]{:S(2)}) async-start(bf16[8,64,768]{2,1,0:T(8,128)(2,1)} %get-tuple-element.10), calls=%async_computation.3 | async-start | bytes 1572864 | tf_op jit(solution)/shard_map/all_to_all | solution.py:314
  74.3 30.6 %all-gather.1 = bf16[2560,128]{1,0:T(8,128)(2,1)S(1)} all-gather(bf16[160,128]{1,0:T(8,128)(2,1)S(1)} %get-tuple-element.11), channel_id=3, replica_groups=mesh['xl'=2,'co'=2,'xh'=2,'y1'=2,'y0'=2,'zt'=8,'zp'=2] {'zt','zp'}, dimensions={0}, use_global_device_ids=true | all-gather | bytes 696320 | tf_op jit(solution)/shard_map/all_gather | solution.py:315
  104.9 0.0 all-to-all-done.3.x_ref
  105.0 6.1 %attend.1 = bf16[8,64,1664]{2,1,0:T(8,128)(2,1)S(1)} custom-call(bf16[8,64,768]{2,1,0:T(8,128)(2,1)S(1)} %all-to-all-done.3.x_ref, bf16[768,1024]{1,0:T(8,128)(2,1)S(1)} %copy-done, bf16[16,160,128]{2,1,0:T(8,128)(2,1)S(1)} %bitcast.6), custom_call_target="tpu_custom_call" | custom-call | tf_op jit(solution)/shard_map/attend/pallas_call | solution.py:316
  111.1 21.9 %all_to_all.25.parts_ref = bf16[8,64,1664]{2,1,0:T(8,128)(2,1)S(1)} all-to-all(bf16[8,64,1664]{2,1,0:T(8,128)(2,1)S(1)} %attend.1), channel_id=1, replica_groups=mesh['xl'=2,'co'=2,'xh'=2,'y1'=2,'y0'=2,'zt'=8,'zp'=2] {'xh','y1','y0'}, dimensions={0} | all-to-all | bytes 3407872 | tf_op jit(solution)/shard_map/all_to_all | solution.py:330
  133.0 1.6 %combine.1 = bf16[64,1536]{1,0:T(8,128)(2,1)} custom-call(bf16[8,64,1664]{2,1,0:T(8,128)(2,1)S(1)} %all_to_all.25.parts_ref), custom_call_target="tpu_custom_call" | custom-call | tf_op jit(solution)/shard_map/combine/pallas_call | solution.py:331
  (10 shorter events, 0.0 us)
Async XLA Ops:
  0.6 0.8 copy-start.3
  2.2 30.0 %all-to-all-start = ((bf16[8,48,128]{2,1,0:T(8,128)(2,1)}), bf16[8,48,128]{2,1,0:T(8,128)(2,1)S(1)}, u32[]{:S(2)}, u32[]{:S(2)}) async-start(bf16[8,48,128]{2,1,0:T(8,128)(2,1)} %pack.1), calls=%async_computation | async-start | bytes 196608 | tf_op jit(solution)/shard_map/all_to_all | solution.py:261
  33.2 16.5 %all-to-all-start.1 = ((bf16[8,8,48,128]{3,2,1,0:T(8,128)(2,1)}), bf16[8,8,48,128]{3,2,1,0:T(8,128)(2,1)S(1)}, u32[]{:S(2)}, u32[]{:S(2)}) async-start(bf16[8,8,48,128]{3,2,1,0:T(8,128)(2,1)} %broadcast_in_dim.13), calls=%async_computation.1 | async-start | bytes 1572864 | tf_op jit(solution)/shard_map/all_to_all | solution.py:24
  40.6 14.4 %collective-permute-start = (bf16[4,64,768]{2,1,0:T(8,128)(2,1)S(1)}, bf16[4,64,768]{2,1,0:T(8,128)(2,1)S(1)}, u32[]{:S(2)}, u32[]{:S(2)}) collective-permute-start(bf16[4,64,768]{2,1,0:T(8,128)(2,1)S(1)} %activate.1.mine_ref), channel_id=1, source_target_pairs={{0,1},{1,0},{2,3},{3,2},{4,5},{5,4},{6,7},{7,6},{8,9},{9,8},{10,11... | collective-permute-start | bytes 1179656 | tf_op jit(solution)/shard_map/ppermute | solution.py:28
  43.7 11.3 %collective-permute-start.1 = (bf16[4,2,768]{2,1,0:T(2,128)(2,1)S(1)}, bf16[4,2,768]{2,1,0:T(2,128)(2,1)S(1)}, u32[]{:S(2)}, u32[]{:S(2)}) collective-permute-start(bf16[4,2,768]{2,1,0:T(2,128)(2,1)S(1)} %broadcast_select_fusion), channel_id=1, source_target_pairs={{1,2},{3,4},{5,6},{7,8},{9,10},{11,12},{13,14},{15,16},{17,18},{19... | collective-permute-start | bytes 36872 | tf_op jit(solution)/shard_map/ppermute | solution.py:282
  47.6 7.4 %collective-permute-start.2 = (bf16[4,2,768]{2,1,0:T(2,128)(2,1)S(1)}, bf16[4,2,768]{2,1,0:T(2,128)(2,1)S(1)}, u32[]{:S(2)}, u32[]{:S(2)}) collective-permute-start(bf16[4,2,768]{2,1,0:T(2,128)(2,1)S(1)} %broadcast_select_fusion), channel_id=1, source_target_pairs={{1,3},{3,5},{5,7},{7,9},{9,11},{11,13},{13,15},{15,17},{17,19},{19... | collective-permute-start | bytes 36872 | tf_op jit(solution)/shard_map/ppermute | solution.py:282
  50.6 13.5 %copy-start.4 = (bf16[768,192]{0,1:T(8,128)(2,1)S(1)}, bf16[768,192]{0,1:T(8,128)(2,1)}, u32[]{:S(2)}) copy-start(bf16[768,192]{0,1:T(8,128)(2,1)} %param.13) | copy-start | bytes 884740
  50.6 13.7 %copy-start.5 = (f32[768]{0:T(1024)S(1)}, f32[768]{0:T(1024)}, u32[]{:S(2)}) copy-start(f32[768]{0:T(1024)} %param.10) | copy-start | bytes 9220
  50.6 17.8 %copy-start.1 = (bf16[64,768]{1,0:T(8,128)(2,1)S(1)}, bf16[64,768]{1,0:T(8,128)(2,1)}, u32[]{:S(2)}) copy-start(bf16[64,768]{1,0:T(8,128)(2,1)} %mine_ref.1) | copy-start | bytes 294916
  50.6 17.8 %copy-start.2 = (bf16[768,128]{1,0:T(8,128)(2,1)S(1)}, bf16[768,128]{1,0:T(8,128)(2,1)}, u32[]{:S(2)}) copy-start(bf16[768,128]{1,0:T(8,128)(2,1)} %kw_ref.1) | copy-start | bytes 589828
  57.7 10.7 %all-to-all-start.2 = ((bf16[8,96,128]{2,1,0:T(8,128)(2,1)}), bf16[8,96,128]{2,1,0:T(8,128)(2,1)S(1)}, u32[]{:S(2)}, u32[]{:S(2)}) async-start(bf16[8,96,128]{2,1,0:T(8,128)(2,1)} %conv.1), calls=%async_computation.2 | async-start | bytes 393216 | tf_op jit(solution)/shard_map/all_to_all | solution.py:300
  64.3 40.7 %copy-start = (bf16[768,1024]{1,0:T(8,128)(2,1)S(1)}, bf16[768,1024]{1,0:T(8,128)(2,1)}, u32[]{:S(2)}) copy-start(bf16[768,1024]{1,0:T(8,128)(2,1)} %qw_ref.1) | copy-start | bytes 4718596
  69.5 35.4 %all-to-all-start.3 = ((bf16[8,64,768]{2,1,0:T(8,128)(2,1)}), bf16[8,64,768]{2,1,0:T(8,128)(2,1)S(1)}, u32[]{:S(2)}, u32[]{:S(2)}) async-start(bf16[8,64,768]{2,1,0:T(8,128)(2,1)} %get-tuple-element.10), calls=%async_computation.3 | async-start | bytes 1572864 | tf_op jit(solution)/shard_map/all_to_all | solution.py:314
